TPU v7x, 32 devices: a whole 2x2x4 slice. The times are simulated.
32 devices in a mesh: blk: 32 (over z, y, x, core).
Axes of the slice: x: 2, y: 2, z: 4, core: 2. Of those that a mesh axis runs over, the one named last changes fastest.
Arguments:
- layer_input: bfloat16 [4096, 2560], P('blk'), may hold values from -6 to 6
- norm1_scale: bfloat16 [2560], P('blk'), may hold values from 0.25 to 1.75
- query_weight: bfloat16 [2560, 2560], P('blk'), may hold values from -0.125 to 0.125
- keyvalue_weight: bfloat16 [2560, 512], P('blk'), may hold values from -0.125 to 0.125
- out_weight: bfloat16 [2560, 2560], P('blk'), may hold values from -1.25 to 1.25
- norm2_scale: bfloat16 [2560], P('blk'), may hold values from 0.25 to 1.75
- gate_weight: bfloat16 [2560, 7680], P('blk'), may hold values from -0.125 to 0.125
- gate_bias: bfloat16 [7680], P('blk'), may hold values from -3 to 3
- up_weight: bfloat16 [2560, 7680], P('blk'), may hold values from -0.125 to 0.125
- up_bias: bfloat16 [7680], P('blk'), may hold values from -3 to 3
- down_weight: bfloat16 [7680, 2560], P('blk'), may hold values from -0.0625 to 0.0625
- down_bias: bfloat16 [2560], P('blk'), may hold values from -2 to 2
- out_cotangent: bfloat16 [4096, 2560], P('blk'), may hold values from -6 to 6
Outputs:
- layer_output: bfloat16 [4096, 2560], P('blk')
- residual_mid: float32 [4096, 2560], P('blk')
- rms_values: float32 [2, 4096], P(None, 'blk')
- input_grad: bfloat16 [4096, 2560], P('blk')
- grad_norm1_scale: float32 [2560], P('blk')
- grad_query_weight: float32 [2560, 2560], P('blk')
- grad_keyvalue_weight: float32 [2560, 512], P('blk')
- grad_out_weight: float32 [2560, 2560], P('blk')
- grad_norm2_scale: float32 [2560], P('blk')
- grad_gate_weight: float32 [2560, 7680], P('blk')
- grad_gate_bias: float32 [7680], P('blk')
- grad_up_weight: float32 [2560, 7680], P('blk')
- grad_up_bias: float32 [7680], P('blk')
- grad_down_weight: float32 [7680, 2560], P('blk')
- grad_down_bias: float32 [2560], P('blk')
All inputs are finite; a program needn't handle non-finite values.
Results may differ from a plain program's by a relative error of at most 0.015.
Values may be sent and summed in bfloat16 or wider, within the bound.
A program may use at most 576 MiB of HBM per device.

v0:
```python
import math

import jax
import jax.numpy as jnp
from jax import lax
from jax.sharding import PartitionSpec as P

HD = 256
WINDOW = 2048


EPSILON = 1e-06
NEGATIVE = -1e30
ROTARY_BASE = 10000.0


def from_behind(x, axis, by):
    peers = lax.axis_size(axis)
    pairs = [(i, i + by) for i in range(peers) if 0 <= i + by < peers]
    return lax.ppermute(x, axis, pairs)


def rotary_tables(positions, quarter):
    frequency = ROTARY_BASE ** (-(jnp.arange(quarter, dtype=jnp.float32) / quarter))
    angles = positions[:, None] * frequency[None, :]
    return (jnp.cos(angles), jnp.sin(angles))


def rotate(vector, cosine, sine_table, quarter):
    leading = vector[..., :quarter]
    trailing = vector[..., quarter : 2 * quarter]
    return jnp.concatenate(
        [
            leading * cosine - trailing * sine_table,
            trailing * cosine + leading * sine_table,
            vector[..., 2 * quarter :],
        ],
        axis=-1,
    )


def rotate_back(gradient, cosine, sine_table, quarter):
    leading = gradient[..., :quarter]
    trailing = gradient[..., quarter : 2 * quarter]
    return jnp.concatenate(
        [
            leading * cosine + trailing * sine_table,
            trailing * cosine - leading * sine_table,
            gradient[..., 2 * quarter :],
        ],
        axis=-1,
    )


def gelu_tanh(values):
    return jax.nn.gelu(values, approximate=True)


def block_scores(query_rows, kv_block, query_pos, key_start, heads):
    tok_rows = query_pos.shape[0]
    key_count = kv_block.shape[0]
    raw_scores = jnp.einsum(
        "rd,kd->rk", query_rows, kv_block[:, :HD], preferred_element_type=jnp.float32
    )
    raw_scores = raw_scores.reshape(heads, tok_rows, key_count)
    key_pos = key_start + jnp.arange(key_count, dtype=jnp.int32)
    distance = query_pos[:, None] - key_pos[None, :]
    allowed = (key_pos[None, :] >= 0) & (distance >= 0) & (distance < WINDOW)
    return jnp.where(allowed[None, :, :], raw_scores, NEGATIVE)


def term_maker(left, right):

    def term(first_row, row_count):
        return jnp.einsum("sa,sb->ab", left, right, preferred_element_type=jnp.float32)

    return term


def reduce_rows(term, rows):
    return lax.psum_scatter(
        term(jnp.int32(0), lax.axis_size("blk") * rows), "blk", scatter_dimension=0, tiled=True
    )


def body(
    layer_input,
    norm1_scale,
    query_weight,
    keyvalue_weight,
    out_weight,
    norm2_scale,
    gate_weight,
    gate_bias,
    up_weight,
    up_bias,
    down_weight,
    down_bias,
    out_cotangent,
):
    tok_rows = layer_input.shape[0]
    width = layer_input.shape[1]
    heads = query_weight.shape[1] // HD
    quarter = HD // 4
    query_scale = 1.0 / math.sqrt(HD)
    reach = (WINDOW + tok_rows - 2) // tok_rows
    device = lax.axis_index("blk")
    query_pos = device * tok_rows + jnp.arange(tok_rows, dtype=jnp.int32)
    cosine, sine_table = rotary_tables(query_pos.astype(jnp.float32), quarter)
    (
        gain_one,
        gain_two,
        bias_gate,
        bias_up,
        bias_down,
        query_full,
        keyvalue_full,
        out_full,
        down_full,
    ) = (
        lax.all_gather(norm1_scale, "blk", axis=0, tiled=True),
        lax.all_gather(norm2_scale, "blk", axis=0, tiled=True),
        lax.all_gather(gate_bias, "blk", axis=0, tiled=True),
        lax.all_gather(up_bias, "blk", axis=0, tiled=True),
        lax.all_gather(down_bias, "blk", axis=0, tiled=True),
        lax.all_gather(query_weight, "blk", axis=0, tiled=True),
        lax.all_gather(keyvalue_weight, "blk", axis=0, tiled=True),
        lax.all_gather(out_weight, "blk", axis=0, tiled=True),
        lax.all_gather(down_weight, "blk", axis=0, tiled=True),
    )
    gain_one_f = gain_one.astype(jnp.float32)
    gain_two_f = gain_two.astype(jnp.float32)
    resid_in = layer_input.astype(jnp.float32)
    square_one = jnp.mean(resid_in * resid_in, axis=1, keepdims=True)
    scale_one = lax.rsqrt(square_one + EPSILON)
    normed_one = resid_in * scale_one
    hidden_one = (normed_one * gain_one_f).astype(jnp.bfloat16)
    query_raw = jnp.dot(hidden_one, query_full, preferred_element_type=jnp.float32)
    keyvalue_raw = jnp.dot(hidden_one, keyvalue_full, preferred_element_type=jnp.float32)
    queries_tok = (
        rotate(
            query_raw.reshape(tok_rows, heads, HD),
            cosine[:, None, :],
            sine_table[:, None, :],
            quarter,
        )
        * query_scale
    ).astype(jnp.bfloat16)
    queries = jnp.transpose(queries_tok, (1, 0, 2))
    keys_rot = rotate(keyvalue_raw[:, :HD], cosine, sine_table, quarter)
    own_block = jnp.concatenate([keys_rot, keyvalue_raw[:, HD:]], axis=1).astype(jnp.bfloat16)
    query_rows = queries.reshape(heads * tok_rows, HD)

    def absorb(kv_block, key_start, running):
        row_max, row_sum = running
        scores = block_scores(query_rows, kv_block, query_pos, key_start, heads)
        new_max = jnp.maximum(row_max, jnp.max(scores, axis=-1))
        row_sum = row_sum * jnp.exp(row_max - new_max) + jnp.sum(
            jnp.exp(scores - new_max[:, :, None]), axis=-1
        )
        return (new_max, row_sum)

    stacked = jnp.zeros((reach + 1, tok_rows, 2 * HD), jnp.bfloat16).at[0].set(own_block)
    running = absorb(
        own_block,
        device * tok_rows,
        (
            jnp.full((heads, tok_rows), NEGATIVE, jnp.float32),
            jnp.zeros((heads, tok_rows), jnp.float32),
        ),
    )

    def fetch(offset, loop_state):
        kv_block, stack_now, row_max, row_sum = loop_state
        kv_block = from_behind(kv_block, "blk", 1)
        stack_now = lax.dynamic_update_index_in_dim(stack_now, kv_block, offset, 0)
        row_max, row_sum = absorb(kv_block, (device - offset) * tok_rows, (row_max, row_sum))
        return (kv_block, stack_now, row_max, row_sum)

    passed, stacked, row_max, row_sum = lax.fori_loop(
        1, reach + 1, fetch, (own_block, stacked, running[0], running[1])
    )
    log_total = row_max + jnp.log(row_sum)

    def gather_values(offset, accum):
        kv_block = lax.dynamic_index_in_dim(stacked, offset, 0, keepdims=False)
        scores = block_scores(query_rows, kv_block, query_pos, (device - offset) * tok_rows, heads)
        probs_low = jnp.exp(scores - log_total[:, :, None]).astype(jnp.bfloat16)
        return accum + jnp.einsum(
            "htk,kd->htd", probs_low, kv_block[:, HD:], preferred_element_type=jnp.float32
        )

    attended = lax.fori_loop(
        0, reach + 1, gather_values, jnp.zeros((heads, tok_rows, HD), jnp.float32)
    )
    attention = (
        jnp.transpose(attended, (1, 0, 2)).reshape(tok_rows, heads * HD).astype(jnp.bfloat16)
    )
    residual_mid = resid_in + jnp.dot(attention, out_full, preferred_element_type=jnp.float32)
    square_two = jnp.mean(residual_mid * residual_mid, axis=1, keepdims=True)
    scale_two = lax.rsqrt(square_two + EPSILON)
    normed_two = residual_mid * scale_two
    hidden_two = (normed_two * gain_two_f).astype(jnp.bfloat16)
    pieces = (
        lax.all_gather(gate_weight, "blk", axis=0, tiled=True),
        lax.all_gather(up_weight, "blk", axis=0, tiled=True),
    )
    gate_sum = jnp.dot(hidden_two, pieces[0], preferred_element_type=jnp.float32)
    up_sum = jnp.dot(hidden_two, pieces[1], preferred_element_type=jnp.float32)
    gate_pre = gate_sum + bias_gate.astype(jnp.float32)
    up_pre = up_sum + bias_up.astype(jnp.float32)
    activated, gelu_pull = jax.vjp(gelu_tanh, gate_pre)
    hidden_ffn = (activated * up_pre).astype(jnp.bfloat16)
    ffn_out = jnp.dot(hidden_ffn, down_full, preferred_element_type=jnp.float32) + bias_down.astype(
        jnp.float32
    )
    layer_output = (residual_mid + ffn_out).astype(jnp.bfloat16)
    rms_values = jnp.stack(
        [jnp.sqrt(square_one[:, 0] + EPSILON), jnp.sqrt(square_two[:, 0] + EPSILON)], axis=0
    )
    query_back, keyvalue_back, out_back, down_back = (
        lax.all_gather(query_weight, "blk", axis=0, tiled=True),
        lax.all_gather(keyvalue_weight, "blk", axis=0, tiled=True),
        lax.all_gather(out_weight, "blk", axis=0, tiled=True),
        lax.all_gather(down_weight, "blk", axis=0, tiled=True),
    )
    upstream = out_cotangent.astype(jnp.float32)
    down_bias_grad = jnp.sum(upstream, axis=0)
    hidden_grad = jnp.einsum(
        "sd,fd->sf", out_cotangent, down_back, preferred_element_type=jnp.float32
    )
    gate_grad = gelu_pull(hidden_grad * up_pre)[0].astype(jnp.bfloat16)
    up_grad = (hidden_grad * activated).astype(jnp.bfloat16)
    gate_bias_grad = jnp.sum(gate_grad.astype(jnp.float32), axis=0)
    up_bias_grad = jnp.sum(up_grad.astype(jnp.float32), axis=0)
    pieces = (
        lax.all_gather(gate_weight, "blk", axis=0, tiled=True),
        lax.all_gather(up_weight, "blk", axis=0, tiled=True),
    )
    part_sum = jnp.einsum(
        "sf,df->sd", gate_grad, pieces[0], preferred_element_type=jnp.float32
    ) + jnp.einsum("sf,df->sd", up_grad, pieces[1], preferred_element_type=jnp.float32)
    norm2_grad = jnp.sum(part_sum * normed_two, axis=0)
    weighted_two = part_sum * gain_two_f
    mid_grad = upstream + scale_two * (
        weighted_two - normed_two * jnp.mean(weighted_two * normed_two, axis=1, keepdims=True)
    )
    mid_grad_low = mid_grad.astype(jnp.bfloat16)
    attention_grad_tok = (
        jnp.einsum("sd,ad->sa", mid_grad_low, out_back, preferred_element_type=jnp.float32)
        .astype(jnp.bfloat16)
        .reshape(tok_rows, heads, HD)
    )
    attention_grad = jnp.transpose(attention_grad_tok, (1, 0, 2))

    def block_terms(offset):
        kv_block = lax.dynamic_index_in_dim(stacked, offset, 0, keepdims=False)
        scores = block_scores(query_rows, kv_block, query_pos, (device - offset) * tok_rows, heads)
        probs = jnp.exp(scores - log_total[:, :, None])
        prob_grad = jnp.einsum(
            "htd,kd->htk", attention_grad, kv_block[:, HD:], preferred_element_type=jnp.float32
        )
        return (kv_block, probs, prob_grad)

    def collect_delta(offset, accum):
        kv_block, probs, prob_grad = block_terms(offset)
        return accum + jnp.sum(probs * prob_grad, axis=-1)

    delta = lax.fori_loop(0, reach + 1, collect_delta, jnp.zeros((heads, tok_rows), jnp.float32))

    def block_grads(offset):
        kv_block, probs, prob_grad = block_terms(offset)
        score_grad = (probs * (prob_grad - delta[:, :, None])).astype(jnp.bfloat16)
        query_part = jnp.einsum(
            "htk,kd->htd", score_grad, kv_block[:, :HD], preferred_element_type=jnp.float32
        )
        key_part = jnp.einsum(
            "htk,htd->kd", score_grad, queries, preferred_element_type=jnp.float32
        )
        value_part = jnp.einsum(
            "htk,htd->kd",
            probs.astype(jnp.bfloat16),
            attention_grad,
            preferred_element_type=jnp.float32,
        )
        return (query_part, jnp.concatenate([key_part, value_part], axis=1))

    empty_query = jnp.zeros((heads, tok_rows, HD), jnp.float32)

    def return_grads(counter, loop_state):
        query_acc, carried = loop_state
        query_part, kv_part = block_grads(reach - counter)
        carried = from_behind((carried + kv_part).astype(jnp.bfloat16), "blk", -1).astype(
            jnp.float32
        )
        return (query_acc + query_part, carried)

    query_acc, carried = lax.fori_loop(
        0, reach, return_grads, (empty_query, jnp.zeros((tok_rows, 2 * HD), jnp.float32))
    )
    query_part, kv_part = block_grads(0)
    query_grad = query_acc + query_part
    kv_grad = carried + kv_part
    query_grad_tok = jnp.transpose(query_grad, (1, 0, 2))
    query_raw_grad = (
        rotate_back(
            query_grad_tok * query_scale, cosine[:, None, :], sine_table[:, None, :], quarter
        )
        .reshape(tok_rows, heads * HD)
        .astype(jnp.bfloat16)
    )
    key_raw_grad = rotate_back(kv_grad[:, :HD], cosine, sine_table, quarter)
    keyvalue_raw_grad = jnp.concatenate([key_raw_grad, kv_grad[:, HD:]], axis=1).astype(
        jnp.bfloat16
    )
    normed_grad_one = jnp.einsum(
        "sa,da->sd", query_raw_grad, query_back, preferred_element_type=jnp.float32
    ) + jnp.einsum(
        "sa,da->sd", keyvalue_raw_grad, keyvalue_back, preferred_element_type=jnp.float32
    )
    norm1_grad = jnp.sum(normed_grad_one * normed_one, axis=0)
    weighted_one = normed_grad_one * gain_one_f
    input_grad = (
        mid_grad
        + scale_one
        * (weighted_one - normed_one * jnp.mean(weighted_one * normed_one, axis=1, keepdims=True))
    ).astype(jnp.bfloat16)
    projection_grads = jnp.concatenate([query_raw_grad, keyvalue_raw_grad], axis=1)
    ffn_cols = gate_weight.shape[1]
    ffn_half = ffn_cols // 2
    width_half = width // 2
    query_cols = query_weight.shape[1]
    input_count = query_weight.shape[0]
    out_count = out_weight.shape[0]
    down_count = down_weight.shape[0]
    work_list = [
        (hidden_one, projection_grads, input_count),
        (hidden_two, gate_grad[:, :ffn_half], input_count),
        (hidden_two, gate_grad[:, ffn_half:], input_count),
        (hidden_two, up_grad[:, :ffn_half], input_count),
        (hidden_two, up_grad[:, ffn_half:], input_count),
        (attention, mid_grad_low, out_count),
        (hidden_ffn, out_cotangent[:, :width_half], down_count),
        (hidden_ffn, out_cotangent[:, width_half:], down_count),
    ]
    results = []
    for left, right, rows in work_list:
        results.append(reduce_rows(term_maker(left, right), rows))
    grad_query = results[0][:, :query_cols]
    grad_keyvalue = results[0][:, query_cols:]
    grad_gate = jnp.concatenate([results[1], results[2]], axis=1)
    grad_up = jnp.concatenate([results[3], results[4]], axis=1)
    grad_out = results[5]
    grad_down = jnp.concatenate([results[6], results[7]], axis=1)
    norm1_share, norm2_share, down_bias_share, gate_bias_share, up_bias_share = (
        lax.psum_scatter(norm1_grad, "blk", scatter_dimension=0, tiled=True),
        lax.psum_scatter(norm2_grad, "blk", scatter_dimension=0, tiled=True),
        lax.psum_scatter(down_bias_grad, "blk", scatter_dimension=0, tiled=True),
        lax.psum_scatter(gate_bias_grad, "blk", scatter_dimension=0, tiled=True),
        lax.psum_scatter(up_bias_grad, "blk", scatter_dimension=0, tiled=True),
    )
    return (
        layer_output,
        residual_mid,
        rms_values,
        input_grad,
        norm1_share,
        grad_query,
        grad_keyvalue,
        grad_out,
        norm2_share,
        grad_gate,
        gate_bias_share,
        grad_up,
        up_bias_share,
        grad_down,
        down_bias_share,
    )


def solution(mesh):
    in_specs = (
        P("blk", None),
        P("blk"),
        P("blk", None),
        P("blk", None),
        P("blk", None),
        P("blk"),
        P("blk", None),
        P("blk"),
        P("blk", None),
        P("blk"),
        P("blk", None),
        P("blk"),
        P("blk", None),
    )
    out_specs = (
        P("blk", None),
        P("blk", None),
        P(None, "blk"),
        P("blk", None),
        P("blk"),
        P("blk", None),
        P("blk", None),
        P("blk", None),
        P("blk"),
        P("blk", None),
        P("blk"),
        P("blk", None),
        P("blk"),
        P("blk", None),
        P("blk"),
    )
    return jax.shard_map(body, mesh=mesh, in_specs=in_specs, out_specs=out_specs, check_vma=False)
```

profile of v0, /device:TPU:0, one launch (start us, length us, event | category | flops | bytes accessed | tf_op | source)
XLA Modules:
  0.0 4199.2 jit_solution(5983073456824585038)
XLA Ops:
  12.6 43.5 %all-reduce.12 = (bf16[2560]{0:T(1024)(128)(2,1)S(1)}, bf16[2560]{0:T(1024)(128)(2,1)S(1)}, bf16[7680]{0:T(1024)(128)(2,1)S(1)}, bf16[7680]{0:T(1024)(128)(2,1)S(1)}, bf16[2560]{0:T(1024)(128)(2,1)}) all-reduce(bf16[2560]{0:T(1024)(128)(2,1)S(1)} %dynamic-update-slice.3, ...), channel_id=1, replica_groups=mesh['blk'=32] {'blk'}, use_global_device_ids=true, to_apply=%add.1 | all-reduce | flops 23040 | bytes 92160
  58.8 12.8 all-gather.7.cloned.1.call-done
  76.7 95.3 %all-gather.9.cloned.1.call-done = bf16[2560,2560]{1,0:T(8,128)(2,1)} async-done(((bf16[80,2560]{1,0:T(8,128)(2,1)}), bf16[2560,2560]{1,0:T(8,128)(2,1)}) %all-gather.9.cloned.1.call-update) | async-done | bytes 13107216 | tf_op jit(solution)/shard_map/all_gather | solution.py:126
  172.0 8.3 fusion.127
  187.2 133.8 %while.69 = (s32[]{:T(128)}, bf16[128,512]{1,0:T(8,128)(2,1)S(1)}, bf16[17,128,512]{2,1,0:T(8,128)(2,1)}, f32[10,128]{1,0:T(8,128)S(1)}, f32[10,128]{1,0:T(8,128...) while((s32[]{:T(128)}, bf16[128,512]{1,0:T(8,128)(2,1)S(1)}, ...), condition=%wide.region_6.7_spmd.clone, body=%wide.region_3.6_spmd.clone.sunk | while | flops 84629000 | bytes 3842543 | solution.py:180
  205.5 8.1 collective-permute-start
  215.7 5.3 collective-permute-start
  230.8 7.8 collective-permute-start
  240.9 8.1 collective-permute-start
  251.2 8.1 collective-permute-start
  261.5 5.3 collective-permute-start
  276.6 5.8 collective-permute-start
  284.5 6.2 collective-permute-start
  292.9 8.9 collective-permute-start
  304.1 6.2 collective-permute-start
  312.5 6.3 collective-permute-start
  321.0 38.9 while.70
  363.7 7.0 multiply_reduce_fusion.2
  373.6 137.1 %all-gather.13.cloned.1.call-done = bf16[2560,7680]{1,0:T(8,128)(2,1)} async-done(((bf16[80,7680]{1,0:T(8,128)(2,1)}), bf16[2560,7680]{1,0:T(8,128)(2,1)}) %all-gather.13.cloned.1.call-update) | async-done | bytes 39321616 | tf_op jit(solution)/shard_map/all_gather | solution.py:205
  510.7 18.2 convolution_add_fusion.3
  528.9 205.2 %all-gather.15.cloned.1.call-done = bf16[2560,7680]{1,0:T(8,128)(2,1)} async-done(((bf16[80,7680]{1,0:T(8,128)(2,1)}), bf16[2560,7680]{1,0:T(8,128)(2,1)}) %all-gather.15.cloned.1.call-update) | async-done | bytes 39321616 | tf_op jit(solution)/shard_map/all_gather | solution.py:206
  734.1 17.9 convolution_add_fusion.2
  752.0 205.5 %all-gather.17.cloned.1.call-done = bf16[7680,2560]{1,0:T(8,128)(2,1)} async-done(((bf16[240,2560]{1,0:T(8,128)(2,1)}), bf16[7680,2560]{1,0:T(8,128)(2,1)}) %all-gather.17.cloned.1.call-update) | async-done | bytes 39321616 | tf_op jit(solution)/shard_map/all_gather | solution.py:129
  957.6 25.8 convert_reduce_fusion
  983.4 19.5 fusion.135
  1002.9 20.8 multiply_reduce_fusion
  1027.2 9.0 convolution_convert_fusion
  1036.9 39.9 while.71
  1078.9 181.4 %while.72 = (s32[]{:T(128)}, f32[10,128,256]{2,1,0:T(8,128)}, f32[128,512]{1,0:T(8,128)}, s32[]{:T(128)}, bf16[17,128,512]{2,1,0:T(8,128)(2,1)}, /*index=5*/bf16...) while((s32[]{:T(128)}, f32[10,128,256]{2,1,0:T(8,128)}, ...), condition=%wide.region_15.16_spmd.clone, body=%wide.region_14.15_spmd.clone.sunk | while | flops 421806592 | bytes 24714864 | solution.py:298
  1170.5 5.3 collective-permute-done.1
  1265.5 9.2 fusion.136
  1277.6 13.4 fusion.79
  1292.6 15.2 fusion.87
  1307.9 15.6 fusion.89
  1325.3 15.3 fusion.75
  1340.7 15.3 fusion.77
  1357.6 15.3 fusion.71
  1373.0 15.6 fusion.73
  1390.0 10.5 fusion.92
  1404.6 15.9 fusion.49
  1429.1 284.6 %reduce-scatter.9.cloned.1.call-done = f32[80,3072]{1,0:T(8,128)} async-done(((f32[2560,3072]{1,0:T(8,128)}), f32[80,3072]{1,0:T(8,128)}) %reduce-scatter.9.cloned.1.call-update) | async-done | bytes 983056 | tf_op jit(solution)/shard_map/reduce_scatter | solution.py:81
  1717.4 362.9 %reduce-scatter.23.cloned.1.call-done = f32[240,1280]{1,0:T(8,128)} async-done(((f32[7680,1280]{1,0:T(8,128)}), f32[240,1280]{1,0:T(8,128)}) %reduce-scatter.23.cloned.1.call-update) | async-done | bytes 1228816 | tf_op jit(solution)/shard_map/reduce_scatter | solution.py:81
  2080.4 366.3 %reduce-scatter.21.cloned.1.call-done = f32[240,1280]{1,0:T(8,128)} async-done(((f32[7680,1280]{1,0:T(8,128)}), f32[240,1280]{1,0:T(8,128)}) %reduce-scatter.21.cloned.1.call-update) | async-done | bytes 1228816 | tf_op jit(solution)/shard_map/reduce_scatter | solution.py:81
  2450.0 362.9 %reduce-scatter.15.cloned.1.call-done = f32[80,3840]{1,0:T(8,128)} async-done(((f32[2560,3840]{1,0:T(8,128)}), f32[80,3840]{1,0:T(8,128)}) %reduce-scatter.15.cloned.1.call-update) | async-done | bytes 1228816 | tf_op jit(solution)/shard_map/reduce_scatter | solution.py:81
  2812.8 365.9 %reduce-scatter.13.cloned.1.call-done = f32[80,3840]{1,0:T(8,128)} async-done(((f32[2560,3840]{1,0:T(8,128)}), f32[80,3840]{1,0:T(8,128)}) %reduce-scatter.13.cloned.1.call-update) | async-done | bytes 1228816 | tf_op jit(solution)/shard_map/reduce_scatter | solution.py:81
  3182.1 363.4 %reduce-scatter.19.cloned.1.call-done = f32[80,3840]{1,0:T(8,128)} async-done(((f32[2560,3840]{1,0:T(8,128)}), f32[80,3840]{1,0:T(8,128)}) %reduce-scatter.19.cloned.1.call-update) | async-done | bytes 1228816 | tf_op jit(solution)/shard_map/reduce_scatter | solution.py:81
  3545.5 366.2 %reduce-scatter.17.cloned.1.call-done = f32[80,3840]{1,0:T(8,128)} async-done(((f32[2560,3840]{1,0:T(8,128)}), f32[80,3840]{1,0:T(8,128)}) %reduce-scatter.17.cloned.1.call-update) | async-done | bytes 1228816 | tf_op jit(solution)/shard_map/reduce_scatter | solution.py:81
  3915.0 277.2 %reduce-scatter.11.cloned.1.call-done = f32[80,2560]{1,0:T(8,128)} async-done(((f32[2560,2560]{1,0:T(8,128)}), f32[80,2560]{1,0:T(8,128)}) %reduce-scatter.11.cloned.1.call-update) | async-done | bytes 819216 | tf_op jit(solution)/shard_map/reduce_scatter | solution.py:81
  (1065 shorter events, 379.2 us)
Async XLA Ops:
  7.2 64.5 %all-gather.7.cloned.1.call-start = ((), (), s32[]{:S(2)}) async-start(), calls=%async_computation.8 | async-start | bytes 2703360 | tf_op jit(solution)/shard_map/all_gather | solution.py:127
  7.9 164.0 %all-gather.9.cloned.1.call-start = ((), (), s32[]{:S(2)}) async-start(), calls=%async_computation.9 | async-start | bytes 13516800 | tf_op jit(solution)/shard_map/all_gather | solution.py:126
  8.7 355.0 %all-gather.11.cloned.1.call-start = ((), (), s32[]{:S(2)}) async-start(), calls=%async_computation.10 | async-start | bytes 13516800 | tf_op jit(solution)/shard_map/all_gather | solution.py:128
  9.5 501.2 %all-gather.13.cloned.1.call-start = ((), (), s32[]{:S(2)}) async-start(), calls=%async_computation.11 | async-start | bytes 40550400 | tf_op jit(solution)/shard_map/all_gather | solution.py:205
  10.0 724.1 %all-gather.15.cloned.1.call-start = ((), (), s32[]{:S(2)}) async-start(), calls=%async_computation.12 | async-start | bytes 40550400 | tf_op jit(solution)/shard_map/all_gather | solution.py:206
  10.6 946.9 %all-gather.17.cloned.1.call-start = ((), (), s32[]{:S(2)}) async-start(), calls=%async_computation.13 | async-start | bytes 40550400 | tf_op jit(solution)/shard_map/all_gather | solution.py:129
  11.2 1411.4 %all-reduce.15.cloned.1.call-start = ((), (), s32[]{:S(2)}) async-start(), calls=%async_computation.22 | async-start | bytes 204800
  187.2 3.1 collective-permute-start
  191.6 5.1 collective-permute-start
  198.0 6.3 collective-permute-start
  205.5 9.0 collective-permute-start
  215.7 6.3 collective-permute-start
  223.3 6.3 collective-permute-start
  230.8 8.8 collective-permute-start
  240.9 9.1 collective-permute-start
  251.2 9.0 collective-permute-start
  261.5 6.3 collective-permute-start
  269.0 6.3 collective-permute-start
  276.6 6.7 collective-permute-start
  284.5 7.2 collective-permute-start
  292.9 9.9 collective-permute-start
  304.1 7.2 collective-permute-start
  312.5 7.3 collective-permute-start
  370.6 653.1 %copy-start.8 = (f32[128,2560]{1,0:T(8,128)}, f32[128,2560]{1,0:T(8,128)S(1)}, u32[]{:S(2)}) copy-start(f32[128,2560]{1,0:T(8,128)S(1)} %get-tuple-element.1035) | copy-start | bytes 3932164
  1082.9 3.2 collective-permute-start.1
  1090.9 6.1 collective-permute-start.1
  1101.7 6.3 collective-permute-start.1
  1112.7 6.3 collective-permute-start.1
  1123.7 6.3 collective-permute-start.1
  1134.7 6.3 collective-permute-start.1
  1145.8 6.3 collective-permute-start.1
  1156.8 7.1 collective-permute-start.1
  1168.6 7.2 collective-permute-start.1
  1180.6 7.2 collective-permute-start.1
  1192.5 7.2 collective-permute-start.1
  1204.5 7.2 collective-permute-start.1
  1216.4 7.2 collective-permute-start.1
  1228.4 7.2 collective-permute-start.1
  1240.3 7.2 collective-permute-start.1
  1252.2 7.2 collective-permute-start.1
  1277.5 436.2 %reduce-scatter.9.cloned.1.call-start = ((), (), s32[]{:S(2)}) async-start(), calls=%async_computation.14 | async-start | bytes 32440320 | tf_op jit(solution)/shard_map/reduce_scatter | solution.py:81
  1291.0 789.4 %reduce-scatter.23.cloned.1.call-start = ((), (), s32[]{:S(2)}) async-start(), calls=%async_computation.21 | async-start | bytes 40550400 | tf_op jit(solution)/shard_map/reduce_scatter | solution.py:81
  1307.9 1138.8 %reduce-scatter.21.cloned.1.call-start = ((), (), s32[]{:S(2)}) async-start(), calls=%async_computation.20 | async-start | bytes 40550400 | tf_op jit(solution)/shard_map/reduce_scatter | solution.py:81
  1323.5 1489.3 %reduce-scatter.15.cloned.1.call-start = ((), (), s32[]{:S(2)}) async-start(), calls=%async_computation.17 | async-start | bytes 40550400 | tf_op jit(solution)/shard_map/reduce_scatter | solution.py:81
  1340.6 1838.2 %reduce-scatter.13.cloned.1.call-start = ((), (), s32[]{:S(2)}) async-start(), calls=%async_computation.16 | async-start | bytes 40550400 | tf_op jit(solution)/shard_map/reduce_scatter | solution.py:81
  1356.0 2189.4 %reduce-scatter.19.cloned.1.call-start = ((), (), s32[]{:S(2)}) async-start(), calls=%async_computation.19 | async-start | bytes 40550400 | tf_op jit(solution)/shard_map/reduce_scatter | solution.py:81
  1372.9 2538.7 %reduce-scatter.17.cloned.1.call-start = ((), (), s32[]{:S(2)}) async-start(), calls=%async_computation.18 | async-start | bytes 40550400 | tf_op jit(solution)/shard_map/reduce_scatter | solution.py:81
  1388.6 2803.6 %reduce-scatter.11.cloned.1.call-start = ((), (), s32[]{:S(2)}) async-start(), calls=%async_computation.15 | async-start | bytes 27033600 | tf_op jit(solution)/shard_map/reduce_scatter | solution.py:81
  (105 other events, 2277.6 us)
Sparse Core Ops, SparseCore 0:
  10.8 60.7 all-gather.6
  74.5 97.3 all-gather.8
  174.8 101.8 all-gather.10
  279.5 231.1 all-gather.12
  513.4 220.6 all-gather.14
  736.9 220.6 all-gather.16
  1277.6 144.9 all-reduce.14
  1429.0 284.6 reduce-scatter.8
  1720.2 360.1 reduce-scatter.22
  2086.6 359.9 reduce-scatter.20
  2453.1 359.7 reduce-scatter.14
  2819.1 359.6 reduce-scatter.12
  3185.2 360.2 reduce-scatter.18
  3551.8 359.8 reduce-scatter.16
  3914.4 277.7 reduce-scatter.10
where the time goes:
time: 4220 us; the launch traced here: 4200 us
  waiting for transfers between devices  3490 us (83%)
  matrix products  362 us (9%)
  starting transfers between devices  120 us (3%)
  local copies, waits for them, and re-layouts  109 us (3%)
  other arithmetic  48.7 us (1%)
  blocking collectives  43.5 us (1%)
    reduce_scatter x8, waiting for transfers between devices, reduce_rows(): lax.psum_scatter(term(jnp.int32(0), lax.axis_size('blk') * rows), 'blk',...  2750 us
    all_gather x1, waiting for transfers between devices, body(): lax.all_gather(down_weight, 'blk', axis=0, tiled=True)  206 us
    all_gather x1, waiting for transfers between devices, body(): lax.all_gather(up_weight, 'blk', axis=0, tiled=True)  205 us
    all_gather x1, waiting for transfers between devices, body(): lax.all_gather(gate_weight, 'blk', axis=0, tiled=True)  137 us
    ppermute x32, starting transfers between devices, from_behind(): return lax.ppermute(x, axis, pairs)  119 us
    dot_general x8, matrix products, term(): jnp.einsum('sa,sb->ab', left, right, preferred_element_type=jnp.float32)  116 us
    all_gather x1, waiting for transfers between devices, body(): lax.all_gather(query_weight, 'blk', axis=0, tiled=True)  95.3 us
  transfers between devices with their start and end apart: 47, of which 46 were waited for; matrix products, arithmetic and copies ran while one was open for 7% of the time, Pallas kernels for 0%

commit v1 on v0

v1 whole, which is shorter than its diff:
```python
import functools
import math

import jax
import jax.numpy as jnp
from jax import lax
from jax.experimental import pallas as pl
from jax.experimental.pallas import tpu as pltpu
from jax.sharding import PartitionSpec as P

HD = 256
WINDOW = 2048
EPSILON = 1e-06
NEGATIVE = -1e30
ROTARY_BASE = 10000.0
AXIS = "blk"
LANES = 128
DEVICES = 32
PAIR = 2
VMEM_BYTES = 48 * 1024 * 1024
F32 = jnp.float32
BF16 = jnp.bfloat16


def rotary_tables(positions, quarter):
    frequency = ROTARY_BASE ** (-(jnp.arange(quarter, dtype=F32) / quarter))
    angles = positions[:, None] * frequency[None, :]
    return (jnp.cos(angles), jnp.sin(angles))


def rotate(vector, cosine, sine_table, quarter):
    leading = vector[..., :quarter]
    trailing = vector[..., quarter : 2 * quarter]
    return jnp.concatenate(
        [
            leading * cosine - trailing * sine_table,
            trailing * cosine + leading * sine_table,
            vector[..., 2 * quarter :],
        ],
        axis=-1,
    )


def gelu_tanh(values):
    return jax.nn.gelu(values, approximate=True)


def dot(left, right, contract):
    return lax.dot_general(left, right, (contract, ((), ())), preferred_element_type=F32)


def round_up(count, step):
    return (count + step - 1) // step * step


def pad_columns(values, columns):
    pad = [(0, 0)] * (values.ndim - 1) + [(0, columns - values.shape[-1])]
    return jnp.pad(values, pad)


def masked_scores(place_ref, query_rows, keys, tok_rows):
    scores = dot(query_rows, keys, ((1,), (1,)))
    rows = lax.broadcasted_iota(jnp.int32, scores.shape, 0) % tok_rows
    columns = lax.broadcasted_iota(jnp.int32, scores.shape, 1)
    distance = rows - columns + place_ref[0]
    return jnp.where((distance >= 0) & (distance < WINDOW), scores, NEGATIVE)


def stack_heads(block):
    return jnp.concatenate([block[:, i * HD : (i + 1) * HD] for i in range(PAIR)], axis=0)


def unstack_heads(rows):
    tok_rows = rows.shape[0] // PAIR
    return jnp.concatenate([rows[i * tok_rows : (i + 1) * tok_rows] for i in range(PAIR)], axis=1)


def attend_kernel(place_ref, query_ref, kv_ref, out_ref, log_ref):
    tok_rows = query_ref.shape[0]
    scores = masked_scores(place_ref, stack_heads(query_ref[...]), kv_ref[:, :HD], tok_rows)
    row_max = jnp.max(scores, axis=1, keepdims=True)
    probs = jnp.exp(scores - row_max)
    row_sum = jnp.sum(probs, axis=1, keepdims=True)
    probs_low = (probs * (1.0 / row_sum)).astype(BF16)
    attended = dot(probs_low, kv_ref[:, HD:], ((1,), (0,)))
    out_ref[...] = unstack_heads(attended).astype(BF16)
    log_ref[0] = jnp.broadcast_to(row_max + jnp.log(row_sum), log_ref.shape[1:])


def attend_back_kernel(place_ref, query_ref, kv_ref, log_ref, grad_ref, query_grad_ref, kv_grad_ref):
    tok_rows = query_ref.shape[0]
    query_rows = stack_heads(query_ref[...])
    grad_rows = stack_heads(grad_ref[...])
    keys, values = kv_ref[:, :HD], kv_ref[:, HD:]
    scores = masked_scores(place_ref, query_rows, keys, tok_rows)
    probs = jnp.exp(scores - log_ref[0][:, :1])
    prob_grad = dot(grad_rows, values, ((1,), (1,)))
    delta = jnp.sum(probs * prob_grad, axis=1, keepdims=True)
    score_grad = (probs * (prob_grad - delta)).astype(BF16)
    query_grad_ref[...] = unstack_heads(dot(score_grad, keys, ((1,), (0,))))
    key_part = dot(score_grad, query_rows, ((0,), (0,)))
    value_part = dot(probs.astype(BF16), grad_rows, ((0,), (0,)))

    @pl.when(pl.program_id(0) == 0)
    def _():
        kv_grad_ref[:, :HD] = key_part
        kv_grad_ref[:, HD:] = value_part

    @pl.when(pl.program_id(0) > 0)
    def _():
        kv_grad_ref[:, :HD] += key_part
        kv_grad_ref[:, HD:] += value_part


def attention_specs(tok_rows, heads, window_rows):
    place = pl.BlockSpec(memory_space=pltpu.SMEM)
    by_head = pl.BlockSpec((tok_rows, PAIR * HD), lambda i: (0, i))
    whole = pl.BlockSpec((window_rows, 2 * HD), lambda i: (0, 0))
    logs = pl.BlockSpec((1, PAIR * tok_rows, LANES), lambda i: (i, 0, 0))
    return place, by_head, whole, logs


def attend(place, queries, kv_window):
    tok_rows, features = queries.shape
    window_rows = kv_window.shape[0]
    pairs = features // HD // PAIR
    place_spec, by_head, whole, logs = attention_specs(tok_rows, features // HD, window_rows)
    work = tok_rows * features * window_rows
    return pl.pallas_call(
        attend_kernel,
        grid=(pairs,),
        out_shape=(
            jax.ShapeDtypeStruct((tok_rows, features), BF16),
            jax.ShapeDtypeStruct((pairs, PAIR * tok_rows, LANES), F32),
        ),
        in_specs=[place_spec, by_head, whole],
        out_specs=(by_head, logs),
        compiler_params=pltpu.CompilerParams(vmem_limit_bytes=VMEM_BYTES),
        cost_estimate=pl.CostEstimate(
            flops=4 * work, bytes_accessed=8 * kv_window.size, transcendentals=work // HD
        ),
        name="attend",
    )(place, queries, kv_window)


def attend_back(place, queries, kv_window, logs_in, grad):
    tok_rows, features = queries.shape
    window_rows = kv_window.shape[0]
    pairs = features // HD // PAIR
    place_spec, by_head, whole, logs = attention_specs(tok_rows, features // HD, window_rows)
    work = tok_rows * features * window_rows
    return pl.pallas_call(
        attend_back_kernel,
        grid=(pairs,),
        out_shape=(
            jax.ShapeDtypeStruct((tok_rows, features), F32),
            jax.ShapeDtypeStruct((window_rows, 2 * HD), F32),
        ),
        in_specs=[place_spec, by_head, whole, logs, by_head],
        out_specs=(by_head, whole),
        compiler_params=pltpu.CompilerParams(vmem_limit_bytes=VMEM_BYTES),
        cost_estimate=pl.CostEstimate(
            flops=10 * work, bytes_accessed=8 * kv_window.size, transcendentals=work // HD
        ),
        name="attend_back",
    )(place, queries, kv_window, logs_in, grad)


MESH=pl.DeviceIdType.MESH

class Place:
    def __init__(self):
        me = lax.axis_index(AXIS)
        self.core = me % 2
        self.x = (me // 2) % 2
        self.y = (me // 4) % 2
        self.z = me // 8
        self.sibling = self.index(self.z, self.y, self.x, 1 - self.core)
        self.next_x = self.index(self.z, self.y, 1 - self.x, self.core)
        self.next_y = self.index(self.z, 1 - self.y, self.x, self.core)
        self.plane = [self.z] + [(self.z + o) % 4 for o in (1, 2, 3)]
        self.line = [self.index(p, self.y, self.x, self.core) for p in self.plane]
    def index(self, z, y, x, core):
        return ((z * 2 + y) * 2 + x) * 2 + core
    def side(self, dy, dx):
        return (1 - self.y if dy else self.y), (1 - self.x if dx else self.x)
    def meet(self):
        barrier = pltpu.get_barrier_semaphore()
        partners = [self.sibling, self.next_x, self.next_y] + self.line[1:]
        for device in partners:
            pl.semaphore_signal(barrier, inc=1, device_id=(device,), device_id_type=MESH)
        pl.semaphore_wait(barrier, len(partners))

def send(src, dst, sems, device):
    copy = pltpu.make_async_remote_copy(src_ref=src, dst_ref=dst, send_sem=sems[0], recv_sem=sems[1], device_id=(device,), device_id_type=MESH)
    copy.start()
    return copy

TILE=16
def add_rows(total, other, first, count):
    planes = other.shape[0]
    steps = count // TILE
    @pl.loop(0, planes * steps)
    def _(i):
        plane, row = i // steps, (i % steps) * TILE
        here = (plane, pl.ds(pl.multiple_of(row + first, TILE), TILE), slice(None))
        there = (plane, pl.ds(pl.multiple_of(row, TILE), TILE), slice(None))
        total[here] = (total[here].astype(F32) + other[there].astype(F32)).astype(BF16)

def sum_kernel(chunk, in_ref, out_ref, acc, got_core, got_diag_x, got_diag_y, got_x, got_y, got_z,
               load_sem, core_sems, diag_sems, side_sems, line_sems):
    place = Place()
    rows, columns = out_ref.shape
    upper = got_diag_x.shape[1]
    lower = rows - upper
    chunks = columns // chunk
    corners = [(1, 1), (0, 1), (1, 0), (0, 0)]
    cols = [pl.ds(k * chunk, chunk) for k in range(chunks)]
    loads, cores, sends = {}, {}, []
    for k in range(chunks):
        for i, (dy, dx) in enumerate(corners):
            y, x = place.side(dy, dx)
            load = pltpu.make_async_copy(in_ref.at[:, y, x, place.core, :, cols[k]], acc.at[i, :, :, cols[k]], load_sem.at[k, i])
            load.start()
            loads[k, i] = load
    place.meet()
    for k in range(chunks):
        for i, (dy, dx) in enumerate(corners):
            y, x = place.side(dy, dx)
            cores[k, i] = send(in_ref.at[:, y, x, 1 - place.core, :, cols[k]], got_core.at[i, :, :, cols[k]],
                               (core_sems.at[0, k, i], core_sems.at[1, k, i]), place.sibling)
    top, bottom = pl.ds(0, upper), pl.ds(upper, lower)
    diag, side, line = {}, {}, {}
    def pair(sems, k, i): return (sems.at[0, k, i], sems.at[1, k, i])
    def stage0(k):
        for i in range(4):
            loads[k, i].wait(); cores[k, i].wait_recv()
            add_rows(acc.at[i, :, :, cols[k]], got_core.at[i, :, :, cols[k]], 0, rows)
            if i == 0:
                diag[k, 0] = send(acc.at[0, :, top, cols[k]], got_diag_x.at[:, :, cols[k]], pair(diag_sems, k, 0), place.next_x)
                diag[k, 1] = send(acc.at[0, :, bottom, cols[k]], got_diag_y.at[:, :, cols[k]], pair(diag_sems, k, 1), place.next_y)
            if i == 1:
                side[k, 0] = send(acc.at[1, :, top, cols[k]], got_x.at[:, top, cols[k]], pair(side_sems, k, 0), place.next_x)
            if i == 2:
                side[k, 1] = send(acc.at[2, :, bottom, cols[k]], got_y.at[:, bottom, cols[k]], pair(side_sems, k, 1), place.next_y)
    def stage1(k):
        diag[k, 0].wait_recv()
        add_rows(acc.at[2, :, :, cols[k]], got_diag_x.at[:, :, cols[k]], 0, upper)
        side[k, 2] = send(acc.at[2, :, top, cols[k]], got_y.at[:, top, cols[k]], pair(side_sems, k, 2), place.next_y)
        diag[k, 1].wait_recv()
        add_rows(acc.at[1, :, :, cols[k]], got_diag_y.at[:, :, cols[k]], upper, lower)
        side[k, 3] = send(acc.at[1, :, bottom, cols[k]], got_x.at[:, bottom, cols[k]], pair(side_sems, k, 3), place.next_x)
    def stage2(k):
        for i in range(4): side[k, i].wait_recv()
        steps = rows // TILE
        @pl.loop(0, 4 * steps)
        def _(i):
            plane, row = i // steps, (i % steps) * TILE
            here = (plane, pl.ds(pl.multiple_of(row, TILE), TILE), cols[k])
            acc[(3,) + here] = (acc[(3,) + here].astype(F32) + got_x[here].astype(F32) + got_y[here].astype(F32)).astype(BF16)
        for o in (1, 2, 3):
            line[k, o] = send(acc.at[3, place.plane[o], :, cols[k]], got_z.at[o - 1, :, cols[k]], pair(line_sems, k, o - 1), place.line[o])
    def stage3(k):
        for o in (1, 2, 3): line[k, o].wait_recv()
        @pl.loop(0, rows // TILE)
        def _(i):
            here = (pl.ds(pl.multiple_of(i * TILE, TILE), TILE), cols[k])
            total = acc[(3, place.z) + here].astype(F32)
            for o in range(3): total += got_z[(o,) + here].astype(F32)
            out_ref[here] = total
    stages = [stage0, stage1, stage2, stage3]
    for step in range(chunks + 3):
        for s in range(3, -1, -1):
            if 0 <= step - s < chunks: stages[s](step - s)
    for group in (cores, diag, side, line):
        for copy in group.values(): copy.wait_send()

def sum_over_devices(partial, chunk, collective_id, name):
    rows, columns = partial.shape[0] // 32, partial.shape[1]
    chunks = columns // chunk
    upper = (rows // 2 + TILE - 1) // TILE * TILE
    def buf(*shape): return pltpu.VMEM(shape, BF16)
    def sems(count): return pltpu.SemaphoreType.DMA((2, chunks, count))
    return pl.pallas_call(
        functools.partial(sum_kernel, chunk),
        out_shape=jax.ShapeDtypeStruct((rows, columns), F32),
        in_specs=[pl.BlockSpec(memory_space=pl.ANY)],
        out_specs=pl.BlockSpec(memory_space=pltpu.VMEM),
        scratch_shapes=[buf(4, 4, rows, columns), buf(4, 4, rows, columns), buf(4, upper, columns), buf(4, rows - upper, columns),
            buf(4, rows, columns), buf(4, rows, columns), buf(3, rows, columns),
            pltpu.SemaphoreType.DMA((chunks, 4)), sems(4), sems(2), sems(4), sems(3)],
        compiler_params=pltpu.CompilerParams(collective_id=collective_id, has_side_effects=True, vmem_limit_bytes=56*1024*1024),
        name=name,
    )(partial.reshape(4, 2, 2, 2, rows, columns))


def gather_rows(values):
    return lax.all_gather(values, AXIS, axis=0, tiled=True)


def sum_rows(partial, chunk, collective_id, name):
    if lax.axis_size(AXIS) == DEVICES:
        return sum_over_devices(partial.astype(BF16), chunk, collective_id, name)
    return lax.psum_scatter(
        partial.astype(BF16), AXIS, scatter_dimension=0, tiled=True
    ).astype(F32)


def swap(pieces):
    return lax.all_to_all(pieces, AXIS, 0, 0, tiled=False)


def feed_forward(hidden_two, out_cotangent, both_own, both_bias, down_own, rows):
    peers = lax.axis_size(AXIS)
    device = lax.axis_index(AXIS)
    tok_rows, width = hidden_two.shape
    ffn_pad = down_own.shape[0]

    def piece(sums, here):
        hidden_own, cotangent_own = here
        cotangent_full = gather_rows(cotangent_own)
        hidden_full = gather_rows(hidden_own)
        both_pre = jnp.dot(hidden_full, both_own, preferred_element_type=F32) + both_bias
        gate_pre, up_pre = both_pre[:, :ffn_pad], both_pre[:, ffn_pad:]
        activated, gelu_pull = jax.vjp(gelu_tanh, gate_pre)
        hidden_ffn = (activated * up_pre).astype(BF16)
        hidden_grad = dot(cotangent_full, down_own, ((1,), (1,)))
        gate_grad = gelu_pull(hidden_grad * up_pre)[0].astype(BF16)
        up_grad = (hidden_grad * activated).astype(BF16)
        both_grad = jnp.concatenate([gate_grad, up_grad], axis=1)
        normed_grad = sum_rows(dot(both_grad, both_own, ((1,), (1,))), 512, 1, "sum_hidden")
        ffn_out = sum_rows(
            jnp.dot(hidden_ffn, down_own, preferred_element_type=F32), 512, 1, "sum_hidden"
        )
        own_cotangent = lax.dynamic_slice_in_dim(cotangent_full, device * rows, rows, 1)
        shares = (
            dot(hidden_full, both_grad, ((0,), (0,))),
            dot(hidden_ffn, cotangent_full, ((0,), (0,))),
            jnp.sum(both_grad.astype(F32), axis=0),
            jnp.sum(own_cotangent.astype(F32), axis=0),
        )
        if sums is not None:
            shares = jax.tree.map(jnp.add, sums, shares)
        return shares, (normed_grad, ffn_out)

    pieces = max(1, peers // DEVICES)
    if pieces == 1:
        shares, (normed_grad, ffn_out) = piece(None, (hidden_two, out_cotangent))
    else:
        zeros = (
            jnp.zeros((width, 2 * ffn_pad), F32),
            jnp.zeros((ffn_pad, width), F32),
            jnp.zeros((2 * ffn_pad,), F32),
            jnp.zeros((rows,), F32),
        )
        cut = (pieces, tok_rows // pieces, width)
        shares, outs = lax.scan(piece, zeros, (hidden_two.reshape(cut), out_cotangent.reshape(cut)))
        normed_grad, ffn_out = (part.reshape(tok_rows, width) for part in outs)
    return (normed_grad, ffn_out) + shares


def body(
    layer_input,
    norm1_scale,
    query_weight,
    keyvalue_weight,
    out_weight,
    norm2_scale,
    gate_weight,
    gate_bias,
    up_weight,
    up_bias,
    down_weight,
    down_bias,
    out_cotangent,
):
    peers = lax.axis_size(AXIS)
    device = lax.axis_index(AXIS)
    tok_rows, width = layer_input.shape
    rows = query_weight.shape[0]
    query_cols = query_weight.shape[1]
    kv_cols = keyvalue_weight.shape[1]
    heads = query_cols // HD
    quarter = HD // 4
    query_scale = 1.0 / math.sqrt(HD)
    ffn_own = down_weight.shape[0]
    ffn_pad = round_up(ffn_own, LANES)

    vectors = jnp.stack([norm1_scale, norm2_scale, down_bias], axis=1)
    first = gather_rows(
        jnp.concatenate([query_weight, keyvalue_weight, pad_columns(vectors, LANES)], axis=1)
    )
    proj_cols = query_cols + kv_cols
    proj_full = first[:, :proj_cols]
    gains = first[:, proj_cols:].astype(F32).T
    gain_one, gain_two, bias_down = gains[0], gains[1], gains[2]

    resid_in = layer_input.astype(F32)
    square_one = jnp.mean(resid_in * resid_in, axis=1, keepdims=True)
    scale_one = lax.rsqrt(square_one + EPSILON)
    normed_one = resid_in * scale_one
    hidden_one = (normed_one * gain_one).astype(BF16)
    projected = jnp.dot(hidden_one, proj_full, preferred_element_type=F32)
    position = device * tok_rows + jnp.arange(tok_rows, dtype=jnp.int32)
    cosine, sine_table = rotary_tables(position.astype(F32), quarter)
    queries = (
        rotate(
            projected[:, :query_cols].reshape(tok_rows, heads, HD),
            cosine[:, None, :],
            sine_table[:, None, :],
            quarter,
        )
        * query_scale
    ).astype(BF16)
    queries = queries.reshape(tok_rows, query_cols)
    keys_rot = rotate(projected[:, query_cols : query_cols + HD], cosine, sine_table, quarter)
    own_kv = jnp.concatenate([keys_rot, projected[:, query_cols + HD :]], axis=1).astype(BF16)

    reach = min((WINDOW + tok_rows - 2) // tok_rows, peers - 1)
    window_rows = (reach + 1) * tok_rows
    window_start = jnp.maximum(device - reach, 0) * tok_rows
    kv_window = lax.dynamic_slice_in_dim(gather_rows(own_kv), window_start, window_rows, 0)
    place = (device * tok_rows - window_start).astype(jnp.int32).reshape(1)
    attention, logs = attend(place, queries, kv_window)

    out_full = gather_rows(out_weight)
    residual_mid = resid_in + jnp.dot(attention, out_full, preferred_element_type=F32)
    square_two = jnp.mean(residual_mid * residual_mid, axis=1, keepdims=True)
    scale_two = lax.rsqrt(square_two + EPSILON)
    normed_two = residual_mid * scale_two
    hidden_two = (normed_two * gain_two).astype(BF16)

    gate_pieces = pad_columns(gate_weight.reshape(rows, peers, ffn_own), ffn_pad)
    up_pieces = pad_columns(up_weight.reshape(rows, peers, ffn_own), ffn_pad)
    both_own = swap(
        jnp.concatenate([gate_pieces, up_pieces], axis=2).transpose(1, 0, 2)
    ).reshape(peers * rows, 2 * ffn_pad)
    both_bias = jnp.concatenate(
        [pad_columns(gate_bias, ffn_pad), pad_columns(up_bias, ffn_pad)]
    ).astype(F32)
    down_own = jnp.pad(down_weight, ((0, ffn_pad - ffn_own), (0, 0)))

    normed_grad_two, ffn_out, grad_both, grad_down, bias_share, down_bias_share = feed_forward(
        hidden_two, out_cotangent, both_own, both_bias, down_own, rows
    )
    layer_output = (residual_mid + (ffn_out + bias_down)).astype(BF16)
    rms_values = jnp.stack(
        [jnp.sqrt(square_one[:, 0] + EPSILON), jnp.sqrt(square_two[:, 0] + EPSILON)], axis=0
    )
    grad_down = grad_down[:ffn_own]
    grad_both = swap(grad_both.astype(BF16).reshape(peers, rows, 2 * ffn_pad)).transpose(1, 0, 2)
    grad_both = grad_both.astype(F32)
    grad_gate = grad_both[:, :, :ffn_own].reshape(rows, peers * ffn_own)
    grad_up = grad_both[:, :, ffn_pad : ffn_pad + ffn_own].reshape(rows, peers * ffn_own)

    norm2_part = jnp.sum(normed_grad_two * normed_two, axis=0)
    weighted_two = normed_grad_two * gain_two
    mid_grad = out_cotangent.astype(F32) + scale_two * (
        weighted_two - normed_two * jnp.mean(weighted_two * normed_two, axis=1, keepdims=True)
    )
    mid_grad_low = mid_grad.astype(BF16)
    attention_grad = dot(mid_grad_low, out_full, ((1,), (1,))).astype(BF16)
    grad_out = sum_rows(dot(attention, mid_grad_low, ((0,), (0,))), 640, 2, "sum_grad_out")

    query_grad, kv_part = attend_back(place, queries, kv_window, logs, attention_grad)
    kv_partial = lax.dynamic_update_slice_in_dim(
        jnp.zeros((peers * tok_rows, 2 * HD), BF16), kv_part.astype(BF16), window_start, 0
    )
    kv_grad = sum_rows(kv_partial, 256, 3, "sum_grad_kv")
    query_raw_grad = (
        rotate(
            query_grad.reshape(tok_rows, heads, HD) * query_scale,
            cosine[:, None, :],
            -sine_table[:, None, :],
            quarter,
        )
        .reshape(tok_rows, query_cols)
        .astype(BF16)
    )
    key_raw_grad = rotate(kv_grad[:, :HD], cosine, -sine_table, quarter)
    kv_raw_grad = jnp.concatenate([key_raw_grad, kv_grad[:, HD:]], axis=1).astype(BF16)
    proj_grad = jnp.concatenate([query_raw_grad, kv_raw_grad], axis=1)
    normed_grad_one = dot(proj_grad, proj_full, ((1,), (1,)))
    norm1_part = jnp.sum(normed_grad_one * normed_one, axis=0)
    weighted_one = normed_grad_one * gain_one
    input_grad = (
        mid_grad
        + scale_one
        * (weighted_one - normed_one * jnp.mean(weighted_one * normed_one, axis=1, keepdims=True))
    ).astype(BF16)

    parts = pad_columns(jnp.stack([norm1_part, norm2_part], axis=1), LANES)
    tail = jnp.concatenate([dot(hidden_one, proj_grad, ((0,), (0,))), parts], axis=1)
    tail = sum_rows(tail, 640, 4, "sum_grad_proj")
    grad_proj = tail[:, :proj_cols]
    norm1_share = tail[:, proj_cols]
    norm2_share = tail[:, proj_cols + 1]
    return (
        layer_output,
        residual_mid,
        rms_values,
        input_grad,
        norm1_share,
        grad_proj[:, :query_cols],
        grad_proj[:, query_cols:],
        grad_out,
        norm2_share,
        grad_gate,
        bias_share[:ffn_own],
        grad_up,
        bias_share[ffn_pad : ffn_pad + ffn_own],
        grad_down,
        down_bias_share,
    )


def solution(mesh):
    by_rows, by_entry = P(AXIS, None), P(AXIS)
    in_specs = (
        by_rows,
        by_entry,
        by_rows,
        by_rows,
        by_rows,
        by_entry,
        by_rows,
        by_entry,
        by_rows,
        by_entry,
        by_rows,
        by_entry,
        by_rows,
    )
    out_specs = (
        by_rows,
        by_rows,
        P(None, AXIS),
        by_rows,
        by_entry,
        by_rows,
        by_rows,
        by_rows,
        by_entry,
        by_rows,
        by_entry,
        by_rows,
        by_entry,
        by_rows,
        by_entry,
    )
    return jax.shard_map(body, mesh=mesh, in_specs=in_specs, out_specs=out_specs, check_vma=False)
```

time: 4220 us -> 1240 us (0.29)
  waiting for transfers between devices: 3490 us -> 540 us
  Pallas kernels: 0 us -> 439 us
  matrix products: 362 us -> 144 us
  starting transfers between devices: 120 us -> 9.19 us
  local copies, waits for them, and re-layouts: 109 us -> 51 us
  blocking collectives: 43.5 us -> 0 us
    reduce_scatter x8 -> x0, waiting for transfers between devices: 2750 us -> none  [reduce_rows(): lax.psum_scatter(term(jnp.int32(0), lax.axis_size('blk') * rows), 'blk',...]
    pallas_call x0 -> x7, Pallas kernels: none -> 439 us  [the longest x5 411 us: sum_over_devices(): pl.pallas_call(functools.partial(sum_kernel, chunk), out_shape=jax.ShapeD...]
    dot_general x190 -> x12, matrix products: 362 us -> 144 us  [the longest x8 102 us: dot(): lax.dot_general(left, right, (contract, ((), ())), preferred_element_type...]
    ppermute x32 -> x0, starting transfers between devices: 119 us -> none  [from_behind(): return lax.ppermute(x, axis, pairs)]
    all_gather x6 -> x5, waiting for transfers between devices: 656 us -> 539 us  [gather_rows(): return lax.all_gather(values, AXIS, axis=0, tiled=True)]
    ppermute x32 -> x0, waiting for transfers between devices: 83.7 us -> none  [from_behind(): return lax.ppermute(x, axis, pairs)]
    squeeze x51 -> x0, local copies, waits for them, and re-layouts: 46.8 us -> none  [the longest x34 31.1 us: block_terms(): kv_block = lax.dynamic_index_in_dim(stacked, offset, 0, keepdims=False)]
    unnamed x1 -> x0, blocking collectives: 43.5 us -> none
  transfers between devices with their start and end apart: 47 -> 7, of which waited for: 46 -> 5; matrix products, arithmetic and copies ran while one was open for 7% -> 8% of each run, Pallas kernels for 0% -> 14%
where the time goes in v1:
time: 1240 us
  waiting for transfers between devices  540 us (44%)
  Pallas kernels  439 us (35%)
  matrix products  144 us (12%)
  local copies, waits for them, and re-layouts  51 us (4%)
  other arithmetic  41.9 us (3%)
  between operations  14.9 us (1%)
    all_gather x5, waiting for transfers between devices, gather_rows(): return lax.all_gather(values, AXIS, axis=0, tiled=True)  539 us
    pallas_call x5, Pallas kernels, sum_over_devices(): pl.pallas_call(functools.partial(sum_kernel, chunk), out_shape=jax.ShapeD...  411 us
    dot_general x8, matrix products, dot(): lax.dot_general(left, right, (contract, ((), ())), preferred_element_type...  102 us
  transfers between devices with their start and end apart: 7, of which 5 were waited for; matrix products, arithmetic and copies ran while one was open for 8% of the time, Pallas kernels for 14%

profile of v1, /device:TPU:0, one launch (start us, length us, event | category | flops | bytes accessed | tf_op | source)
XLA Modules:
  0.0 1239.6 jit_solution(2155703219781729253)
XLA Ops:
  8.0 1.9 fusion.33
  11.9 115.4 %all-gather.6.cloned.1.call-done = bf16[2560,3200]{1,0:T(8,128)(2,1)} async-done(((bf16[80,3200]{1,0:T(8,128)(2,1)}), bf16[2560,3200]{1,0:T(8,128)(2,1)}) %all-gather.6.cloned.1.call-update) | async-done | bytes 16384016 | tf_op jit(solution)/shard_map/all_gather | solution.py:298
  128.4 1.8 slice_reduce_fusion
  130.2 6.8 fusion.2
  144.3 56.0 %all-gather.8.cloned.1.call-done = bf16[4096,512]{1,0:T(8,128)(2,1)} async-done(((bf16[128,512]{1,0:T(8,128)(2,1)}), bf16[4096,512]{1,0:T(8,128)(2,1)}) %all-gather.8.cloned.1.call-update) | async-done | bytes 4194320 | tf_op jit(solution)/shard_map/all_gather | solution.py:298
  200.3 1.8 constant_dynamic-slice_fusion.kv_ref
  202.0 10.8 attend.1
  213.7 86.5 %all-gather.10.cloned.1.call-done = bf16[2560,2560]{1,0:T(8,128)(2,1)} async-done(((bf16[80,2560]{1,0:T(8,128)(2,1)}), bf16[2560,2560]{1,0:T(8,128)(2,1)}) %all-gather.10.cloned.1.call-update) | async-done | bytes 13107216 | tf_op jit(solution)/shard_map/all_gather | solution.py:298
  300.2 6.8 multiply_reduce_fusion.2
  309.1 4.9 reshape.242
  314.0 4.8 reshape.243
  318.9 2.4 fusion.14
  321.3 2.9 copy.81
  324.3 3.9 all-to-all-start
  328.9 147.1 %all-gather.14.cloned.1.call-done = bf16[4096,2560]{1,0:T(8,128)(2,1)} async-done(((bf16[128,2560]{1,0:T(8,128)(2,1)}), bf16[4096,2560]{1,0:T(8,128)(2,1)}) %all-gather.14.cloned.1.call-update) | async-done | bytes 20971536 | tf_op jit(solution)/shard_map/all_gather | solution.py:298
  476.0 2.7 convert_reduce_fusion.1
  478.7 133.7 %all-gather.12.cloned.1.call-done = bf16[4096,2560]{1,0:T(8,128)(2,1)} async-done(((bf16[128,2560]{1,0:T(8,128)(2,1)}), bf16[4096,2560]{1,0:T(8,128)(2,1)}) %all-gather.12.cloned.1.call-update) | async-done | bytes 20971536 | tf_op jit(solution)/shard_map/all_gather | solution.py:298
  612.4 18.0 %convolution_add_fusion = f32[4096,512]{0,1:T(8,128)} fusion(bf16[4096,2560]{1,0:T(8,128)(2,1)} %all-gather.12.cloned.1.call-done, bf16[2560,512]{1,0:T(8,128)(2,1)} %bitcast.8, f32[512]{0:T(512)S(1)} %fusion.56), kind=kOutput, calls=%fused_computation.10 | convolution fusion | flops 10739515392 | bytes 31983616 | tf_op jit(solution)/shard_map/dot_general | solution.py:323
  630.4 15.9 %fusion.12 = (bf16[4096,256]{0,1:T(8,128)(2,1)}, bf16[4096,256]{0,1:T(8,128)(2,1)}, bf16[4096,256]{0,1:T(8,128)(2,1)}) fusion(f32[4096,512]{0,1:T(8,128)} %convolution_add_fusion, bf16[4096,2560]{1,0:T(8,128)(2,1)} %all-gather.14.cloned.1.call-done, bf16[240,2560]{1,0:T(8,128)(2,1)} %param.23), kind=kOutput, calls=%fused_computation.26 | convolution fusion | flops 5395972096 | bytes 36880384 | tf_op jit(solution)/shard_map/dot_general | solution.py:49
  646.4 18.6 %convolution_convert_fusion = bf16[4096,2560]{1,0:T(8,128)(2,1)} fusion(bf16[2560,512]{1,0:T(8,128)(2,1)} %bitcast.8, bf16[4096,256]{0,1:T(8,128)(2,1)} %get-tuple-element.33, bf16[4096,256]{0,1:T(8,128)(2,1)} %get-tuple-element.32), kind=kOutput, calls=%fused_computation | convolution fusion | flops 10756292608 | bytes 27787264 | tf_op jit(solution)/shard_map/dot_general | solution.py:49
  665.0 105.4 %sum_hidden.3 = f32[128,2560]{1,0:T(8,128)} custom-call(bf16[4,2,2,2,128,2560]{5,4,3,2,1,0:T(8,128)(2,1)} %bitcast.42), custom_call_target="tpu_custom_call" | custom-call | tf_op jit(solution)/shard_map/sum_hidden/pallas_call | solution.py:284
  770.4 1.9 multiply_reduce_fusion
  772.4 10.2 convolution_convert_fusion.1
  782.5 104.6 %sum_hidden.2 = f32[128,2560]{1,0:T(8,128)} custom-call(bf16[4,2,2,2,128,2560]{5,4,3,2,1,0:T(8,128)(2,1)} %bitcast.39), custom_call_target="tpu_custom_call" | custom-call | tf_op jit(solution)/shard_map/sum_hidden/pallas_call | solution.py:284
  887.2 2.7 multiply_add_fusion
  889.9 9.5 convolution_convert_fusion.5.grad_ref
  899.5 16.7 %attend_back.1 = (f32[128,2560]{1,0:T(8,128)S(1)}, f32[2176,512]{1,0:T(8,128)}) custom-call(s32[1]{0:T(128)} %bitcast.place_ref, bf16[128,2560]{1,0:T(8,128)(2,1)S(1)} %copy.80.query_ref, bf16[2176,512]{1,0:T(8,128)(2,1)S(1)} %constant_dynamic-slice_fusion.kv_ref, f32[5,256,128]{2,1,0:T(8,128)S(1)} %copy-done.5, ...), custom_call_target="tpu_custom_call" | custom-call | flops 7130316800 | bytes 8912896 | tf_op jit(solution)/shard_map/attend_back/pallas_call | solution.py:152
  917.2 2.6 convert_dynamic-update-slice_fusion
  919.9 1.9 copy-done.10
  921.8 34.0 %sum_grad_kv.1 = f32[128,512]{1,0:T(8,128)} custom-call(bf16[4,2,2,2,128,512]{5,4,3,2,1,0:T(8,128)(2,1)} %bitcast.43), custom_call_target="tpu_custom_call" | custom-call | tf_op jit(solution)/shard_map/sum_grad_kv/pallas_call | solution.py:284
  958.0 17.0 %convolution_convert_fusion.4 = bf16[2560,512]{1,0:T(8,128)(2,1)} fusion(bf16[4096,2560]{1,0:T(8,128)(2,1)} %all-gather.12.cloned.1.call-done, bf16[4096,256]{0,1:T(8,128)(2,1)} %get-tuple-element.33, bf16[4096,256]{0,1:T(8,128)(2,1)S(1)} %copy-done.18), kind=kOutput, calls=%fused_computation.19 | convolution fusion | flops 10747117568 | bytes 27787264 | tf_op jit(solution)/shard_map/dot_general | solution.py:49
  975.0 4.9 all-to-all-start.1
  980.1 1.5 copy.83
  984.3 9.4 convolution_convert_fusion.3
  993.8 13.5 %fusion.27 = (bf16[2560]{0:T(1024)(128)(2,1)S(1)}, f32[128]{0:T(128)S(1)}, f32[128,2560]{1,0:T(8,128)}) fusion(bf16[128,2560]{1,0:T(8,128)(2,1)S(1)} %copy-done.13, f32[128]{0:T(128)S(1)} %get-tuple-element.55, f32[2560]{0:T(1024)S(1)} %copy-done.28, bf16[2560,3200]{1,0:T(8,128)(2,1)} %all-gather.6.cloned.1.call-done, bf16[128,384]{0,1:T(8,128)(2,1)S(1)} %copy.87, ...), kind=kOutput, calls=%fused_computation.51 | convolution fusion | flops 2018702720 | bytes 18497536 | tf_op jit(solution)/shard_map/dot_general | solution.py:49
  1007.8 13.5 %pad_maximum_fusion.in_ref = bf16[4,2,2,2,80,3200]{5,4,3,2,1,0:T(8,128)(2,1)} fusion(bf16[4,2,2,2,80,128]{5,4,3,2,1,0:T(8,128)(2,1)S(1)} %bitcast.52, bf16[4,2,2,2,80,3072]{5,4,3,2,1,0:T(8,128)(2,1)} %bitcast.40), kind=kLoop, calls=%fused_computation.4 | loop fusion | flops 32768000 | bytes 32768000 | tf_op jit(solution)/shard_map/concatenate | solution.py:493
  1021.3 93.0 %sum_grad_proj.1 = f32[80,3200]{1,0:T(8,128)} custom-call(bf16[4,2,2,2,80,3200]{5,4,3,2,1,0:T(8,128)(2,1)} %pad_maximum_fusion.in_ref), custom_call_target="tpu_custom_call" | custom-call | tf_op jit(solution)/shard_map/sum_grad_proj/pallas_call | solution.py:284
  1114.3 1.7 slice.127
  1116.1 2.1 slice.126
  1118.2 7.0 convolution_convert_fusion.2
  1125.1 74.4 %sum_grad_out.1 = f32[80,2560]{1,0:T(8,128)} custom-call(bf16[4,2,2,2,80,2560]{5,4,3,2,1,0:T(8,128)(2,1)} %bitcast.41), custom_call_target="tpu_custom_call" | custom-call | tf_op jit(solution)/shard_map/sum_grad_out/pallas_call | solution.py:284
  1199.5 1.6 slice_reduce_fusion.3
  1203.7 11.1 fusion.15
  1214.8 2.5 convert_bitcast_fusion
  1217.7 3.0 copy.90
  1220.8 3.9 reshape.251
  1224.7 3.0 copy.89
  1227.7 4.0 reshape.250
  (130 shorter events, 25.4 us)
Async XLA Ops:
  7.2 120.1 %all-gather.6.cloned.1.call-start = ((), (), s32[]{:S(2)}) async-start(), calls=%async_computation.2 | async-start | bytes 16896000 | tf_op jit(solution)/shard_map/all_gather | solution.py:298
  9.9 190.3 %all-gather.8.cloned.1.call-start = ((), (), s32[]{:S(2)}) async-start(), calls=%async_computation.3 | async-start | bytes 4325376 | tf_op jit(solution)/shard_map/all_gather | solution.py:298
  10.0 127.1 %copy-start.30 = (f32[64]{0:T(128)}, f32[64]{0:T(128)S(1)}, u32[]{:S(2)}) copy-start(f32[64]{0:T(128)S(1)} %negate_power_fusion) | copy-start | bytes 772
  10.0 127.0 %copy-start.32 = (f32[128]{0:T(128)}, f32[128]{0:T(128)S(1)}, u32[]{:S(2)}) copy-start(f32[128]{0:T(128)S(1)} %add_convert_fusion.2) | copy-start | bytes 1540
  128.4 1.8 copy-start.12
  130.2 6.8 copy-start.27
  137.0 1.1 copy-start.21
  139.9 160.3 %all-gather.10.cloned.1.call-start = ((), (), s32[]{:S(2)}) async-start(), calls=%async_computation.4 | async-start | bytes 13516800 | tf_op jit(solution)/shard_map/all_gather | solution.py:298
  140.6 335.4 %all-gather.14.cloned.1.call-start = ((), (), s32[]{:S(2)}) async-start(), calls=%async_computation.6 | async-start | bytes 21626880 | tf_op jit(solution)/shard_map/all_gather | solution.py:298
  141.2 471.2 %all-gather.12.cloned.1.call-start = ((), (), s32[]{:S(2)}) async-start(), calls=%async_computation.5 | async-start | bytes 21626880 | tf_op jit(solution)/shard_map/all_gather | solution.py:298
  143.4 0.6 copy-start.24
  212.9 0.8 copy-start.4
  213.7 93.3 %copy-start = (bf16[128,2560]{1,0:T(8,128)(2,1)}, bf16[128,2560]{1,0:T(8,128)(2,1)S(1)}, u32[]{:S(2)}) copy-start(bf16[128,2560]{1,0:T(8,128)(2,1)S(1)} %get-tuple-element.19) | copy-start | bytes 1966084
  307.0 1.1 copy-start.8
  324.2 3.9 copy-start.34
  324.2 4.0 copy-start.35
  324.2 4.0 copy-start.26
  324.2 4.1 copy-start.36
  324.3 154.5 %all-to-all-start = ((bf16[32,80,512]{2,1,0:T(8,128)(2,1)}), bf16[32,80,512]{2,1,0:T(8,128)(2,1)}, u32[]{:S(2)}, u32[]{:S(2)}) async-start(bf16[32,80,512]{2,1,0:T(8,128)(2,1)} %copy.81), calls=%async_computation | async-start | bytes 5242880 | tf_op jit(solution)/shard_map/all_to_all | solution.py:310
  665.0 105.4 %copy-start.9 = (f32[128,2560]{1,0:T(8,128)S(1)}, f32[128,2560]{1,0:T(8,128)}, u32[]{:S(2)}) copy-start(f32[128,2560]{1,0:T(8,128)} %copy-done.8) | copy-start | bytes 3932164
  665.0 107.3 %copy-start.23 = (bf16[240,2560]{1,0:T(8,128)(2,1)S(1)}, bf16[240,2560]{1,0:T(8,128)(2,1)}, u32[]{:S(2)}) copy-start(bf16[240,2560]{1,0:T(8,128)(2,1)} %param.23) | copy-start | bytes 3686404
  770.4 2.0 copy-start.15
  782.5 104.6 %copy-start.11 = (f32[128,2560]{1,0:T(8,128)S(1)}, f32[128,2560]{1,0:T(8,128)}, u32[]{:S(2)}) copy-start(f32[128,2560]{1,0:T(8,128)} %sum_hidden.3) | copy-start | bytes 3932164
  782.5 104.6 %copy-start.17 = (bf16[128,2560]{1,0:T(8,128)(2,1)S(1)}, bf16[128,2560]{1,0:T(8,128)(2,1)}, u32[]{:S(2)}) copy-start(bf16[128,2560]{1,0:T(8,128)(2,1)} %param.25) | copy-start | bytes 1966084
  782.5 104.7 %copy-start.29 = (f32[2560]{0:T(1024)S(1)}, f32[2560]{0:T(1024)}, u32[]{:S(2)}) copy-start(f32[2560]{0:T(1024)} %get-tuple-element.27) | copy-start | bytes 30724
  889.9 9.6 copy-start.6
  889.9 9.6 copy-start.5
  916.1 1.1 copy-start.2
  919.9 1.9 copy-start.10
  921.8 34.0 %copy-start.31 = (f32[64]{0:T(128)S(1)}, f32[64]{0:T(128)}, u32[]{:S(2)}) copy-start(f32[64]{0:T(128)} %copy-done.30) | copy-start | bytes 772
  921.8 34.0 %copy-start.33 = (f32[128]{0:T(128)S(1)}, f32[128]{0:T(128)}, u32[]{:S(2)}) copy-start(f32[128]{0:T(128)} %copy-done.32) | copy-start | bytes 1540
  921.8 36.2 %copy-start.18 = (bf16[4096,256]{0,1:T(8,128)(2,1)S(1)}, bf16[4096,256]{0,1:T(8,128)(2,1)}, u32[]{:S(2)}) copy-start(bf16[4096,256]{0,1:T(8,128)(2,1)} %get-tuple-element.32) | copy-start | bytes 6291460
  975.0 4.9 copy-start.3
  975.0 239.7 %all-to-all-start.1 = ((bf16[32,80,512]{2,1,0:T(8,128)(2,1)}), bf16[32,80,512]{2,1,0:T(8,128)(2,1)}, u32[]{:S(2)}, u32[]{:S(2)}) async-start(bf16[32,80,512]{2,1,0:T(8,128)(2,1)} %bitcast.50), calls=%async_computation.1 | async-start | bytes 5242880 | tf_op jit(solution)/shard_map/all_to_all | solution.py:310
  980.0 3.0 copy-start.25
  981.6 2.7 copy-start.13
  981.6 2.7 copy-start.28
  1114.3 3.9 copy-start.1
  1114.3 3.8 copy-start.7
  1125.1 76.0 %copy-start.19 = (bf16[4096,256]{0,1:T(8,128)(2,1)S(1)}, bf16[4096,256]{0,1:T(8,128)(2,1)}, u32[]{:S(2)}) copy-start(bf16[4096,256]{0,1:T(8,128)(2,1)} %get-tuple-element.32) | copy-start | bytes 6291460
  1125.1 76.0 %copy-start.20 = (bf16[4096,256]{0,1:T(8,128)(2,1)S(1)}, bf16[4096,256]{0,1:T(8,128)(2,1)}, u32[]{:S(2)}) copy-start(bf16[4096,256]{0,1:T(8,128)(2,1)} %get-tuple-element.33) | copy-start | bytes 6291460
  1201.1 1.3 copy-start.22
  1201.7 2.0 copy-start.16
  1227.7 4.0 copy-start.14
Sparse Core Ops, SparseCore 0:
  11.4 115.7 all-gather.5
  140.0 60.1 all-gather.7
  203.1 97.0 all-gather.9
  302.9 173.0 all-gather.13
  479.3 133.0 all-gather.11

commit v2 on v1

--- a/solution.py
+++ b/solution.py
@@ -39,10 +39,6 @@
         ],
         axis=-1,
     )
-
-
-def gelu_tanh(values):
-    return jax.nn.gelu(values, approximate=True)
 
 
 def dot(left, right, contract):
@@ -294,8 +290,259 @@
     )(partial.reshape(4, 2, 2, 2, rows, columns))
 
 
-def gather_rows(values):
-    return lax.all_gather(values, AXIS, axis=0, tiled=True)
+PLANES=4
+def plane_order(z):
+    near = jnp.minimum(z, 3 - z)
+    flip = z // 2
+    order = []
+    for k in range(4):
+        swapped = 1 - k if k < 2 else k
+        plane = near * swapped + (1 - near) * k
+        order.append(flip * (3 - plane) + (1 - flip) * plane)
+    return order
+
+class Gather:
+    COPIES = 11
+    def __init__(self, place, own, held, cols, sems):
+        self.place, self.held, self.cols, self.sems = place, held, cols, sems
+        self.own = own.at[:, cols]
+        rows = held.shape[4]
+        upper = (rows // 2 + TILE - 1) // TILE * TILE
+        self.halves = pl.ds(0, upper), pl.ds(upper, rows - upper)
+        self.order = plane_order(place.z)
+        self.sent = []
+        self.kept = []
+    def at(self, plane, y, x, core, part=slice(None)):
+        return self.held.at[plane, y, x, core, part, self.cols]
+    def pair(self, slot, k):
+        return self.sems.at[0, slot, k], self.sems.at[1, slot, k]
+    def push(self, src, dst, slot, k, device):
+        copy = send(src, dst, self.pair(slot, k), device)
+        self.sent.append(copy)
+    def arrived(self, ref, slot, k):
+        pltpu.make_async_remote_copy(src_ref=ref, dst_ref=ref, send_sem=self.sems.at[0, slot, k], recv_sem=self.sems.at[1, slot, k], device_id=(self.place.sibling,), device_id_type=MESH).wait_recv()
+    def start(self):
+        p = self.place
+        mine = self.at(p.z, p.y, p.x, p.core)
+        keep = pltpu.make_async_copy(self.own, mine, self.sems.at[0, 10, 0])
+        keep.start()
+        self.kept.append(keep)
+        for k in (1, 2, 3):
+            plane = self.order[k]
+            copy = pltpu.make_async_remote_copy(src_ref=self.own, dst_ref=mine, send_sem=self.sems.at[0, 0, k], recv_sem=self.sems.at[1, 0, p.z], device_id=(p.index(plane, p.y, p.x, p.core),), device_id_type=MESH)
+            copy.start(); self.sent.append(copy)
+    def line(self, k):
+        p = self.place
+        plane = self.order[k]
+        block = self.at(plane, p.y, p.x, p.core)
+        source = self.own if k == 0 else block
+        if k > 0:
+            pltpu.make_async_remote_copy(src_ref=block, dst_ref=block, send_sem=self.sems.at[0, 0, k], recv_sem=self.sems.at[1, 0, plane], device_id=(p.sibling,), device_id_type=MESH).wait_recv()
+        self.push(source, block, 1, k, p.next_x)
+        self.push(source, block, 2, k, p.next_y)
+        self.push(source, block, 5, k, p.sibling)
+    def side(self, k):
+        p, plane = self.place, self.order[k]
+        top, bottom = self.halves
+        self.arrived(self.at(plane, p.y, 1 - p.x, p.core), 1, k)
+        block = self.at(plane, p.y, 1 - p.x, p.core, top)
+        self.push(block, block, 4, k, p.next_y)
+        block = self.at(plane, p.y, 1 - p.x, p.core)
+        self.push(block, block, 6, k, p.sibling)
+        self.arrived(self.at(plane, 1 - p.y, p.x, p.core), 2, k)
+        block = self.at(plane, 1 - p.y, p.x, p.core, bottom)
+        self.push(block, block, 3, k, p.next_x)
+        block = self.at(plane, 1 - p.y, p.x, p.core)
+        self.push(block, block, 7, k, p.sibling)
+    def diag(self, k):
+        p, plane = self.place, self.order[k]
+        for slot, part in ((4, self.halves[0]), (3, self.halves[1])):
+            block = self.at(plane, 1 - p.y, 1 - p.x, p.core, part)
+            self.arrived(block, slot, k)
+            self.push(block, block, slot + 5, k, p.sibling)
+    def ready(self, k):
+        p, plane = self.place, self.order[k]
+        top, bottom = self.halves
+        if k == 0:
+            for keep in self.kept: keep.wait()
+        other = 1 - p.core
+        self.arrived(self.at(plane, p.y, p.x, other), 5, k)
+        self.arrived(self.at(plane, p.y, 1 - p.x, other), 6, k)
+        self.arrived(self.at(plane, 1 - p.y, p.x, other), 7, k)
+        self.arrived(self.at(plane, 1 - p.y, 1 - p.x, other, top), 9, k)
+        self.arrived(self.at(plane, 1 - p.y, 1 - p.x, other, bottom), 8, k)
+    def finish(self):
+        for copy in self.sent: copy.wait_send()
+
+def pipeline(stages, count):
+    for step in range(count + len(stages) - 1):
+        for s in range(len(stages) - 1, -1, -1):
+            if 0 <= step - s < count:
+                stages[s](step - s)
+
+def gather_kernel(chunks, *refs):
+    n = len(chunks)
+    ins, outs, sems = refs[:n], refs[n:2*n], refs[2*n:]
+    place = Place()
+    place.meet()
+    items = []
+    for a in range(n):
+        width = ins[a].shape[1] // chunks[a]
+        for j in range(chunks[a]):
+            items.append(Gather(place, ins[a], outs[a], pl.ds(j * width, width), sems[a].at[j]))
+    def line(s):
+        if s % PLANES == 0:
+            items[s // PLANES].start()
+        items[s // PLANES].line(s % PLANES)
+    def side(s): items[s // PLANES].side(s % PLANES)
+    def diag(s): items[s // PLANES].diag(s % PLANES)
+    pipeline([line, side, diag], len(items) * PLANES)
+    for item in items:
+        for k in range(PLANES): item.ready(k)
+    for item in items: item.finish()
+
+def gather_all(arrays, chunks, collective_id, name):
+    outs = pl.pallas_call(
+        functools.partial(gather_kernel, chunks),
+        out_shape=tuple(jax.ShapeDtypeStruct((4,2,2,2)+a.shape, BF16) for a in arrays),
+        in_specs=[pl.BlockSpec(memory_space=pl.ANY)]*len(arrays),
+        out_specs=tuple(pl.BlockSpec(memory_space=pl.ANY) for _ in arrays),
+        scratch_shapes=[pltpu.SemaphoreType.DMA((c, 2, Gather.COPIES, PLANES)) for c in chunks],
+        compiler_params=pltpu.CompilerParams(collective_id=collective_id, has_side_effects=True),
+        name=name,
+    )(*arrays)
+    return [o.reshape(32 * a.shape[0], a.shape[1]) for o, a in zip(outs, arrays)]
+
+
+GELU_SCALE = math.sqrt(2.0 / math.pi)
+GELU_CUBE = 0.044715
+
+def gelu_and_slope(v):
+    square = v * v
+    t = jnp.tanh(GELU_SCALE * v * (1.0 + GELU_CUBE * square))
+    half = 0.5 * (1.0 + t)
+    slope = half + 0.5 * v * (1.0 - t * t) * (GELU_SCALE * (1.0 + 3.0 * GELU_CUBE * square))
+    return v * half, slope
+
+def ffn_kernel(hidden_ref, cotangent_ref, both_ref, down_ref, bias_ref,
+               hidden_out, ffn_out, grad_both_ref, grad_down_ref, bias_grad_ref,
+               held, cot, both_keep, ffn_keep, stage, gather_sems, cot_sems, out_sems):
+    place = Place()
+    width = hidden_ref.shape[1]
+    pad = down_ref.shape[0]
+    rows = 2 * hidden_ref.shape[0]
+    order = plane_order(place.z)
+    fetch = [pltpu.make_async_copy(cotangent_ref.at[order[k]], cot.at[k % 2], cot_sems.at[k]) for k in range(PLANES)]
+    fetch[0].start()
+    fetch[1].start()
+    place.meet()
+    gather = Gather(place, hidden_ref, held, pl.ds(0, width), gather_sems)
+    gather.start()
+    grad_both_ref[...] = jnp.zeros_like(grad_both_ref)
+    grad_down_ref[...] = jnp.zeros_like(grad_down_ref)
+    bias_grad_ref[...] = jnp.zeros_like(bias_grad_ref)
+
+    def emit(kind, slot, plane, y, x):
+        target = (hidden_out, ffn_out)[kind]
+        return pltpu.make_async_copy(stage.at[kind, slot], target.at[plane, y, x], out_sems.at[kind, slot])
+
+    def compute(k):
+        plane = order[k]
+        fetch[k].wait()
+        @pl.loop(0, 4)
+        def _(i):
+            y, x, slot = i // 2, i % 2, i % 2
+            hidden = held[plane, y, x].reshape(rows, width)
+            cotangent = cot[k % 2, y, x].reshape(rows, width)
+            both_pre = dot(hidden, both_ref[...], ((1,), (0,))) + bias_ref[0:1]
+            hidden_grad = dot(cotangent, down_ref[...], ((1,), (1,)))
+            activated, slope = gelu_and_slope(both_pre[:, :pad])
+            up_pre = both_pre[:, pad:]
+            hidden_ffn = (activated * up_pre).astype(BF16)
+            both_grad = jnp.concatenate([(hidden_grad * up_pre * slope).astype(BF16), (hidden_grad * activated).astype(BF16)], axis=1)
+            here = pl.ds(pl.multiple_of(i * rows, rows), rows)
+            both_keep[here] = both_grad
+            ffn_keep[here] = hidden_ffn
+            bias_grad_ref[...] += jnp.sum(both_grad.astype(F32), axis=0, keepdims=True)
+            def drain():
+                for kind in range(2): emit(kind, slot, plane, y, x).wait()
+            if k > 0: drain()
+            else: pl.when(i >= 2)(drain)
+            half = stage.shape[3]
+            stage[0, slot] = dot(both_grad, both_ref[...], ((1,), (1,))).astype(BF16).reshape(2, half, width)
+            emit(0, slot, plane, y, x).start()
+            stage[1, slot] = dot(hidden_ffn, down_ref[...], ((1,), (0,))).astype(BF16).reshape(2, half, width)
+            emit(1, slot, plane, y, x).start()
+        step = 512
+        @pl.loop(0, width // step)
+        def _(j):
+            cols = pl.ds(pl.multiple_of(j * step, step), step)
+            hidden = held[plane, :, :, :, :, cols].reshape(4 * rows, step)
+            grad_both_ref[:, cols] += dot(both_keep[...], hidden, ((0,), (0,)))
+            cotangent = cot[k % 2, :, :, :, :, cols].reshape(4 * rows, step)
+            grad_down_ref[:, cols] += dot(ffn_keep[...], cotangent, ((0,), (0,)))
+        if k + 2 < PLANES: fetch[k + 2].start()
+
+    gather.line(0)
+    gather.line(1)
+    gather.side(0)
+    gather.line(2)
+    gather.side(1)
+    gather.diag(0)
+    gather.ready(0)
+    compute(0)
+    gather.line(3)
+    gather.side(2)
+    gather.diag(1)
+    gather.side(3)
+    gather.ready(1)
+    compute(1)
+    gather.diag(2)
+    gather.diag(3)
+    gather.ready(2)
+    compute(2)
+    gather.ready(3)
+    compute(3)
+    for slot in range(2):
+        for kind in range(2): emit(kind, slot, 0, 0, 0).wait()
+    gather.finish()
+
+def ffn(hidden_two, cotangent_full, both_own, both_bias, down_own, collective_id):
+    tok_rows, width = hidden_two.shape
+    pad = down_own.shape[0]
+    full = (4, 2, 2, 2, tok_rows, width)
+    hbm = pl.BlockSpec(memory_space=pl.ANY)
+    vmem = pl.BlockSpec(memory_space=pltpu.VMEM)
+    dma = pltpu.SemaphoreType.DMA
+    hidden_part, ffn_part, grad_both, grad_down, bias_grad = pl.pallas_call(
+        ffn_kernel,
+        out_shape=(
+            jax.ShapeDtypeStruct(full, BF16),
+            jax.ShapeDtypeStruct(full, BF16),
+            jax.ShapeDtypeStruct((2 * pad, width), F32),
+            jax.ShapeDtypeStruct((pad, width), F32),
+            jax.ShapeDtypeStruct((8, 2 * pad), F32),
+        ),
+        in_specs=[hbm, hbm, vmem, vmem, vmem],
+        out_specs=(hbm, hbm, vmem, vmem, vmem),
+        scratch_shapes=[
+            pltpu.VMEM(full, BF16),
+            pltpu.VMEM((2,) + full[1:], BF16),
+            pltpu.VMEM((8 * tok_rows, 2 * pad), BF16),
+            pltpu.VMEM((8 * tok_rows, pad), BF16),
+            pltpu.VMEM((2, 2, 2, tok_rows, width), BF16),
+            dma((2, Gather.COPIES, PLANES)), dma((PLANES,)), dma((2, 2)),
+        ],
+        compiler_params=pltpu.CompilerParams(collective_id=collective_id, has_side_effects=True, vmem_limit_bytes=62*1024*1024),
+        name="feed_forward",
+    )(hidden_two, cotangent_full.reshape(full), both_own, down_own, jnp.broadcast_to(both_bias, (8, 2 * pad)))
+    return (hidden_part.reshape(32 * tok_rows, width), ffn_part.reshape(32 * tok_rows, width), grad_both, grad_down, bias_grad[0])
+
+
+def gather_rows(arrays, collective_id, name):
+    if lax.axis_size(AXIS) == DEVICES:
+        return gather_all(arrays, [1] * len(arrays), collective_id, name)
+    return [lax.all_gather(values, AXIS, axis=0, tiled=True) for values in arrays]
 
 
 def sum_rows(partial, chunk, collective_id, name):
@@ -310,53 +557,58 @@
     return lax.all_to_all(pieces, AXIS, 0, 0, tiled=False)
 
 
-def feed_forward(hidden_two, out_cotangent, both_own, both_bias, down_own, rows):
+def feed_forward(hidden_two, cotangent_full, both_own, both_bias, down_own, rows):
     peers = lax.axis_size(AXIS)
     device = lax.axis_index(AXIS)
     tok_rows, width = hidden_two.shape
     ffn_pad = down_own.shape[0]
+    own_cotangent = lax.dynamic_slice_in_dim(cotangent_full, device * rows, rows, 1)
+    down_bias_share = jnp.sum(own_cotangent.astype(F32), axis=0)
+    if peers == DEVICES:
+        hidden_part, ffn_part, grad_both, grad_down, bias_share = ffn(
+            hidden_two, cotangent_full, both_own, both_bias, down_own, 7
+        )
+        normed_grad = sum_rows(hidden_part, 512, 1, "sum_hidden")
+        ffn_out = sum_rows(ffn_part, 512, 1, "sum_hidden")
+        return normed_grad, ffn_out, grad_both.T, grad_down, bias_share, down_bias_share
 
     def piece(sums, here):
-        hidden_own, cotangent_own = here
-        cotangent_full = gather_rows(cotangent_own)
-        hidden_full = gather_rows(hidden_own)
+        hidden_own, cotangent_piece = here
+        hidden_full = gather_rows([hidden_own], None, None)[0]
         both_pre = jnp.dot(hidden_full, both_own, preferred_element_type=F32) + both_bias
-        gate_pre, up_pre = both_pre[:, :ffn_pad], both_pre[:, ffn_pad:]
-        activated, gelu_pull = jax.vjp(gelu_tanh, gate_pre)
+        activated, slope = gelu_and_slope(both_pre[:, :ffn_pad])
+        up_pre = both_pre[:, ffn_pad:]
         hidden_ffn = (activated * up_pre).astype(BF16)
-        hidden_grad = dot(cotangent_full, down_own, ((1,), (1,)))
-        gate_grad = gelu_pull(hidden_grad * up_pre)[0].astype(BF16)
+        hidden_grad = dot(cotangent_piece, down_own, ((1,), (1,)))
+        gate_grad = (hidden_grad * up_pre * slope).astype(BF16)
         up_grad = (hidden_grad * activated).astype(BF16)
         both_grad = jnp.concatenate([gate_grad, up_grad], axis=1)
-        normed_grad = sum_rows(dot(both_grad, both_own, ((1,), (1,))), 512, 1, "sum_hidden")
+        normed_grad = sum_rows(dot(both_grad, both_own, ((1,), (1,))), None, None, None)
         ffn_out = sum_rows(
-            jnp.dot(hidden_ffn, down_own, preferred_element_type=F32), 512, 1, "sum_hidden"
+            jnp.dot(hidden_ffn, down_own, preferred_element_type=F32), None, None, None
         )
-        own_cotangent = lax.dynamic_slice_in_dim(cotangent_full, device * rows, rows, 1)
         shares = (
             dot(hidden_full, both_grad, ((0,), (0,))),
-            dot(hidden_ffn, cotangent_full, ((0,), (0,))),
+            dot(hidden_ffn, cotangent_piece, ((0,), (0,))),
             jnp.sum(both_grad.astype(F32), axis=0),
-            jnp.sum(own_cotangent.astype(F32), axis=0),
         )
-        if sums is not None:
-            shares = jax.tree.map(jnp.add, sums, shares)
-        return shares, (normed_grad, ffn_out)
+        return jax.tree.map(jnp.add, sums, shares), (normed_grad, ffn_out)
 
     pieces = max(1, peers // DEVICES)
-    if pieces == 1:
-        shares, (normed_grad, ffn_out) = piece(None, (hidden_two, out_cotangent))
-    else:
-        zeros = (
-            jnp.zeros((width, 2 * ffn_pad), F32),
-            jnp.zeros((ffn_pad, width), F32),
-            jnp.zeros((2 * ffn_pad,), F32),
-            jnp.zeros((rows,), F32),
-        )
-        cut = (pieces, tok_rows // pieces, width)
-        shares, outs = lax.scan(piece, zeros, (hidden_two.reshape(cut), out_cotangent.reshape(cut)))
-        normed_grad, ffn_out = (part.reshape(tok_rows, width) for part in outs)
-    return (normed_grad, ffn_out) + shares
+    cut = tok_rows // pieces
+    zeros = (
+        jnp.zeros((width, 2 * ffn_pad), F32),
+        jnp.zeros((ffn_pad, width), F32),
+        jnp.zeros((2 * ffn_pad,), F32),
+    )
+    cotangent_pieces = cotangent_full.reshape(peers, pieces, cut, width).transpose(1, 0, 2, 3)
+    shares, outs = lax.scan(
+        piece,
+        zeros,
+        (hidden_two.reshape(pieces, cut, width), cotangent_pieces.reshape(pieces, -1, width)),
+    )
+    normed_grad, ffn_out = (part.reshape(tok_rows, width) for part in outs)
+    return (normed_grad, ffn_out) + shares + (down_bias_share,)
 
 
 def body(
@@ -387,8 +639,11 @@
     ffn_pad = round_up(ffn_own, LANES)
 
     vectors = jnp.stack([norm1_scale, norm2_scale, down_bias], axis=1)
-    first = gather_rows(
-        jnp.concatenate([query_weight, keyvalue_weight, pad_columns(vectors, LANES)], axis=1)
+    packed = jnp.concatenate(
+        [query_weight, keyvalue_weight, pad_columns(vectors, LANES)], axis=1
+    )
+    first, out_full, cotangent_full = gather_rows(
+        [packed, out_weight, out_cotangent], 5, "gather_weights"
     )
     proj_cols = query_cols + kv_cols
     proj_full = first[:, :proj_cols]
@@ -419,11 +674,10 @@
     reach = min((WINDOW + tok_rows - 2) // tok_rows, peers - 1)
     window_rows = (reach + 1) * tok_rows
     window_start = jnp.maximum(device - reach, 0) * tok_rows
-    kv_window = lax.dynamic_slice_in_dim(gather_rows(own_kv), window_start, window_rows, 0)
+    kv_window = lax.dynamic_slice_in_dim(gather_rows([own_kv], 6, "gather_kv")[0], window_start, window_rows, 0)
     place = (device * tok_rows - window_start).astype(jnp.int32).reshape(1)
     attention, logs = attend(place, queries, kv_window)
 
-    out_full = gather_rows(out_weight)
     residual_mid = resid_in + jnp.dot(attention, out_full, preferred_element_type=F32)
     square_two = jnp.mean(residual_mid * residual_mid, axis=1, keepdims=True)
     scale_two = lax.rsqrt(square_two + EPSILON)
@@ -441,7 +695,7 @@
     down_own = jnp.pad(down_weight, ((0, ffn_pad - ffn_own), (0, 0)))
 
     normed_grad_two, ffn_out, grad_both, grad_down, bias_share, down_bias_share = feed_forward(
-        hidden_two, out_cotangent, both_own, both_bias, down_own, rows
+        hidden_two, cotangent_full, both_own, both_bias, down_own, rows
     )
     layer_output = (residual_mid + (ffn_out + bias_down)).astype(BF16)
     rms_values = jnp.stack(

time: 1240 us -> 1090 us (0.88)
  waiting for transfers between devices: 540 us -> 0.01 us
  Pallas kernels: 439 us -> 919 us
  matrix products: 144 us -> 50.7 us
  between operations: 14.9 us -> 1.67 us
    all_gather x5 -> x0, waiting for transfers between devices: 539 us -> none  [gather_rows(): return lax.all_gather(values, AXIS, axis=0, tiled=True)]
    pallas_call x0 -> x3, Pallas kernels: none -> 480 us  [the longest x2 321 us: gather_all(): pl.pallas_call(functools.partial(gather_kernel, chunks), out_shape=tuple(...]
    dot_general x8 -> x4, matrix products: 102 us -> 37.3 us  [dot(): lax.dot_general(left, right, (contract, ((), ())), preferred_element_type...]
    dot_general x2 -> x0, matrix products: 28.2 us -> none  [the longest x1 18 us: piece(): jnp.dot(hidden_full, both_own, preferred_element_type=F32) + both_bias]
  transfers between devices with their start and end apart: 7 -> 2, of which waited for: 5 -> 0; matrix products, arithmetic and copies ran while one was open for 8% -> 8% of each run, Pallas kernels for 14% -> 46%
where the time goes in v2:
time: 1090 us
  Pallas kernels  919 us (84%)
  local copies, waits for them, and re-layouts  61.1 us (6%)
  matrix products  50.7 us (5%)
  other arithmetic  44.4 us (4%)
  starting transfers between devices  12.6 us (1%)
    pallas_call x5, Pallas kernels, sum_over_devices(): pl.pallas_call(functools.partial(sum_kernel, chunk), out_shape=jax.ShapeD...  412 us
    pallas_call x2, Pallas kernels, gather_all(): pl.pallas_call(functools.partial(gather_kernel, chunks), out_shape=tuple(...  321 us
    pallas_call x1, Pallas kernels, ffn(): pl.pallas_call(ffn_kernel, out_shape=(jax.ShapeDtypeStruct(full, BF16), j...  159 us
    dot_general x4, matrix products, dot(): lax.dot_general(left, right, (contract, ((), ())), preferred_element_type...  37.3 us
  transfers between devices with their start and end apart: 2, of which 0 were waited for; matrix products, arithmetic and copies ran while one was open for 8% of the time, Pallas kernels for 46%

profile of v2, /device:TPU:0, one launch (start us, length us, event | category | flops | bytes accessed | tf_op | source)
XLA Modules:
  0.0 1089.7 jit_solution(11802748330506803530)
XLA Ops:
  0.6 4.0 reshape.238
  5.4 4.0 reshape.239
  10.2 2.0 fusion.7
  12.2 7.6 all-to-all-start
  20.8 287.9 %gather_weights.1 = (bf16[4,2,2,2,80,3200]{5,4,3,2,1,0:T(8,128)(2,1)}, bf16[4,2,2,2,80,2560]{5,4,3,2,1,0:T(8,128)(2,1)}, bf16[4,2,2,2,128,2560]{5,4,3,2,1,0:T(8,128)(2,1)}) custom-call(bf16[80,3200]{1,0:T(8,128)(2,1)} %fusion.22.refs_0_, bf16[80,2560]{1,0:T(8,128)(2,1)} %refs_1_.1, bf16[128,2560]{1,0:T(8,128)(2,1)} %refs_2_.1), custom_call_target="tpu_custom_call" | custom-call | tf_op jit(solution)/shard_map/gather_weights/pallas_call | solution.py:405
  312.7 6.7 fusion.2
  325.3 32.9 %gather_kv.1 = bf16[4,2,2,2,128,512]{5,4,3,2,1,0:T(8,128)(2,1)} custom-call(bf16[128,512]{1,0:T(8,128)(2,1)} %pad_maximum_fusion.5.refs_0_), custom_call_target="tpu_custom_call" | custom-call | tf_op jit(solution)/shard_map/gather_kv/pallas_call | solution.py:405
  358.9 1.1 pad.30.down_ref
  360.1 2.7 convert_reduce_fusion
  362.8 1.8 constant_dynamic-slice_fusion.kv_ref
  364.6 10.8 attend.1
  375.5 6.7 multiply_reduce_fusion.2
  384.9 159.1 %feed_forward.1 = (bf16[4,2,2,2,128,2560]{5,4,3,2,1,0:T(8,128)(2,1)}, bf16[4,2,2,2,128,2560]{5,4,3,2,1,0:T(8,128)(2,1)}, f32[512,2560]{1,0:T(8,128)}, f32[256,2560]{1,0:T(8,128)}, f32[8,512]{1,0:T(8,128)}) custom-call(bf16[128,2560]{1,0:T(8,128)(2,1)} %multiply_convert_fusion.hidden_ref, bf16[4,2,2,2,128,2560]{5,4,3,2,1,0:T(8,128)(2,1)} %get-tuple-element.30.cotangent_ref, ...), custom_call_target="tpu_custom_call" | custom-call | tf_op jit(solution)/shard_map/feed_forward/pallas_call | solution.py:517
  544.0 105.6 %sum_hidden.3 = f32[128,2560]{1,0:T(8,128)} custom-call(bf16[4,2,2,2,128,2560]{5,4,3,2,1,0:T(8,128)(2,1)} %get-tuple-element.32.in_ref), custom_call_target="tpu_custom_call" | custom-call | tf_op jit(solution)/shard_map/sum_hidden/pallas_call | solution.py:280
  649.6 1.7 multiply_reduce_fusion
  651.3 105.2 %sum_hidden.2 = f32[128,2560]{1,0:T(8,128)} custom-call(bf16[4,2,2,2,128,2560]{5,4,3,2,1,0:T(8,128)(2,1)} %get-tuple-element.31.in_ref), custom_call_target="tpu_custom_call" | custom-call | tf_op jit(solution)/shard_map/sum_hidden/pallas_call | solution.py:280
  756.5 2.7 multiply_add_fusion
  759.2 9.2 convolution_convert_fusion.2.grad_ref
  768.5 16.7 %attend_back.1 = (f32[128,2560]{1,0:T(8,128)S(1)}, f32[2176,512]{1,0:T(8,128)}) custom-call(s32[1]{0:T(128)} %bitcast.place_ref, bf16[128,2560]{1,0:T(8,128)(2,1)S(1)} %copy.97.query_ref, bf16[2176,512]{1,0:T(8,128)(2,1)S(1)} %copy-done.1, f32[5,256,128]{2,1,0:T(8,128)S(1)} %get-tuple-element.33.log_ref, bf16[128,2560]{1,0:T(8,128)(2,1)S(1)} %convolution_convert_fusion.2.grad_ref), custom_call_target="tpu_custom_call" | custom-call | flops 7130316800 | bytes 8912896 | tf_op jit(solution)/shard_map/attend_back/pallas_call | solution.py:148
  785.1 2.3 broadcast_in_dim.5
  787.4 3.9 convert_dynamic-update-slice_fusion
  791.3 33.6 %sum_grad_kv.1 = f32[128,512]{1,0:T(8,128)} custom-call(bf16[4,2,2,2,128,512]{5,4,3,2,1,0:T(8,128)(2,1)} %bitcast.16.in_ref), custom_call_target="tpu_custom_call" | custom-call | tf_op jit(solution)/shard_map/sum_grad_kv/pallas_call | solution.py:280
  824.9 1.6 slice.184
  826.5 1.9 fusion.39
  828.5 1.5 copy.101
  830.0 1.9 slice.183
  831.9 1.8 subtract_convert_fusion
  834.7 4.3 convert_bitcast_fusion.1
  838.9 4.5 copy.107
  843.4 4.9 all-to-all-start.1
  849.6 11.9 %fusion.18 = (bf16[2560]{0:T(1024)(128)(2,1)S(1)}, f32[128]{0:T(128)S(1)}, f32[128,2560]{1,0:T(8,128)}) fusion(bf16[128,2560]{1,0:T(8,128)(2,1)S(1)} %copy-done.6, f32[128]{0:T(128)S(1)} %copy-done.26, f32[2560]{0:T(1024)S(1)} %copy-done.18, bf16[2560,3200]{1,0:T(8,128)(2,1)} %bitcast.53, bf16[128,384]{0,1:T(8,128)(2,1)} %copy.105, ...), kind=kOutput, calls=%fused_computation.31 | convolution fusion | flops 2018702720 | bytes 18497536 | tf_op jit(solution)/shard_map/dot_general | solution.py:45
  862.7 2.1 pad.33.clone
  864.8 9.5 convolution_convert_fusion.1
  874.3 13.6 %pad_maximum_fusion.in_ref = bf16[4,2,2,2,80,3200]{5,4,3,2,1,0:T(8,128)(2,1)} fusion(bf16[4,2,2,2,80,128]{5,4,3,2,1,0:T(8,128)(2,1)} %bitcast.50, bf16[4,2,2,2,80,3072]{5,4,3,2,1,0:T(8,128)(2,1)} %bitcast.36), kind=kLoop, calls=%fused_computation.2 | loop fusion | flops 32768000 | bytes 32768000 | tf_op jit(solution)/shard_map/concatenate | solution.py:747
  887.8 93.0 %sum_grad_proj.1 = f32[80,3200]{1,0:T(8,128)} custom-call(bf16[4,2,2,2,80,3200]{5,4,3,2,1,0:T(8,128)(2,1)} %pad_maximum_fusion.in_ref), custom_call_target="tpu_custom_call" | custom-call | tf_op jit(solution)/shard_map/sum_grad_proj/pallas_call | solution.py:280
  980.8 2.1 slice.127
  982.9 1.6 slice.128
  984.5 6.7 convolution_convert_fusion
  991.2 74.5 %sum_grad_out.1 = f32[80,2560]{1,0:T(8,128)} custom-call(bf16[4,2,2,2,80,2560]{5,4,3,2,1,0:T(8,128)(2,1)} %bitcast.39), custom_call_target="tpu_custom_call" | custom-call | tf_op jit(solution)/shard_map/sum_grad_out/pallas_call | solution.py:280
  1065.7 1.6 slice.136
  1067.3 1.6 slice_reduce_fusion
  1068.9 1.3 fusion.51
  1070.2 1.3 fusion.17
  1071.5 2.5 convert_bitcast_fusion
  1074.4 3.0 copy.108
  1077.4 3.9 reshape.244
  1081.4 3.0 copy.109
  1084.4 4.0 reshape.245
  (117 shorter events, 20.4 us)
Async XLA Ops:
  12.2 7.7 copy-start.31
  12.2 7.7 copy-start.32
  12.2 7.7 copy-start.33
  12.2 7.8 copy-start.12
  12.2 7.8 copy-start.23
  12.2 372.1 %all-to-all-start = ((bf16[32,80,512]{2,1,0:T(8,128)(2,1)}), bf16[32,80,512]{2,1,0:T(8,128)(2,1)}, u32[]{:S(2)}, u32[]{:S(2)}) async-start(bf16[32,80,512]{2,1,0:T(8,128)(2,1)} %fusion.7), calls=%async_computation | async-start | bytes 5242880 | tf_op jit(solution)/shard_map/all_to_all | solution.py:557
  310.1 1.1 copy-start.5
  312.1 0.6 copy-start.17
  312.1 0.6 copy-start.25
  320.2 1.1 copy-start.27
  320.2 1.1 copy-start.29
  323.7 0.9 copy-start.15
  323.7 0.9 copy-start.20
  323.7 0.9 copy-start.21
  325.3 32.9 %copy-start.16 = (f32[128,64]{1,0:T(8,128)S(1)}, f32[128,64]{1,0:T(8,128)}, u32[]{:S(2)}) copy-start(f32[128,64]{1,0:T(8,128)} %get-tuple-element.62) | copy-start | bytes 98308
  325.3 33.6 %copy-start.11 = (bf16[240,2560]{1,0:T(8,128)(2,1)S(1)}, bf16[240,2560]{1,0:T(8,128)(2,1)}, u32[]{:S(2)}) copy-start(bf16[240,2560]{1,0:T(8,128)(2,1)} %param.23) | copy-start | bytes 3686404
  364.6 10.9 copy-start
  375.4 7.4 copy-start.34
  375.5 7.4 copy-start.35
  382.2 1.1 copy-start.2
  544.0 105.6 %copy-start.3 = (f32[128,2560]{1,0:T(8,128)S(1)}, f32[128,2560]{1,0:T(8,128)}, u32[]{:S(2)}) copy-start(f32[128,2560]{1,0:T(8,128)} %copy-done.2) | copy-start | bytes 3932164
  651.3 105.2 %copy-start.4 = (f32[128,2560]{1,0:T(8,128)S(1)}, f32[128,2560]{1,0:T(8,128)}, u32[]{:S(2)}) copy-start(f32[128,2560]{1,0:T(8,128)} %sum_hidden.3) | copy-start | bytes 3932164
  651.3 105.2 %copy-start.8 = (bf16[128,2560]{1,0:T(8,128)(2,1)S(1)}, bf16[128,2560]{1,0:T(8,128)(2,1)}, u32[]{:S(2)}) copy-start(bf16[128,2560]{1,0:T(8,128)(2,1)} %refs_2_.1) | copy-start | bytes 1966084
  651.3 105.2 %copy-start.24 = (f32[2560]{0:T(1024)S(1)}, f32[2560]{0:T(1024)}, u32[]{:S(2)}) copy-start(f32[2560]{0:T(1024)} %get-tuple-element.43) | copy-start | bytes 30724
  759.2 9.2 copy-start.1
  791.3 35.2 %copy-start.28 = (f32[128]{0:T(128)S(1)}, f32[128]{0:T(128)}, u32[]{:S(2)}) copy-start(f32[128]{0:T(128)} %copy-done.27) | copy-start | bytes 1540
  791.3 35.2 %copy-start.30 = (f32[64]{0:T(128)S(1)}, f32[64]{0:T(128)}, u32[]{:S(2)}) copy-start(f32[64]{0:T(128)} %copy-done.29) | copy-start | bytes 772
  828.5 3.4 copy-start.19
  830.0 3.8 copy-start.14
  830.0 4.5 copy-start.22
  843.4 228.1 %all-to-all-start.1 = ((bf16[32,80,512]{2,1,0:T(8,128)(2,1)}), bf16[32,80,512]{2,1,0:T(8,128)(2,1)}, u32[]{:S(2)}, u32[]{:S(2)}) async-start(bf16[32,80,512]{2,1,0:T(8,128)(2,1)} %bitcast.41), calls=%async_computation.1 | async-start | bytes 5242880 | tf_op jit(solution)/shard_map/all_to_all | solution.py:557
  848.3 1.3 copy-start.6
  848.3 1.3 copy-start.18
  848.3 1.2 copy-start.26
  861.5 3.3 copy-start.13
  991.2 74.5 %copy-start.9 = (f32[256,2560]{1,0:T(8,128)S(1)}, f32[256,2560]{1,0:T(8,128)}, u32[]{:S(2)}) copy-start(f32[256,2560]{1,0:T(8,128)} %get-tuple-element.38) | copy-start | bytes 7864324
  1065.7 4.5 copy-start.10
  1084.4 4.0 copy-start.7

commit v3 on v2

--- a/solution.py
+++ b/solution.py
@@ -288,6 +288,150 @@
         compiler_params=pltpu.CompilerParams(collective_id=collective_id, has_side_effects=True, vmem_limit_bytes=56*1024*1024),
         name=name,
     )(partial.reshape(4, 2, 2, 2, rows, columns))
+
+
+CORNERS = ((1, 1), (0, 1), (1, 0), (0, 0))
+
+def add_tiles(count, rows, target, parts):
+    steps = rows // TILE
+    @pl.loop(0, count * steps)
+    def _(i):
+        index, here = i // steps, pl.ds(pl.multiple_of((i % steps) * TILE, TILE), TILE)
+        total = None
+        for ref, first in parts:
+            at = here if first == 0 else pl.ds(pl.multiple_of((i % steps) * TILE + first, TILE), TILE)
+            part = ref[index, at].astype(F32)
+            total = part if total is None else total + part
+        ref, first = target
+        at = here if first == 0 else pl.ds(pl.multiple_of((i % steps) * TILE + first, TILE), TILE)
+        ref[index, at] = total.astype(BF16)
+
+class SumBuffers:
+    def __init__(self, refs):
+        self.acc, self.core, self.diag_x, self.diag_y, self.x, self.y, self.z, self.sems = refs
+    @staticmethod
+    def shapes(rows, columns, units):
+        upper = (rows // 2 + TILE - 1) // TILE * TILE
+        buf = lambda *shape: pltpu.VMEM(shape + (columns,), BF16)
+        return [buf(4, 4, rows), buf(4, 4, rows), buf(4, upper), buf(4, rows - upper), buf(4, rows), buf(4, rows), buf(3, rows),
+                pltpu.SemaphoreType.DMA((units, 2, Sum.COPIES))]
+    COUNT = 8
+
+class Sum:
+    COPIES = 14
+    def __init__(self, place, bufs, unit, cols, own, other, out):
+        self.p, self.b, self.unit, self.own, self.other, self.out = place, bufs, unit, own, other, out
+        self.rows = bufs.acc.shape[2]
+        self.upper = bufs.diag_x.shape[1]
+        self.lower = self.rows - self.upper
+        self.acc = bufs.acc.at[:, :, :, cols]
+        self.core = bufs.core.at[:, :, :, cols]
+        self.diag_x, self.diag_y = bufs.diag_x.at[:, :, cols], bufs.diag_y.at[:, :, cols]
+        self.x, self.y, self.z = bufs.x.at[:, :, cols], bufs.y.at[:, :, cols], bufs.z.at[:, :, cols]
+        self.copies = {}
+    def push(self, slot, src, dst, device):
+        sems = self.b.sems
+        self.copies[slot] = send(src, dst, (sems.at[self.unit, 0, slot], sems.at[self.unit, 1, slot]), device)
+    def begin(self):
+        for i in range(4):
+            self.push(i, self.other(i), self.core.at[i], self.p.sibling)
+    def stage0(self):
+        top, bottom = pl.ds(0, self.upper), pl.ds(self.upper, self.lower)
+        for i in range(4):
+            self.copies[i].wait_recv()
+            add_tiles(4, self.rows, (self.acc.at[i], 0), [(self.own(i), 0), (self.core.at[i], 0)])
+            if i == 0:
+                self.push(4, self.acc.at[0, :, top], self.diag_x, self.p.next_x)
+                self.push(5, self.acc.at[0, :, bottom], self.diag_y, self.p.next_y)
+            if i == 1:
+                self.push(6, self.acc.at[1, :, top], self.x.at[:, top], self.p.next_x)
+            if i == 2:
+                self.push(7, self.acc.at[2, :, bottom], self.y.at[:, bottom], self.p.next_y)
+    def stage1(self):
+        top, bottom = pl.ds(0, self.upper), pl.ds(self.upper, self.lower)
+        self.copies[4].wait_recv()
+        add_tiles(4, self.upper, (self.acc.at[2], 0), [(self.acc.at[2], 0), (self.diag_x, 0)])
+        self.push(8, self.acc.at[2, :, top], self.y.at[:, top], self.p.next_y)
+        self.copies[5].wait_recv()
+        add_tiles(4, self.lower, (self.acc.at[1], self.upper), [(self.acc.at[1], self.upper), (self.diag_y, 0)])
+        self.push(9, self.acc.at[1, :, bottom], self.x.at[:, bottom], self.p.next_x)
+    def stage2(self):
+        for slot in (6, 7, 8, 9):
+            self.copies[slot].wait_recv()
+        add_tiles(4, self.rows, (self.acc.at[3], 0), [(self.acc.at[3], 0), (self.x, 0), (self.y, 0)])
+        for o in (1, 2, 3):
+            self.push(9 + o, self.acc.at[3, self.p.plane[o]], self.z.at[o - 1], self.p.line[o])
+    def stage3(self):
+        for o in (1, 2, 3):
+            self.copies[9 + o].wait_recv()
+        @pl.loop(0, self.rows // TILE)
+        def _(i):
+            here = pl.ds(pl.multiple_of(i * TILE, TILE), TILE)
+            total = self.acc[3, self.p.z, here].astype(F32)
+            for o in range(3):
+                total += self.z[o, here].astype(F32)
+            self.out[here] = total
+    def core_sent(self):
+        for i in range(4): self.copies[i].wait_send()
+    def finish(self):
+        for slot in range(4, 13): self.copies[slot].wait_send()
+
+def product_sums_kernel(chunk, left_a, right_a, left_b, right_b, extra, out_a, out_b, part, *scratch):
+    place = Place()
+    bufs = SumBuffers(scratch)
+    rows = out_a.shape[0]
+    wide = 8 * rows
+    units = []
+    def add_unit(left, right, out, first, span, more):
+        k = len(units)
+        slot = k % 2
+        def own(i):
+            y, x = place.side(*CORNERS[i])
+            return part.at[slot, :, y, x, place.core]
+        def other(i):
+            y, x = place.side(*CORNERS[i])
+            return part.at[slot, :, y, x, 1 - place.core]
+        cols = pl.ds(k * chunk, chunk)
+        unit = Sum(place, bufs, k, cols, own, other, out.at[:, pl.ds(first, chunk)])
+        def make():
+            if k >= 2: units[k - 2][0].core_sent()
+            @pl.loop(0, 4)
+            def _(z):
+                here = pl.ds(pl.multiple_of(z * wide, wide), wide)
+                product = lax.dot_general(left[:, here], right[:, pl.ds(first, span)], (((0,), (0,)), ((), ())), preferred_element_type=F32)
+                part[slot, z, :, :, :, :, pl.ds(0, span)] = product.astype(BF16).reshape(2, 2, 2, rows, span)
+                if more is not None:
+                    part[slot, z, :, :, :, :, pl.ds(span, chunk - span)] = more[here].reshape(2, 2, 2, rows, chunk - span)
+            unit.begin()
+        units.append((unit, make))
+    for first in range(0, out_a.shape[1], chunk):
+        add_unit(left_a, right_a, out_a, first, chunk, None)
+    for first in range(0, out_b.shape[1], chunk):
+        span = min(chunk, right_b.shape[1] - first)
+        add_unit(left_b, right_b, out_b, first, span, None if span == chunk else extra)
+    place.meet()
+    count = len(units)
+    stages = [lambda k: units[k][1](), lambda k: units[k][0].stage0(), lambda k: units[k][0].stage1(), lambda k: units[k][0].stage2(), lambda k: units[k][0].stage3()]
+    for step in range(count + 4):
+        for s in (1, 2, 3, 4, 0):
+            if 0 <= step - s < count: stages[s](step - s)
+    for unit, _ in units[-2:]: unit.core_sent()
+    for unit, _ in units: unit.finish()
+
+def product_sums(left_a, right_a, left_b, right_b, extra, chunk, collective_id, name):
+    rows = left_a.shape[1] // 32
+    columns_a, columns_b = right_a.shape[1], right_b.shape[1] + extra.shape[1]
+    total = columns_a + columns_b
+    vmem = pl.BlockSpec(memory_space=pltpu.VMEM)
+    return pl.pallas_call(
+        functools.partial(product_sums_kernel, chunk),
+        out_shape=(jax.ShapeDtypeStruct((rows, columns_a), F32), jax.ShapeDtypeStruct((rows, columns_b), F32)),
+        in_specs=[vmem] * 5,
+        out_specs=(vmem, vmem),
+        scratch_shapes=[pltpu.VMEM((2, 4, 2, 2, 2, rows, chunk), BF16)] + SumBuffers.shapes(rows, total, total // chunk),
+        compiler_params=pltpu.CompilerParams(collective_id=collective_id, has_side_effects=True, vmem_limit_bytes=62*1024*1024),
+        name=name,
+    )(left_a, right_a, left_b, right_b, extra)
 
 
 PLANES=4
@@ -424,64 +568,164 @@
     slope = half + 0.5 * v * (1.0 - t * t) * (GELU_SCALE * (1.0 + 3.0 * GELU_CUBE * square))
     return v * half, slope
 
+class PlaneSum:
+    SLOTS = 10
+    def __init__(self, place, order, kind, k, acc, outgoing, out, land, load, sems, line_sems, load_sems):
+        self.p, self.k, self.order = place, k, order
+        self.acc, self.outgoing = acc.at[kind, k], outgoing.at[kind]
+        self.out = out
+        core, diag_x, diag_y, side_x, side_y, line = land
+        self.core, self.side_x, self.side_y = core.at[kind, k], side_x.at[kind, k], side_y.at[kind, k]
+        self.diag_x, self.diag_y, self.land = diag_x.at[kind, k], diag_y.at[kind, k], line.at[kind]
+        self.load, self.load_sems = load, load_sems
+        self.sems, self.line_sems = sems.at[kind, k], line_sems.at[kind]
+        self.rows = self.acc.shape[1]
+        self.upper = self.diag_x.shape[0]
+        self.top, self.bottom = pl.ds(0, self.upper), pl.ds(self.upper, self.rows - self.upper)
+    def mine(self, i): return self.acc.at[i]
+    def copy(self, src, dst, slot, device):
+        return pltpu.make_async_remote_copy(src_ref=src, dst_ref=dst, send_sem=self.sems.at[0, slot], recv_sem=self.sems.at[1, slot], device_id=(device,), device_id_type=MESH)
+    def across(self, i):
+        return self.copy(self.outgoing.at[i % 2], self.core.at[i], i, self.p.sibling)
+    def make(self, slot):
+        p, mine = self.p, self.mine
+        src, dst, device = {
+            4: (mine(0).at[self.top], self.diag_x, p.next_x),
+            5: (mine(0).at[self.bottom], self.diag_y, p.next_y),
+            6: (mine(1).at[self.top], self.side_x.at[self.top], p.next_x),
+            7: (mine(2).at[self.bottom], self.side_y.at[self.bottom], p.next_y),
+            8: (mine(2).at[self.top], self.side_y.at[self.top], p.next_y),
+            9: (mine(1).at[self.bottom], self.side_x.at[self.bottom], p.next_x),
+        }[slot]
+        return self.copy(src, dst, slot, device)
+    def line_copy(self):
+        p, plane = self.p, self.order[self.k]
+        return pltpu.make_async_remote_copy(src_ref=self.mine(3), dst_ref=self.land.at[p.z], send_sem=self.line_sems.at[0, self.k], recv_sem=self.line_sems.at[1, p.z], device_id=(p.index(plane, p.y, p.x, p.core),), device_id_type=MESH)
+    def fetch(self, src, slot):
+        rows = src.shape[0]
+        copy = pltpu.make_async_copy(src, self.load.at[slot, pl.ds(0, rows)], self.load_sems.at[slot])
+        copy.start()
+        return copy
+    def add(self, target, slots, rows):
+        @pl.loop(0, rows // TILE)
+        def _(i):
+            here = pl.ds(pl.multiple_of(i * TILE, TILE), TILE)
+            total = target[here].astype(F32)
+            for slot in slots: total += self.load[slot, here].astype(F32)
+            target[here] = total.astype(target.dtype)
+    def stage0(self):
+        self.across(0).wait_recv()
+        fetched = self.fetch(self.core.at[0], 0)
+        for i in range(4):
+            current = fetched
+            if i < 3:
+                self.across(i + 1).wait_recv()
+                fetched = self.fetch(self.core.at[i + 1], (i + 1) % 2)
+            current.wait()
+            self.add(self.mine(i), [i % 2], self.rows)
+            for slot in ((4, 5), (6,), (7,), ())[i]:
+                self.make(slot).start()
+    def stage1(self):
+        self.make(4).wait_recv()
+        self.fetch(self.diag_x, 0).wait()
+        self.add(self.mine(2).at[self.top], [0], self.upper)
+        self.make(8).start()
+        self.make(5).wait_recv()
+        self.fetch(self.diag_y, 1).wait()
+        self.add(self.mine(1).at[self.bottom], [1], self.rows - self.upper)
+        self.make(9).start()
+    def stage2(self):
+        for slot in (6, 9): self.make(slot).wait_recv()
+        first = self.fetch(self.side_x, 0)
+        for slot in (7, 8): self.make(slot).wait_recv()
+        second = self.fetch(self.side_y, 1)
+        first.wait(); second.wait()
+        if self.k > 0:
+            self.add(self.mine(3), [0, 1], self.rows)
+            self.line_copy().start()
+        else:
+            mine, out = self.mine(3), self.out
+            @pl.loop(0, self.rows // TILE)
+            def _(i):
+                here = pl.ds(pl.multiple_of(i * TILE, TILE), TILE)
+                out[here] = mine[here].astype(F32) + self.load[0, here].astype(F32) + self.load[1, here].astype(F32)
+    def sent(self):
+        for slot in range(4, 10): self.make(slot).wait_send()
+        if self.k > 0: self.line_copy().wait_send()
+    def last(self):
+        p, plane = self.p, self.order[self.k]
+        land = self.land.at[plane]
+        pltpu.make_async_remote_copy(src_ref=land, dst_ref=land, send_sem=self.line_sems.at[0, self.k], recv_sem=self.line_sems.at[1, plane], device_id=(p.sibling,), device_id_type=MESH).wait_recv()
+        self.fetch(land, self.k % 2).wait()
+        self.add(self.out, [self.k % 2], self.rows)
+
 def ffn_kernel(hidden_ref, cotangent_ref, both_ref, down_ref, bias_ref,
-               hidden_out, ffn_out, grad_both_ref, grad_down_ref, bias_grad_ref,
-               held, cot, both_keep, ffn_keep, stage, gather_sems, cot_sems, out_sems):
+               hidden_sum, ffn_sum, grad_both_ref, grad_down_ref, bias_grad_ref,
+               held, land_core, land_dx, land_dy, land_x, land_y, land_z,
+               tokens, cot, both_keep, ffn_keep, acc, outgoing, load, gather_sems, cot_sems, sum_sems, line_sems, load_sems):
     place = Place()
     width = hidden_ref.shape[1]
     pad = down_ref.shape[0]
     rows = 2 * hidden_ref.shape[0]
     order = plane_order(place.z)
-    fetch = [pltpu.make_async_copy(cotangent_ref.at[order[k]], cot.at[k % 2], cot_sems.at[k]) for k in range(PLANES)]
-    fetch[0].start()
-    fetch[1].start()
+    def fetch_cot(k): return pltpu.make_async_copy(cotangent_ref.at[order[k]], cot, cot_sems.at[0, k])
+    def fetch_tokens(k): return pltpu.make_async_copy(held.at[order[k]], tokens, cot_sems.at[1, k])
+    fetch_cot(0).start()
     place.meet()
     gather = Gather(place, hidden_ref, held, pl.ds(0, width), gather_sems)
     gather.start()
     grad_both_ref[...] = jnp.zeros_like(grad_both_ref)
     grad_down_ref[...] = jnp.zeros_like(grad_down_ref)
     bias_grad_ref[...] = jnp.zeros_like(bias_grad_ref)
-
-    def emit(kind, slot, plane, y, x):
-        target = (hidden_out, ffn_out)[kind]
-        return pltpu.make_async_copy(stage.at[kind, slot], target.at[plane, y, x], out_sems.at[kind, slot])
+    land = (land_core, land_dx, land_dy, land_x, land_y, land_z)
+    sums = [[PlaneSum(place, order, kind, k, acc, outgoing, (hidden_sum, ffn_sum)[kind], land, load, sum_sems, line_sems, load_sems) for k in range(PLANES)] for kind in range(2)]
 
     def compute(k):
-        plane = order[k]
-        fetch[k].wait()
+        gather.ready(k)
+        fetch_tokens(k).start()
+        fetch_tokens(k).wait()
+        fetch_cot(k).wait()
+        half = rows // 2
         @pl.loop(0, 4)
         def _(i):
-            y, x, slot = i // 2, i % 2, i % 2
-            hidden = held[plane, y, x].reshape(rows, width)
-            cotangent = cot[k % 2, y, x].reshape(rows, width)
+            dy, dx = 1 - i % 2, 1 - i // 2
+            y, x = place.y + dy * (1 - 2 * place.y), place.x + dx * (1 - 2 * place.x)
+            hidden = tokens[y, x].reshape(rows, width)
+            cotangent = cot[y, x].reshape(rows, width)
             both_pre = dot(hidden, both_ref[...], ((1,), (0,))) + bias_ref[0:1]
             hidden_grad = dot(cotangent, down_ref[...], ((1,), (1,)))
             activated, slope = gelu_and_slope(both_pre[:, :pad])
             up_pre = both_pre[:, pad:]
             hidden_ffn = (activated * up_pre).astype(BF16)
             both_grad = jnp.concatenate([(hidden_grad * up_pre * slope).astype(BF16), (hidden_grad * activated).astype(BF16)], axis=1)
-            here = pl.ds(pl.multiple_of(i * rows, rows), rows)
+            here = pl.ds(pl.multiple_of((y * 2 + x) * rows, rows), rows)
             both_keep[here] = both_grad
             ffn_keep[here] = hidden_ffn
             bias_grad_ref[...] += jnp.sum(both_grad.astype(F32), axis=0, keepdims=True)
             def drain():
-                for kind in range(2): emit(kind, slot, plane, y, x).wait()
-            if k > 0: drain()
-            else: pl.when(i >= 2)(drain)
-            half = stage.shape[3]
-            stage[0, slot] = dot(both_grad, both_ref[...], ((1,), (1,))).astype(BF16).reshape(2, half, width)
-            emit(0, slot, plane, y, x).start()
-            stage[1, slot] = dot(hidden_ffn, down_ref[...], ((1,), (0,))).astype(BF16).reshape(2, half, width)
-            emit(1, slot, plane, y, x).start()
+                for kind in range(2): sums[kind][k].across(i - 2).wait_send()
+            def drain_before():
+                for kind in range(2): sums[kind][k - 1].across(i + 2).wait_send()
+            pl.when(i >= 2)(drain)
+            if k > 0: pl.when(i < 2)(drain_before)
+            for kind, part in ((0, lambda: dot(both_grad, both_ref[...], ((1,), (1,)))), (1, lambda: dot(hidden_ffn, down_ref[...], ((1,), (0,))))):
+                result = part().astype(BF16)
+                low, high = result[:half], result[half:]
+                acc[kind, k, i] = jnp.where(place.core == 0, low, high)
+                outgoing[kind, i % 2] = jnp.where(place.core == 0, high, low)
+                sums[kind][k].across(i).start()
         step = 512
         @pl.loop(0, width // step)
         def _(j):
             cols = pl.ds(pl.multiple_of(j * step, step), step)
-            hidden = held[plane, :, :, :, :, cols].reshape(4 * rows, step)
+            hidden = tokens[:, :, :, :, cols].reshape(4 * rows, step)
             grad_both_ref[:, cols] += dot(both_keep[...], hidden, ((0,), (0,)))
-            cotangent = cot[k % 2, :, :, :, :, cols].reshape(4 * rows, step)
+            cotangent = cot[:, :, :, :, cols].reshape(4 * rows, step)
             grad_down_ref[:, cols] += dot(ffn_keep[...], cotangent, ((0,), (0,)))
-        if k + 2 < PLANES: fetch[k + 2].start()
+        if k + 1 < PLANES: fetch_cot(k + 1).start()
+
+    def both(name, k):
+        for kind in range(2): getattr(sums[kind][k], name)()
 
     gather.line(0)
     gather.line(1)
@@ -489,54 +733,72 @@
     gather.line(2)
     gather.side(1)
     gather.diag(0)
-    gather.ready(0)
     compute(0)
     gather.line(3)
     gather.side(2)
     gather.diag(1)
     gather.side(3)
-    gather.ready(1)
     compute(1)
     gather.diag(2)
     gather.diag(3)
-    gather.ready(2)
+    both("stage0", 1)
     compute(2)
-    gather.ready(3)
+    both("stage1", 1)
+    both("stage0", 2)
     compute(3)
-    for slot in range(2):
-        for kind in range(2): emit(kind, slot, 0, 0, 0).wait()
+    both("stage2", 1)
+    both("stage1", 2)
+    both("stage0", 3)
+    both("stage2", 2)
+    both("stage1", 3)
+    both("stage0", 0)
+    both("stage2", 3)
+    both("stage1", 0)
+    both("stage2", 0)
+    for kind in range(2):
+        for i in (2, 3): sums[kind][3].across(i).wait_send()
+    for kind in range(2):
+        for k in (1, 2, 3): sums[kind][k].last()
+    for k in range(PLANES): both("sent", k)
     gather.finish()
 
 def ffn(hidden_two, cotangent_full, both_own, both_bias, down_own, collective_id):
     tok_rows, width = hidden_two.shape
     pad = down_own.shape[0]
     full = (4, 2, 2, 2, tok_rows, width)
+    upper = (tok_rows // 2 + TILE - 1) // TILE * TILE
     hbm = pl.BlockSpec(memory_space=pl.ANY)
     vmem = pl.BlockSpec(memory_space=pltpu.VMEM)
     dma = pltpu.SemaphoreType.DMA
-    hidden_part, ffn_part, grad_both, grad_down, bias_grad = pl.pallas_call(
+    low = lambda *shape: jax.ShapeDtypeStruct(shape + (width,), BF16)
+    outs = pl.pallas_call(
         ffn_kernel,
         out_shape=(
-            jax.ShapeDtypeStruct(full, BF16),
-            jax.ShapeDtypeStruct(full, BF16),
+            jax.ShapeDtypeStruct((tok_rows, width), F32),
+            jax.ShapeDtypeStruct((tok_rows, width), F32),
             jax.ShapeDtypeStruct((2 * pad, width), F32),
             jax.ShapeDtypeStruct((pad, width), F32),
             jax.ShapeDtypeStruct((8, 2 * pad), F32),
+            low(4, 2, 2, 2, tok_rows),
+            low(2, 4, 4, tok_rows), low(2, 4, upper), low(2, 4, tok_rows - upper),
+            low(2, 4, tok_rows), low(2, 4, tok_rows), low(2, 4, tok_rows),
         ),
         in_specs=[hbm, hbm, vmem, vmem, vmem],
-        out_specs=(hbm, hbm, vmem, vmem, vmem),
+        out_specs=(vmem,) * 5 + (hbm,) * 7,
         scratch_shapes=[
-            pltpu.VMEM(full, BF16),
-            pltpu.VMEM((2,) + full[1:], BF16),
+            pltpu.VMEM(full[1:], BF16),
+            pltpu.VMEM(full[1:], BF16),
             pltpu.VMEM((8 * tok_rows, 2 * pad), BF16),
             pltpu.VMEM((8 * tok_rows, pad), BF16),
-            pltpu.VMEM((2, 2, 2, tok_rows, width), BF16),
-            dma((2, Gather.COPIES, PLANES)), dma((PLANES,)), dma((2, 2)),
+            pltpu.VMEM((2, 4, 4, tok_rows, width), BF16),
+            pltpu.VMEM((2, 2, tok_rows, width), BF16),
+            pltpu.VMEM((2, tok_rows, width), BF16),
+            dma((2, Gather.COPIES, PLANES)), dma((2, PLANES)), dma((2, PLANES, 2, PlaneSum.SLOTS)), dma((2, 2, PLANES)), dma((2,)),
         ],
-        compiler_params=pltpu.CompilerParams(collective_id=collective_id, has_side_effects=True, vmem_limit_bytes=62*1024*1024),
+        compiler_params=pltpu.CompilerParams(collective_id=collective_id, has_side_effects=True, vmem_limit_bytes=63*1024*1024),
         name="feed_forward",
     )(hidden_two, cotangent_full.reshape(full), both_own, down_own, jnp.broadcast_to(both_bias, (8, 2 * pad)))
-    return (hidden_part.reshape(32 * tok_rows, width), ffn_part.reshape(32 * tok_rows, width), grad_both, grad_down, bias_grad[0])
+    return outs[0], outs[1], outs[2], outs[3], outs[4][0]
 
 
 def gather_rows(arrays, collective_id, name):
@@ -551,6 +813,17 @@
     return lax.psum_scatter(
         partial.astype(BF16), AXIS, scatter_dimension=0, tiled=True
     ).astype(F32)
+
+
+def sum_products(left_a, right_a, left_b, right_b, extra):
+    if lax.axis_size(AXIS) == DEVICES:
+        return product_sums(left_a, right_a, left_b, right_b, extra, 640, 2, "sum_products")
+    product_a = dot(left_a, right_a, ((0,), (0,)))
+    product_b = dot(left_b, right_b, ((0,), (0,))).astype(BF16)
+    return (
+        sum_rows(product_a, None, None, None),
+        sum_rows(jnp.concatenate([product_b, extra], axis=1), None, None, None),
+    )
 
 
 def swap(pieces):
@@ -565,11 +838,9 @@
     own_cotangent = lax.dynamic_slice_in_dim(cotangent_full, device * rows, rows, 1)
     down_bias_share = jnp.sum(own_cotangent.astype(F32), axis=0)
     if peers == DEVICES:
-        hidden_part, ffn_part, grad_both, grad_down, bias_share = ffn(
+        normed_grad, ffn_out, grad_both, grad_down, bias_share = ffn(
             hidden_two, cotangent_full, both_own, both_bias, down_own, 7
         )
-        normed_grad = sum_rows(hidden_part, 512, 1, "sum_hidden")
-        ffn_out = sum_rows(ffn_part, 512, 1, "sum_hidden")
         return normed_grad, ffn_out, grad_both.T, grad_down, bias_share, down_bias_share
 
     def piece(sums, here):
@@ -714,7 +985,6 @@
     )
     mid_grad_low = mid_grad.astype(BF16)
     attention_grad = dot(mid_grad_low, out_full, ((1,), (1,))).astype(BF16)
-    grad_out = sum_rows(dot(attention, mid_grad_low, ((0,), (0,))), 640, 2, "sum_grad_out")
 
     query_grad, kv_part = attend_back(place, queries, kv_window, logs, attention_grad)
     kv_partial = lax.dynamic_update_slice_in_dim(
@@ -744,8 +1014,9 @@
     ).astype(BF16)
 
     parts = pad_columns(jnp.stack([norm1_part, norm2_part], axis=1), LANES)
-    tail = jnp.concatenate([dot(hidden_one, proj_grad, ((0,), (0,))), parts], axis=1)
-    tail = sum_rows(tail, 640, 4, "sum_grad_proj")
+    grad_out, tail = sum_products(
+        attention, mid_grad_low, hidden_one, proj_grad, parts.astype(BF16)
+    )
     grad_proj = tail[:, :proj_cols]
     norm1_share = tail[:, proj_cols]
     norm2_share = tail[:, proj_cols + 1]

time: 1090 us -> 1000 us (0.917)
  Pallas kernels: 919 us -> 868 us
  other arithmetic: 44.4 us -> 19.8 us
  matrix products: 50.7 us -> 35.8 us
    pallas_call x5 -> x1, Pallas kernels: 412 us -> 49.4 us  [sum_over_devices(): pl.pallas_call(functools.partial(sum_kernel, chunk), out_shape=jax.ShapeD...]
    pallas_call x1 -> x2, Pallas kernels: 159 us -> 471 us  [the longest x1 315 us: ffn(): pl.pallas_call(ffn_kernel, out_shape=(jax.ShapeDtypeStruct((tok_rows, wid...]
    dot_general x4 -> x2, matrix products: 37.3 us -> 21.6 us  [dot(): lax.dot_general(left, right, (contract, ((), ())), preferred_element_type...]
    concatenate x1 -> x0, other arithmetic: 13.6 us -> none  [body(): jnp.concatenate([dot(hidden_one, proj_grad, ((0,), (0,))), parts], axis=1)]
  transfers between devices with their start and end apart: 2 -> 2, of which waited for: 0 -> 0; matrix products, arithmetic and copies ran while one was open for 8% -> 6% of each run, Pallas kernels for 46% -> 56%
where the time goes in v3:
time: 1000 us; the launch traced here: 994 us
  Pallas kernels  868 us (87%)
  local copies, waits for them, and re-layouts  57.1 us (6%)
  matrix products  35.8 us (4%)
  other arithmetic  19.8 us (2%)
  starting transfers between devices  11.5 us (1%)
    pallas_call x2, Pallas kernels, gather_all(): pl.pallas_call(functools.partial(gather_kernel, chunks), out_shape=tuple(...  321 us
    pallas_call x1, Pallas kernels, ffn(): pl.pallas_call(ffn_kernel, out_shape=(jax.ShapeDtypeStruct((tok_rows, wid...  315 us
    pallas_call x1, Pallas kernels, product_sums(): pl.pallas_call(functools.partial(product_sums_kernel, chunk), out_shape=(...  156 us
    pallas_call x1, Pallas kernels, sum_over_devices(): pl.pallas_call(functools.partial(sum_kernel, chunk), out_shape=jax.ShapeD...  49.4 us
    dot_general x2, matrix products, dot(): lax.dot_general(left, right, (contract, ((), ())), preferred_element_type...  21.6 us
  transfers between devices with their start and end apart: 2, of which 0 were waited for; matrix products, arithmetic and copies ran while one was open for 6% of the time, Pallas kernels for 56%

profile of v3, /device:TPU:0, one launch (start us, length us, event | category | flops | bytes accessed | tf_op | source)
XLA Modules:
  0.0 994.4 jit_solution(10310245836338420333)
XLA Ops:
  0.6 4.0 reshape.231
  4.7 0.7 copy.95
  5.4 4.0 reshape.230
  9.5 0.7 copy.94
  10.2 2.0 fusion.7
  12.2 7.6 all-to-all-start
  20.2 0.8 fusion.22.refs_0_
  21.0 287.7 %gather_weights.1 = (bf16[4,2,2,2,80,3200]{5,4,3,2,1,0:T(8,128)(2,1)}, bf16[4,2,2,2,80,2560]{5,4,3,2,1,0:T(8,128)(2,1)}, bf16[4,2,2,2,128,2560]{5,4,3,2,1,0:T(8,128)(2,1)}) custom-call(bf16[80,3200]{1,0:T(8,128)(2,1)} %fusion.22.refs_0_, bf16[80,2560]{1,0:T(8,128)(2,1)} %refs_1_.1, bf16[128,2560]{1,0:T(8,128)(2,1)} %refs_2_.1), custom_call_target="tpu_custom_call" | custom-call | tf_op jit(solution)/shard_map/gather_weights/pallas_call | solution.py:549
  308.7 1.1 slice.137
  311.1 7.0 fusion.2
  318.1 1.3 slice.140
  319.7 1.7 copy.89
  321.5 1.2 fusion.31
  323.8 0.9 pad_maximum_fusion.1.refs_0_
  324.7 32.9 %gather_kv.1 = bf16[4,2,2,2,128,512]{5,4,3,2,1,0:T(8,128)(2,1)} custom-call(bf16[128,512]{1,0:T(8,128)(2,1)} %pad_maximum_fusion.1.refs_0_), custom_call_target="tpu_custom_call" | custom-call | tf_op jit(solution)/shard_map/gather_kv/pallas_call | solution.py:549
  357.6 1.1 pad.30.down_ref
  358.8 2.7 convert_reduce_fusion
  361.5 1.8 constant_dynamic-slice_fusion.kv_ref
  363.3 10.8 %attend.1 = (bf16[128,2560]{1,0:T(8,128)(2,1)S(1)}, f32[5,256,128]{2,1,0:T(8,128)S(1)}) custom-call(s32[1]{0:T(128)} %bitcast.place_ref, bf16[128,2560]{1,0:T(8,128)(2,1)S(1)} %copy.93.query_ref, bf16[2176,512]{1,0:T(8,128)(2,1)S(1)} %constant_dynamic-slice_fusion.kv_ref), custom_call_target="tpu_custom_call" | custom-call | flops 2852126720 | bytes 8912896 | tf_op jit(solution)/shard_map/attend/pallas_call | solution.py:125
  374.2 7.2 multiply_reduce_fusion.2
  382.4 1.0 multiply_convert_fusion.hidden_ref
  384.1 314.8 %feed_forward.1 = (f32[128,2560]{1,0:T(8,128)}, f32[128,2560]{1,0:T(8,128)}, f32[512,2560]{1,0:T(8,128)}, f32[256,2560]{1,0:T(8,128)}, f32[8,512]{1,0:T(8,128)},...) custom-call(bf16[128,2560]{1,0:T(8,128)(2,1)} %multiply_convert_fusi, ...), custom_call_target="tpu_custom_call" | custom-call | tf_op jit(solution)/shard_map/feed_forward/pallas_call | solution.py:774
  698.9 2.8 multiply_reduce_fusion
  702.3 9.5 convolution_convert_fusion.grad_ref
  712.1 2.7 copy.101
  714.7 3.9 all-to-all-start.1
  718.7 1.1 copy-done.6
  719.8 16.6 %attend_back.1 = (f32[128,2560]{1,0:T(8,128)S(1)}, f32[2176,512]{1,0:T(8,128)}) custom-call(s32[1]{0:T(128)} %bitcast.place_ref, bf16[128,2560]{1,0:T(8,128)(2,1)S(1)} %copy-done.4, bf16[2176,512]{1,0:T(8,128)(2,1)S(1)} %copy-done.2, f32[5,256,128]{2,1,0:T(8,128)S(1)} %copy-done.6, bf16[128,2560]{1,0:T(8,128)(2,1)S(1)} %convolution_convert_fusion.grad_ref), custom_call_target="tpu_custom_call" | custom-call | flops 7130316800 | bytes 8912896 | tf_op jit(solution)/shard_map/attend_back/pallas_call | solution.py:148
  737.3 1.9 copy-done.18
  739.6 2.0 copy-done.10
  741.6 49.4 %sum_grad_kv.1 = f32[128,512]{1,0:T(8,128)} custom-call(bf16[4,2,2,2,128,512]{5,4,3,2,1,0:T(8,128)(2,1)} %bitcast.38), custom_call_target="tpu_custom_call" | custom-call | tf_op jit(solution)/shard_map/sum_grad_kv/pallas_call | solution.py:280
  790.9 0.9 slice.184
  791.9 1.2 fusion.37
  794.5 12.2 %fusion.18 = (bf16[2560]{0:T(1024)(128)(2,1)S(1)}, f32[128]{0:T(128)S(1)}, f32[128,2560]{1,0:T(8,128)}) fusion(bf16[128,2560]{1,0:T(8,128)(2,1)S(1)} %copy-done.14, f32[128]{0:T(128)S(1)} %copy-done.35, f32[2560]{0:T(1024)S(1)} %copy-done.30, bf16[128,3072]{1,0:T(8,128)(2,1)S(1)} %concatenate.34.right_b, bf16[2560,3200]{1,0:T(8,128)(2,1)} %bitcast.51), kind=kOutput, calls=%fused_computation.28 | convolution fusion | flops 2015556992 | bytes 18497536 | tf_op jit(solution)/shard_map/dot_general | solution.py:45
  807.1 1.0 pad.33.extra
  808.1 156.2 %sum_products.1 = (f32[80,2560]{1,0:T(8,128)}, f32[80,3200]{1,0:T(8,128)}) custom-call(bf16[128,2560]{1,0:T(8,128)(2,1)} %copy-done, bf16[128,2560]{1,0:T(8,128)(2,1)} %copy-done.15, bf16[128,2560]{1,0:T(8,128)(2,1)} %copy-done.20, bf16[128,3072]{1,0:T(8,128)(2,1)} %copy-done.19, bf16[2560,128]{1,0:T(8,128)(2,1)} %pad.33.extra), custom_call_target="tpu_custom_call" | custom-call | tf_op jit(solution)/shard_map/sum_products/pallas_call | solution.py:426
  964.4 2.2 slice.127
  966.6 1.6 slice.128
  968.2 3.4 slice.136
  971.6 1.6 slice_reduce_fusion
  973.2 1.3 fusion.46
  974.5 1.8 fusion.17
  976.3 2.5 convert_bitcast_fusion
  979.3 3.0 copy.102
  982.3 3.9 reshape.235
  986.2 3.0 copy.103
  989.2 4.0 reshape.236
  993.3 0.9 copy.107
  (138 shorter events, 9.0 us)
Async XLA Ops:
  12.1 7.6 copy-start.13
  12.1 7.9 copy-start.42
  12.1 7.9 copy-start.43
  12.1 7.9 copy-start.44
  12.2 8.0 copy-start.26
  12.2 8.0 copy-start.31
  12.2 371.3 %all-to-all-start = ((bf16[32,80,512]{2,1,0:T(8,128)(2,1)}), bf16[32,80,512]{2,1,0:T(8,128)(2,1)}, u32[]{:S(2)}, u32[]{:S(2)}) async-start(bf16[32,80,512]{2,1,0:T(8,128)(2,1)} %fusion.7), calls=%async_computation | async-start | bytes 5242880 | tf_op jit(solution)/shard_map/all_to_all | solution.py:830
  20.0 290.8 %copy-start.34 = (f32[128]{0:T(128)}, f32[128]{0:T(128)S(1)}, u32[]{:S(2)}) copy-start(f32[128]{0:T(128)S(1)} %get-tuple-element.70) | copy-start | bytes 1540
  310.8 7.2 copy-start.29
  311.1 7.0 copy-start.20
  318.1 1.6 copy-start.21
  321.5 1.4 copy-start.36
  321.5 1.3 copy-start.38
  323.8 39.5 %copy-start.3 = (bf16[128,2560]{1,0:T(8,128)(2,1)}, bf16[128,2560]{1,0:T(8,128)(2,1)S(1)}, u32[]{:S(2)}) copy-start(bf16[128,2560]{1,0:T(8,128)(2,1)S(1)} %copy.93.query_ref) | copy-start | bytes 1966084
  324.7 32.9 %copy-start.24 = (bf16[240,2560]{1,0:T(8,128)(2,1)S(1)}, bf16[240,2560]{1,0:T(8,128)(2,1)}, u32[]{:S(2)}) copy-start(bf16[240,2560]{1,0:T(8,128)(2,1)} %param.23) | copy-start | bytes 3686404
  363.3 10.9 %copy-start.1 = (bf16[2176,512]{1,0:T(8,128)(2,1)}, bf16[2176,512]{1,0:T(8,128)(2,1)S(1)}, u32[]{:S(2)}) copy-start(bf16[2176,512]{1,0:T(8,128)(2,1)S(1)} %constant_dynamic-slice_fusion.kv_ref) | copy-start | bytes 6684676
  374.2 7.2 copy-start
  374.2 7.2 copy-start.5
  374.2 7.9 copy-start.45
  374.2 7.9 copy-start.46
  381.4 1.1 copy-start.7
  384.1 317.7 %copy-start.16 = (bf16[128,2560]{1,0:T(8,128)(2,1)S(1)}, bf16[128,2560]{1,0:T(8,128)(2,1)}, u32[]{:S(2)}) copy-start(bf16[128,2560]{1,0:T(8,128)(2,1)} %refs_2_.1) | copy-start | bytes 1966084
  698.9 2.9 copy-start.8
  698.9 2.9 copy-start.11
  701.8 10.0 %slice-start = ((s8[5242880]{0:T(1024)(128)(4,1)}), s8[4194304]{0:T(1024)(128)(4,1)S(1)}, s32[]{:S(2)}) async-start(s8[5242880]{0:T(1024)(128)(4,1)} %bitcast.43), calls=%async_computation.2 | async-start | bytes 8388608
  702.3 9.5 copy-start.15
  702.3 9.5 slice-start.1
  714.7 3.9 copy-start.2
  714.7 4.0 copy-start.4
  714.7 261.6 %all-to-all-start.1 = ((bf16[32,80,512]{2,1,0:T(8,128)(2,1)}), bf16[32,80,512]{2,1,0:T(8,128)(2,1)}, u32[]{:S(2)}, u32[]{:S(2)}) async-start(bf16[32,80,512]{2,1,0:T(8,128)(2,1)} %bitcast.39), calls=%async_computation.1 | async-start | bytes 5242880 | tf_op jit(solution)/shard_map/all_to_all | solution.py:830
  718.7 1.1 copy-start.6
  736.9 2.3 copy-start.18
  739.6 2.0 copy-start.10
  741.6 50.3 %copy-start.37 = (f32[128]{0:T(128)S(1)}, f32[128]{0:T(128)}, u32[]{:S(2)}) copy-start(f32[128]{0:T(128)} %copy-done.36) | copy-start | bytes 1540
  741.6 50.3 %copy-start.39 = (f32[64]{0:T(128)S(1)}, f32[64]{0:T(128)}, u32[]{:S(2)}) copy-start(f32[64]{0:T(128)} %copy-done.38) | copy-start | bytes 772
  741.6 51.7 %copy-start.28 = (f32[128,64]{0,1:T(8,128)S(1)}, f32[128,64]{0,1:T(8,128)}, u32[]{:S(2)}) copy-start(f32[128,64]{0,1:T(8,128)} %copy-done.27) | copy-start | bytes 98308
  793.4 1.1 copy-start.14
  793.4 1.1 copy-start.30
  793.4 1.1 copy-start.35
  794.5 12.2 %copy-start.19 = (bf16[128,3072]{1,0:T(8,128)(2,1)}, bf16[128,3072]{1,0:T(8,128)(2,1)S(1)}, u32[]{:S(2)}) copy-start(bf16[128,3072]{1,0:T(8,128)(2,1)S(1)} %concatenate.34.right_b) | copy-start | bytes 2359300
  964.3 10.1 %copy-start.23 = (f32[128,2560]{1,0:T(8,128)S(1)}, f32[128,2560]{1,0:T(8,128)}, u32[]{:S(2)}) copy-start(f32[128,2560]{1,0:T(8,128)} %get-tuple-element.75) | copy-start | bytes 3932164
  968.2 6.3 copy-start.9
  968.2 6.3 copy-start.12
  968.2 6.3 copy-start.17
  968.2 6.3 copy-start.22
  968.2 6.3 copy-start.32
  968.2 6.3 copy-start.41
  989.2 4.0 copy-start.25
  (3 other events, 1.9 us)

commit v4 on v3

--- a/solution.py
+++ b/solution.py
@@ -54,11 +54,11 @@
     return jnp.pad(values, pad)
 
 
-def masked_scores(place_ref, query_rows, keys, tok_rows):
+def masked_scores(ahead, query_rows, keys, tok_rows):
     scores = dot(query_rows, keys, ((1,), (1,)))
     rows = lax.broadcasted_iota(jnp.int32, scores.shape, 0) % tok_rows
     columns = lax.broadcasted_iota(jnp.int32, scores.shape, 1)
-    distance = rows - columns + place_ref[0]
+    distance = rows - columns + ahead
     return jnp.where((distance >= 0) & (distance < WINDOW), scores, NEGATIVE)
 
 
@@ -71,16 +71,21 @@
     return jnp.concatenate([rows[i * tok_rows : (i + 1) * tok_rows] for i in range(PAIR)], axis=1)
 
 
-def attend_kernel(place_ref, query_ref, kv_ref, out_ref, log_ref):
-    tok_rows = query_ref.shape[0]
-    scores = masked_scores(place_ref, stack_heads(query_ref[...]), kv_ref[:, :HD], tok_rows)
+def attend_pair(ahead, query, keys, values):
+    tok_rows = query.shape[0]
+    scores = masked_scores(ahead, stack_heads(query), keys, tok_rows)
     row_max = jnp.max(scores, axis=1, keepdims=True)
     probs = jnp.exp(scores - row_max)
     row_sum = jnp.sum(probs, axis=1, keepdims=True)
     probs_low = (probs * (1.0 / row_sum)).astype(BF16)
-    attended = dot(probs_low, kv_ref[:, HD:], ((1,), (0,)))
-    out_ref[...] = unstack_heads(attended).astype(BF16)
-    log_ref[0] = jnp.broadcast_to(row_max + jnp.log(row_sum), log_ref.shape[1:])
+    attended = dot(probs_low, values, ((1,), (0,)))
+    return unstack_heads(attended).astype(BF16), row_max + jnp.log(row_sum)
+
+
+def attend_kernel(place_ref, query_ref, kv_ref, out_ref, log_ref):
+    attended, logs = attend_pair(place_ref[0], query_ref[...], kv_ref[:, :HD], kv_ref[:, HD:])
+    out_ref[...] = attended
+    log_ref[0] = jnp.broadcast_to(logs, log_ref.shape[1:])
 
 
 def attend_back_kernel(place_ref, query_ref, kv_ref, log_ref, grad_ref, query_grad_ref, kv_grad_ref):
@@ -88,7 +93,7 @@
     query_rows = stack_heads(query_ref[...])
     grad_rows = stack_heads(grad_ref[...])
     keys, values = kv_ref[:, :HD], kv_ref[:, HD:]
-    scores = masked_scores(place_ref, query_rows, keys, tok_rows)
+    scores = masked_scores(place_ref[0], query_rows, keys, tok_rows)
     probs = jnp.exp(scores - log_ref[0][:, :1])
     prob_grad = dot(grad_rows, values, ((1,), (1,)))
     delta = jnp.sum(probs * prob_grad, axis=1, keepdims=True)
@@ -567,6 +572,102 @@
     half = 0.5 * (1.0 + t)
     slope = half + 0.5 * v * (1.0 - t * t) * (GELU_SCALE * (1.0 + 3.0 * GELU_CUBE * square))
     return v * half, slope
+
+def gather_attend_kernel(
+    kv_ref, weight_ref, cotangent_ref, query_ref,
+    kv_held, weight_held, cotangent_held, window, out_ref, log_ref,
+    kv_sems, weight_sems, cotangent_sems, load_sems,
+):
+    place = Place()
+    me = lax.axis_index(AXIS)
+    tok_rows, features = query_ref.shape
+    blocks = window.shape[0] // tok_rows
+    start = jnp.maximum(me - (blocks - 1), 0)
+    place.meet()
+
+    def item(own, held, sems):
+        return Gather(place, own, held, pl.ds(0, own.shape[1]), sems)
+
+    kv = item(kv_ref, kv_held, kv_sems)
+    weight = item(weight_ref, weight_held, weight_sems)
+    cotangent = item(cotangent_ref, cotangent_held, cotangent_sems)
+    for one in (kv, weight, cotangent):
+        one.start()
+
+    def run(*steps):
+        for one, name, k in steps:
+            getattr(one, name)(k)
+
+    run(
+        (kv, "line", 0), (weight, "line", 0), (kv, "line", 1), (kv, "side", 0),
+        (kv, "line", 2), (kv, "side", 1), (kv, "diag", 0), (kv, "line", 3),
+        (kv, "side", 2), (kv, "diag", 1), (kv, "side", 3), (kv, "diag", 2), (kv, "diag", 3),
+        (weight, "line", 1), (cotangent, "line", 0), (weight, "side", 0), (weight, "line", 2),
+        (weight, "side", 1), (weight, "diag", 0), (weight, "line", 3), (cotangent, "line", 1),
+        (kv, "ready", 0), (kv, "ready", 1), (kv, "ready", 2), (kv, "ready", 3),
+    )
+    loads = []
+    for j in range(blocks):
+        block = start + j
+        load = pltpu.make_async_copy(
+            kv_held.at[block // 8, (block // 4) % 2, (block // 2) % 2, block % 2],
+            window.at[pl.ds(j * tok_rows, tok_rows)],
+            load_sems.at[j],
+        )
+        load.start()
+        loads.append(load)
+    for load in loads:
+        load.wait()
+    run((weight, "side", 2), (weight, "diag", 1))
+    ahead = (me - start) * tok_rows
+
+    @pl.loop(0, features // (PAIR * HD))
+    def _(i):
+        here = pl.ds(pl.multiple_of(i * PAIR * HD, PAIR * HD), PAIR * HD)
+        attended, logs = attend_pair(ahead, query_ref[:, here], window[:, :HD], window[:, HD:])
+        out_ref[:, here] = attended
+        log_ref[i] = jnp.broadcast_to(logs, log_ref.shape[1:])
+
+    run(
+        (cotangent, "side", 0), (weight, "side", 3), (weight, "diag", 2), (cotangent, "line", 2),
+        (weight, "diag", 3), (cotangent, "side", 1), (cotangent, "diag", 0),
+        (cotangent, "line", 3), (cotangent, "side", 2), (cotangent, "diag", 1),
+        (cotangent, "side", 3), (cotangent, "diag", 2), (cotangent, "diag", 3),
+    )
+    for one in (weight, cotangent):
+        for k in range(PLANES):
+            one.ready(k)
+    for one in (kv, weight, cotangent):
+        one.finish()
+
+
+def gather_attend(own_kv, out_weight, out_cotangent, queries, collective_id):
+    tok_rows, features = queries.shape
+    blocks = (WINDOW + tok_rows - 2) // tok_rows + 1
+    pairs = features // HD // PAIR
+    arrays = (own_kv, out_weight, out_cotangent)
+    hbm = pl.BlockSpec(memory_space=pl.ANY)
+    vmem = pl.BlockSpec(memory_space=pltpu.VMEM)
+    outs = pl.pallas_call(
+        gather_attend_kernel,
+        out_shape=tuple(jax.ShapeDtypeStruct((4, 2, 2, 2) + a.shape, BF16) for a in arrays)
+        + (
+            jax.ShapeDtypeStruct((blocks * tok_rows, own_kv.shape[1]), BF16),
+            jax.ShapeDtypeStruct((tok_rows, features), BF16),
+            jax.ShapeDtypeStruct((pairs, PAIR * tok_rows, LANES), F32),
+        ),
+        in_specs=[hbm] * 3 + [vmem],
+        out_specs=(hbm,) * 3 + (vmem,) * 3,
+        scratch_shapes=[pltpu.SemaphoreType.DMA((2, Gather.COPIES, PLANES)) for _ in arrays]
+        + [pltpu.SemaphoreType.DMA((blocks,))],
+        compiler_params=pltpu.CompilerParams(
+            collective_id=collective_id, has_side_effects=True, vmem_limit_bytes=VMEM_BYTES
+        ),
+        name="gather_attend",
+    )(*arrays, queries)
+    full = [o.reshape(32 * a.shape[0], a.shape[1]) for o, a in zip(outs[1:3], arrays[1:])]
+    return full[0], full[1], outs[3], outs[4], outs[5]
+
 
 class PlaneSum:
     SLOTS = 10
@@ -913,9 +1014,7 @@
     packed = jnp.concatenate(
         [query_weight, keyvalue_weight, pad_columns(vectors, LANES)], axis=1
     )
-    first, out_full, cotangent_full = gather_rows(
-        [packed, out_weight, out_cotangent], 5, "gather_weights"
-    )
+    first = gather_rows([packed], 5, "gather_weights")[0]
     proj_cols = query_cols + kv_cols
     proj_full = first[:, :proj_cols]
     gains = first[:, proj_cols:].astype(F32).T
@@ -945,9 +1044,17 @@
     reach = min((WINDOW + tok_rows - 2) // tok_rows, peers - 1)
     window_rows = (reach + 1) * tok_rows
     window_start = jnp.maximum(device - reach, 0) * tok_rows
-    kv_window = lax.dynamic_slice_in_dim(gather_rows([own_kv], 6, "gather_kv")[0], window_start, window_rows, 0)
     place = (device * tok_rows - window_start).astype(jnp.int32).reshape(1)
-    attention, logs = attend(place, queries, kv_window)
+    if peers == DEVICES:
+        out_full, cotangent_full, kv_window, attention, logs = gather_attend(
+            own_kv, out_weight, out_cotangent, queries, 6
+        )
+    else:
+        kv_full, out_full, cotangent_full = gather_rows(
+            [own_kv, out_weight, out_cotangent], None, None
+        )
+        kv_window = lax.dynamic_slice_in_dim(kv_full, window_start, window_rows, 0)
+        attention, logs = attend(place, queries, kv_window)
 
     residual_mid = resid_in + jnp.dot(attention, out_full, preferred_element_type=F32)
     square_two = jnp.mean(residual_mid * residual_mid, axis=1, keepdims=True)

time: 1000 us -> 985 us (0.985)
  Pallas kernels: 868 us -> 848 us
    pallas_call x2 -> x1, Pallas kernels: 321 us -> 145 us  [gather_all(): pl.pallas_call(functools.partial(gather_kernel, chunks), out_shape=tuple(...]
    pallas_call x1, Pallas kernels: 10.8 us -> 169 us  [gather_attend(): pl.pallas_call(gather_attend_kernel, out_shape=tuple((jax.ShapeDtypeStruc...]
  transfers between devices with their start and end apart: 2 -> 2, of which waited for: 0 -> 0; matrix products, arithmetic and copies ran while one was open for 6% -> 6% of each run, Pallas kernels for 56% -> 54%
where the time goes in v4:
time: 985 us; the launch traced here: 979 us
  Pallas kernels  848 us (86%)
  local copies, waits for them, and re-layouts  58.1 us (6%)
  matrix products  36.1 us (4%)
  other arithmetic  23.7 us (2%)
  starting transfers between devices  11.4 us (1%)
    pallas_call x1, Pallas kernels, ffn(): pl.pallas_call(ffn_kernel, out_shape=(jax.ShapeDtypeStruct((tok_rows, wid...  315 us
    pallas_call x1, Pallas kernels, gather_attend(): pl.pallas_call(gather_attend_kernel, out_shape=tuple((jax.ShapeDtypeStruc...  169 us
    pallas_call x1, Pallas kernels, product_sums(): pl.pallas_call(functools.partial(product_sums_kernel, chunk), out_shape=(...  156 us
    pallas_call x1, Pallas kernels, gather_all(): pl.pallas_call(functools.partial(gather_kernel, chunks), out_shape=tuple(...  145 us
    pallas_call x1, Pallas kernels, sum_over_devices(): pl.pallas_call(functools.partial(sum_kernel, chunk), out_shape=jax.ShapeD...  46.9 us
    dot_general x2, matrix products, dot(): lax.dot_general(left, right, (contract, ((), ())), preferred_element_type...  22.4 us
  transfers between devices with their start and end apart: 2, of which 0 were waited for; matrix products, arithmetic and copies ran while one was open for 6% of the time, Pallas kernels for 54%

profile of v4, /device:TPU:0, one launch (start us, length us, event | category | flops | bytes accessed | tf_op | source)
XLA Modules:
  0.0 978.8 jit_solution(6376561335015929059)
XLA Ops:
  0.6 4.0 reshape.225
  4.7 0.7 copy.94
  5.4 4.0 reshape.226
  9.5 0.7 copy.95
  10.2 2.0 fusion.7
  12.2 7.6 all-to-all-start
  20.0 0.8 fusion.22.refs_0_
  20.8 144.7 %gather_weights.1 = bf16[4,2,2,2,80,3200]{5,4,3,2,1,0:T(8,128)(2,1)} custom-call(bf16[80,3200]{1,0:T(8,128)(2,1)} %fusion.22.refs_0_), custom_call_target="tpu_custom_call" | custom-call | tf_op jit(solution)/shard_map/gather_weights/pallas_call | solution.py:554
  165.5 1.1 slice.137
  167.0 0.9 copy-done.16
  168.5 7.0 fusion.2
  177.2 2.7 pad.30.down_ref
  180.0 168.6 %gather_attend.1 = (bf16[4,2,2,2,128,512]{5,4,3,2,1,0:T(8,128)(2,1)}, bf16[4,2,2,2,80,2560]{5,4,3,2,1,0:T(8,128)(2,1)}, bf16[4,2,2,2,128,2560]{5,4,3,2,1,0:T(8,1...) custom-call(bf16[128,512]{1,0:T(8,128)(2,1)S(1)} %pad_maximum_fusion.1.kv_ref, ...), custom_call_target="tpu_custom_call" | custom-call | tf_op jit(solution)/shard_map/gather_attend/pallas_call | solution.py:651
  348.6 4.0 convert_reduce_fusion
  352.6 6.7 multiply_reduce_fusion.2
  360.4 1.0 multiply_convert_fusion.hidden_ref
  362.0 314.9 %feed_forward.1 = (f32[128,2560]{1,0:T(8,128)}, f32[128,2560]{1,0:T(8,128)}, f32[512,2560]{1,0:T(8,128)}, f32[256,2560]{1,0:T(8,128)}, f32[8,512]{1,0:T(8,128)},...) custom-call(bf16[128,2560]{1,0:T(8,128)(2,1)} %multiply_convert_fusi, ...), custom_call_target="tpu_custom_call" | custom-call | tf_op jit(solution)/shard_map/feed_forward/pallas_call | solution.py:875
  677.0 2.3 multiply_reduce_fusion
  679.9 10.3 %convolution_convert_fusion.grad_ref = bf16[128,2560]{1,0:T(8,128)(2,1)} fusion(bf16[128,2560]{1,0:T(8,128)(2,1)S(1)} %fusion.44.right_a, bf16[2560,2560]{1,0:T(8,128)(2,1)} %bitcast.35), kind=kOutput, calls=%fused_computation.10 | convolution fusion | flops 1678049280 | bytes 14417920 | tf_op jit(solution)/shard_map/dot_general | solution.py:45
  690.2 1.8 convert_bitcast_fusion.1
  692.0 4.5 copy.101
  696.4 3.8 all-to-all-start.1
  700.3 1.1 copy-done.4
  701.4 1.6 copy-done.7
  703.0 1.1 copy-done.9
  704.1 16.6 %attend_back.1 = (f32[128,2560]{1,0:T(8,128)S(1)}, f32[2176,512]{1,0:T(8,128)}) custom-call(s32[1]{0:T(128)} %bitcast.12.place_ref, bf16[128,2560]{1,0:T(8,128)(2,1)S(1)} %copy-done.3, bf16[2176,512]{1,0:T(8,128)(2,1)S(1)} %copy-done.7, f32[5,256,128]{2,1,0:T(8,128)S(1)} %copy-done.9, bf16[128,2560]{1,0:T(8,128)(2,1)S(1)} %copy-done.4), custom_call_target="tpu_custom_call" | custom-call | flops 7130316800 | bytes 8912896 | tf_op jit(solution)/shard_map/attend_back/pallas_call | solution.py:153
  721.0 2.7 convert_dynamic-update-slice_fusion
  723.7 1.9 copy-done.13
  725.6 46.9 %sum_grad_kv.1 = f32[128,512]{1,0:T(8,128)} custom-call(bf16[4,2,2,2,128,512]{5,4,3,2,1,0:T(8,128)(2,1)} %bitcast.40), custom_call_target="tpu_custom_call" | custom-call | tf_op jit(solution)/shard_map/sum_grad_kv/pallas_call | solution.py:285
  772.5 0.9 slice.184
  773.4 1.2 fusion.37
  774.7 1.2 broadcast_multiply_fusion
  775.9 1.7 copy.97
  778.9 12.2 %fusion.18 = (bf16[2560]{0:T(1024)(128)(2,1)S(1)}, f32[128]{0:T(128)S(1)}, f32[128,2560]{1,0:T(8,128)}) fusion(bf16[128,2560]{1,0:T(8,128)(2,1)S(1)} %copy-done.18, f32[128]{0:T(128)S(1)} %get-tuple-element.72, f32[2560]{0:T(1024)S(1)} %get-tuple-element.49, bf16[128,3072]{1,0:T(8,128)(2,1)S(1)} %concatenate.34.right_b, bf16[2560,3200]{1,0:T(8,128)(2,1)} %bitcast.39), kind=kOutput, calls=%fused_computation.28 | convolution fusion | flops 2015556992 | bytes 18497536 | tf_op jit(solution)/shard_map/dot_general | solution.py:45
  791.6 1.0 pad.33.extra
  792.5 156.3 %sum_products.1 = (f32[80,2560]{1,0:T(8,128)}, f32[80,3200]{1,0:T(8,128)}) custom-call(bf16[128,2560]{1,0:T(8,128)(2,1)} %copy-done.1, bf16[128,2560]{1,0:T(8,128)(2,1)} %copy-done.19, bf16[128,2560]{1,0:T(8,128)(2,1)} %copy-done.21, bf16[128,3072]{1,0:T(8,128)(2,1)} %copy-done.20, bf16[2560,128]{1,0:T(8,128)(2,1)} %pad.33.extra), custom_call_target="tpu_custom_call" | custom-call | tf_op jit(solution)/shard_map/sum_products/pallas_call | solution.py:431
  948.8 2.1 slice.127
  951.0 1.7 slice.128
  952.7 3.4 slice.136
  956.1 1.6 slice_reduce_fusion
  957.7 1.3 fusion.46
  959.0 1.8 fusion.17
  960.8 2.5 convert_bitcast_fusion
  963.7 3.0 copy.102
  966.8 3.9 reshape.231
  970.7 3.0 copy.103
  973.7 4.0 reshape.232
  977.7 0.9 copy.107
  (106 shorter events, 7.6 us)
Async XLA Ops:
  12.2 7.6 copy-start.27
  12.2 7.6 copy-start.28
  12.2 7.6 copy-start.29
  12.2 7.8 copy-start.25
  12.2 7.8 copy-start.26
  12.2 349.2 %all-to-all-start = ((bf16[32,80,512]{2,1,0:T(8,128)(2,1)}), bf16[32,80,512]{2,1,0:T(8,128)(2,1)}, u32[]{:S(2)}, u32[]{:S(2)}) async-start(bf16[32,80,512]{2,1,0:T(8,128)(2,1)} %fusion.7), calls=%async_computation | async-start | bytes 5242880 | tf_op jit(solution)/shard_map/all_to_all | solution.py:931
  166.9 1.1 copy-start.16
  168.5 7.0 copy-start.21
  177.1 2.8 copy-start.2
  177.2 2.8 copy-start
  177.2 2.8 copy-start.5
  180.0 172.6 %copy-start.17 = (bf16[128,2560]{1,0:T(8,128)(2,1)S(1)}, bf16[128,2560]{1,0:T(8,128)(2,1)}, u32[]{:S(2)}) copy-start(bf16[128,2560]{1,0:T(8,128)(2,1)} %param.13) | copy-start | bytes 1966084
  348.6 10.7 %copy-start.1 = (bf16[128,2560]{1,0:T(8,128)(2,1)}, bf16[128,2560]{1,0:T(8,128)(2,1)S(1)}, u32[]{:S(2)}) copy-start(bf16[128,2560]{1,0:T(8,128)(2,1)S(1)} %get-tuple-element.29.left_a) | copy-start | bytes 1966084
  348.6 10.7 %copy-start.6 = (bf16[2176,512]{1,0:T(8,128)(2,1)}, bf16[2176,512]{1,0:T(8,128)(2,1)S(1)}, u32[]{:S(2)}) copy-start(bf16[2176,512]{1,0:T(8,128)(2,1)S(1)} %get-tuple-element.34.kv_ref) | copy-start | bytes 6684676
  348.6 10.7 %copy-start.8 = (f32[5,256,128]{2,1,0:T(8,128)}, f32[5,256,128]{2,1,0:T(8,128)S(1)}, u32[]{:S(2)}) copy-start(f32[5,256,128]{2,1,0:T(8,128)S(1)} %get-tuple-element.35.log_ref) | copy-start | bytes 1966084
  352.6 7.4 copy-start.30
  352.6 7.4 copy-start.31
  359.3 1.1 copy-start.10
  676.9 2.3 copy-start.11
  676.9 2.5 copy-start.14
  679.4 10.7 %slice-start = ((s8[5242880]{0:T(1024)(128)(4,1)}), s8[4194304]{0:T(1024)(128)(4,1)S(1)}, s32[]{:S(2)}) async-start(s8[5242880]{0:T(1024)(128)(4,1)} %bitcast.44), calls=%async_computation.2 | async-start | bytes 8388608
  679.9 10.3 %copy-start.19 = (bf16[128,2560]{1,0:T(8,128)(2,1)}, bf16[128,2560]{1,0:T(8,128)(2,1)S(1)}, u32[]{:S(2)}) copy-start(bf16[128,2560]{1,0:T(8,128)(2,1)S(1)} %fusion.44.right_a) | copy-start | bytes 1966084
  679.9 10.3 %slice-start.1 = ((s8[5242880]{0:T(1024)(128)(4,1)}), s8[1048576]{0:T(1024)(128)(4,1)S(1)}, s32[]{:S(2)}) async-start(s8[5242880]{0:T(1024)(128)(4,1)} %bitcast.44), calls=%async_computation.3 | async-start | bytes 2097152
  696.4 3.8 copy-start.3
  696.4 264.3 %all-to-all-start.1 = ((bf16[32,80,512]{2,1,0:T(8,128)(2,1)}), bf16[32,80,512]{2,1,0:T(8,128)(2,1)}, u32[]{:S(2)}, u32[]{:S(2)}) async-start(bf16[32,80,512]{2,1,0:T(8,128)(2,1)} %bitcast.41), calls=%async_computation.1 | async-start | bytes 5242880 | tf_op jit(solution)/shard_map/all_to_all | solution.py:931
  700.3 1.1 copy-start.4
  701.4 1.6 copy-start.7
  703.0 1.1 copy-start.9
  723.6 1.9 copy-start.13
  777.8 1.1 copy-start.18
  778.9 12.2 %copy-start.20 = (bf16[128,3072]{1,0:T(8,128)(2,1)}, bf16[128,3072]{1,0:T(8,128)(2,1)S(1)}, u32[]{:S(2)}) copy-start(bf16[128,3072]{1,0:T(8,128)(2,1)S(1)} %concatenate.34.right_b) | copy-start | bytes 2359300
  950.9 8.0 copy-start.23
  952.6 6.3 copy-start.12
  952.6 6.3 copy-start.15
  952.7 6.3 copy-start.22
  973.7 4.0 copy-start.24

commit v5 on v4

--- a/solution.py
+++ b/solution.py
@@ -88,19 +88,24 @@
     log_ref[0] = jnp.broadcast_to(logs, log_ref.shape[1:])
 
 
-def attend_back_kernel(place_ref, query_ref, kv_ref, log_ref, grad_ref, query_grad_ref, kv_grad_ref):
-    tok_rows = query_ref.shape[0]
-    query_rows = stack_heads(query_ref[...])
-    grad_rows = stack_heads(grad_ref[...])
-    keys, values = kv_ref[:, :HD], kv_ref[:, HD:]
-    scores = masked_scores(place_ref[0], query_rows, keys, tok_rows)
-    probs = jnp.exp(scores - log_ref[0][:, :1])
+def attend_back_pair(ahead, query, grad, keys, values, logs):
+    tok_rows = query.shape[0]
+    query_rows, grad_rows = stack_heads(query), stack_heads(grad)
+    scores = masked_scores(ahead, query_rows, keys, tok_rows)
+    probs = jnp.exp(scores - logs)
     prob_grad = dot(grad_rows, values, ((1,), (1,)))
     delta = jnp.sum(probs * prob_grad, axis=1, keepdims=True)
     score_grad = (probs * (prob_grad - delta)).astype(BF16)
-    query_grad_ref[...] = unstack_heads(dot(score_grad, keys, ((1,), (0,))))
+    query_grad = unstack_heads(dot(score_grad, keys, ((1,), (0,))))
     key_part = dot(score_grad, query_rows, ((0,), (0,)))
     value_part = dot(probs.astype(BF16), grad_rows, ((0,), (0,)))
+    return query_grad, key_part, value_part
+
+
+def attend_back_kernel(place_ref, query_ref, kv_ref, log_ref, grad_ref, query_grad_ref, kv_grad_ref):
+    query_grad_ref[...], key_part, value_part = attend_back_pair(
+        place_ref[0], query_ref[...], grad_ref[...], kv_ref[:, :HD], kv_ref[:, HD:], log_ref[0][:, :1]
+    )
 
     @pl.when(pl.program_id(0) == 0)
     def _():
@@ -198,102 +203,6 @@
     return copy
 
 TILE=16
-def add_rows(total, other, first, count):
-    planes = other.shape[0]
-    steps = count // TILE
-    @pl.loop(0, planes * steps)
-    def _(i):
-        plane, row = i // steps, (i % steps) * TILE
-        here = (plane, pl.ds(pl.multiple_of(row + first, TILE), TILE), slice(None))
-        there = (plane, pl.ds(pl.multiple_of(row, TILE), TILE), slice(None))
-        total[here] = (total[here].astype(F32) + other[there].astype(F32)).astype(BF16)
-
-def sum_kernel(chunk, in_ref, out_ref, acc, got_core, got_diag_x, got_diag_y, got_x, got_y, got_z,
-               load_sem, core_sems, diag_sems, side_sems, line_sems):
-    place = Place()
-    rows, columns = out_ref.shape
-    upper = got_diag_x.shape[1]
-    lower = rows - upper
-    chunks = columns // chunk
-    corners = [(1, 1), (0, 1), (1, 0), (0, 0)]
-    cols = [pl.ds(k * chunk, chunk) for k in range(chunks)]
-    loads, cores, sends = {}, {}, []
-    for k in range(chunks):
-        for i, (dy, dx) in enumerate(corners):
-            y, x = place.side(dy, dx)
-            load = pltpu.make_async_copy(in_ref.at[:, y, x, place.core, :, cols[k]], acc.at[i, :, :, cols[k]], load_sem.at[k, i])
-            load.start()
-            loads[k, i] = load
-    place.meet()
-    for k in range(chunks):
-        for i, (dy, dx) in enumerate(corners):
-            y, x = place.side(dy, dx)
-            cores[k, i] = send(in_ref.at[:, y, x, 1 - place.core, :, cols[k]], got_core.at[i, :, :, cols[k]],
-                               (core_sems.at[0, k, i], core_sems.at[1, k, i]), place.sibling)
-    top, bottom = pl.ds(0, upper), pl.ds(upper, lower)
-    diag, side, line = {}, {}, {}
-    def pair(sems, k, i): return (sems.at[0, k, i], sems.at[1, k, i])
-    def stage0(k):
-        for i in range(4):
-            loads[k, i].wait(); cores[k, i].wait_recv()
-            add_rows(acc.at[i, :, :, cols[k]], got_core.at[i, :, :, cols[k]], 0, rows)
-            if i == 0:
-                diag[k, 0] = send(acc.at[0, :, top, cols[k]], got_diag_x.at[:, :, cols[k]], pair(diag_sems, k, 0), place.next_x)
-                diag[k, 1] = send(acc.at[0, :, bottom, cols[k]], got_diag_y.at[:, :, cols[k]], pair(diag_sems, k, 1), place.next_y)
-            if i == 1:
-                side[k, 0] = send(acc.at[1, :, top, cols[k]], got_x.at[:, top, cols[k]], pair(side_sems, k, 0), place.next_x)
-            if i == 2:
-                side[k, 1] = send(acc.at[2, :, bottom, cols[k]], got_y.at[:, bottom, cols[k]], pair(side_sems, k, 1), place.next_y)
-    def stage1(k):
-        diag[k, 0].wait_recv()
-        add_rows(acc.at[2, :, :, cols[k]], got_diag_x.at[:, :, cols[k]], 0, upper)
-        side[k, 2] = send(acc.at[2, :, top, cols[k]], got_y.at[:, top, cols[k]], pair(side_sems, k, 2), place.next_y)
-        diag[k, 1].wait_recv()
-        add_rows(acc.at[1, :, :, cols[k]], got_diag_y.at[:, :, cols[k]], upper, lower)
-        side[k, 3] = send(acc.at[1, :, bottom, cols[k]], got_x.at[:, bottom, cols[k]], pair(side_sems, k, 3), place.next_x)
-    def stage2(k):
-        for i in range(4): side[k, i].wait_recv()
-        steps = rows // TILE
-        @pl.loop(0, 4 * steps)
-        def _(i):
-            plane, row = i // steps, (i % steps) * TILE
-            here = (plane, pl.ds(pl.multiple_of(row, TILE), TILE), cols[k])
-            acc[(3,) + here] = (acc[(3,) + here].astype(F32) + got_x[here].astype(F32) + got_y[here].astype(F32)).astype(BF16)
-        for o in (1, 2, 3):
-            line[k, o] = send(acc.at[3, place.plane[o], :, cols[k]], got_z.at[o - 1, :, cols[k]], pair(line_sems, k, o - 1), place.line[o])
-    def stage3(k):
-        for o in (1, 2, 3): line[k, o].wait_recv()
-        @pl.loop(0, rows // TILE)
-        def _(i):
-            here = (pl.ds(pl.multiple_of(i * TILE, TILE), TILE), cols[k])
-            total = acc[(3, place.z) + here].astype(F32)
-            for o in range(3): total += got_z[(o,) + here].astype(F32)
-            out_ref[here] = total
-    stages = [stage0, stage1, stage2, stage3]
-    for step in range(chunks + 3):
-        for s in range(3, -1, -1):
-            if 0 <= step - s < chunks: stages[s](step - s)
-    for group in (cores, diag, side, line):
-        for copy in group.values(): copy.wait_send()
-
-def sum_over_devices(partial, chunk, collective_id, name):
-    rows, columns = partial.shape[0] // 32, partial.shape[1]
-    chunks = columns // chunk
-    upper = (rows // 2 + TILE - 1) // TILE * TILE
-    def buf(*shape): return pltpu.VMEM(shape, BF16)
-    def sems(count): return pltpu.SemaphoreType.DMA((2, chunks, count))
-    return pl.pallas_call(
-        functools.partial(sum_kernel, chunk),
-        out_shape=jax.ShapeDtypeStruct((rows, columns), F32),
-        in_specs=[pl.BlockSpec(memory_space=pl.ANY)],
-        out_specs=pl.BlockSpec(memory_space=pltpu.VMEM),
-        scratch_shapes=[buf(4, 4, rows, columns), buf(4, 4, rows, columns), buf(4, upper, columns), buf(4, rows - upper, columns),
-            buf(4, rows, columns), buf(4, rows, columns), buf(3, rows, columns),
-            pltpu.SemaphoreType.DMA((chunks, 4)), sems(4), sems(2), sems(4), sems(3)],
-        compiler_params=pltpu.CompilerParams(collective_id=collective_id, has_side_effects=True, vmem_limit_bytes=56*1024*1024),
-        name=name,
-    )(partial.reshape(4, 2, 2, 2, rows, columns))
-
 
 CORNERS = ((1, 1), (0, 1), (1, 0), (0, 0))
 
@@ -381,62 +290,186 @@
     def finish(self):
         for slot in range(4, 13): self.copies[slot].wait_send()
 
-def product_sums_kernel(chunk, left_a, right_a, left_b, right_b, extra, out_a, out_b, part, *scratch):
-    place = Place()
-    bufs = SumBuffers(scratch)
-    rows = out_a.shape[0]
+def product_units(place, bufs, part, chunk, left, right, out, extra):
+    rows = out.shape[0]
     wide = 8 * rows
     units = []
-    def add_unit(left, right, out, first, span, more):
-        k = len(units)
+
+    def add_unit(k, first):
         slot = k % 2
-        def own(i):
+        span = min(chunk, right.shape[1] - first)
+
+        def half(i, core):
             y, x = place.side(*CORNERS[i])
-            return part.at[slot, :, y, x, place.core]
-        def other(i):
-            y, x = place.side(*CORNERS[i])
-            return part.at[slot, :, y, x, 1 - place.core]
-        cols = pl.ds(k * chunk, chunk)
-        unit = Sum(place, bufs, k, cols, own, other, out.at[:, pl.ds(first, chunk)])
+            return part.at[slot, :, y, x, core]
+
+        unit = Sum(
+            place, bufs, k, pl.ds(k * chunk, chunk),
+            lambda i: half(i, place.core), lambda i: half(i, 1 - place.core),
+            out.at[:, pl.ds(first, chunk)],
+        )
+
         def make():
-            if k >= 2: units[k - 2][0].core_sent()
+            if k >= 2:
+                units[k - 2][0].core_sent()
+
             @pl.loop(0, 4)
             def _(z):
                 here = pl.ds(pl.multiple_of(z * wide, wide), wide)
-                product = lax.dot_general(left[:, here], right[:, pl.ds(first, span)], (((0,), (0,)), ((), ())), preferred_element_type=F32)
-                part[slot, z, :, :, :, :, pl.ds(0, span)] = product.astype(BF16).reshape(2, 2, 2, rows, span)
-                if more is not None:
-                    part[slot, z, :, :, :, :, pl.ds(span, chunk - span)] = more[here].reshape(2, 2, 2, rows, chunk - span)
+                product = dot(left[:, here], right[:, pl.ds(first, span)], ((0,), (0,)))
+                block = (2, 2, 2, rows)
+                part[slot, z, :, :, :, :, pl.ds(0, span)] = product.astype(BF16).reshape(block + (span,))
+                if span < chunk:
+                    part[slot, z, :, :, :, :, pl.ds(span, chunk - span)] = extra[here].reshape(
+                        block + (chunk - span,)
+                    )
+
             unit.begin()
+
         units.append((unit, make))
-    for first in range(0, out_a.shape[1], chunk):
-        add_unit(left_a, right_a, out_a, first, chunk, None)
-    for first in range(0, out_b.shape[1], chunk):
-        span = min(chunk, right_b.shape[1] - first)
-        add_unit(left_b, right_b, out_b, first, span, None if span == chunk else extra)
+
+    for k, first in enumerate(range(0, out.shape[1], chunk)):
+        add_unit(k, first)
+    return units
+
+
+def product_sum_kernel(chunk, left, right, extra, out, part, *scratch):
+    place = Place()
+    units = product_units(place, SumBuffers(scratch), part, chunk, left, right, out, extra)
     place.meet()
     count = len(units)
-    stages = [lambda k: units[k][1](), lambda k: units[k][0].stage0(), lambda k: units[k][0].stage1(), lambda k: units[k][0].stage2(), lambda k: units[k][0].stage3()]
+    stages = [lambda k: units[k][1]()] + [
+        lambda k, name=name: getattr(units[k][0], name)()
+        for name in ("stage0", "stage1", "stage2", "stage3")
+    ]
     for step in range(count + 4):
         for s in (1, 2, 3, 4, 0):
-            if 0 <= step - s < count: stages[s](step - s)
-    for unit, _ in units[-2:]: unit.core_sent()
-    for unit, _ in units: unit.finish()
-
-def product_sums(left_a, right_a, left_b, right_b, extra, chunk, collective_id, name):
-    rows = left_a.shape[1] // 32
-    columns_a, columns_b = right_a.shape[1], right_b.shape[1] + extra.shape[1]
-    total = columns_a + columns_b
+            if 0 <= step - s < count:
+                stages[s](step - s)
+    for unit, _ in units[-2:]:
+        unit.core_sent()
+    for unit, _ in units:
+        unit.finish()
+
+
+def product_sum(left, right, extra, chunk, collective_id, name):
+    rows = left.shape[1] // 32
+    columns = right.shape[1] + extra.shape[1]
     vmem = pl.BlockSpec(memory_space=pltpu.VMEM)
     return pl.pallas_call(
-        functools.partial(product_sums_kernel, chunk),
-        out_shape=(jax.ShapeDtypeStruct((rows, columns_a), F32), jax.ShapeDtypeStruct((rows, columns_b), F32)),
-        in_specs=[vmem] * 5,
-        out_specs=(vmem, vmem),
-        scratch_shapes=[pltpu.VMEM((2, 4, 2, 2, 2, rows, chunk), BF16)] + SumBuffers.shapes(rows, total, total // chunk),
-        compiler_params=pltpu.CompilerParams(collective_id=collective_id, has_side_effects=True, vmem_limit_bytes=62*1024*1024),
+        functools.partial(product_sum_kernel, chunk),
+        out_shape=jax.ShapeDtypeStruct((rows, columns), F32),
+        in_specs=[vmem] * 3,
+        out_specs=vmem,
+        scratch_shapes=[pltpu.VMEM((2, 4, 2, 2, 2, rows, chunk), BF16)]
+        + SumBuffers.shapes(rows, columns, columns // chunk),
+        compiler_params=pltpu.CompilerParams(
+            collective_id=collective_id, has_side_effects=True, vmem_limit_bytes=62 * 1024 * 1024
+        ),
         name=name,
-    )(left_a, right_a, left_b, right_b, extra)
+    )(left, right, extra)
+
+
+def back_sums_kernel(
+    chunk, left, right, query_ref, window, log_ref, grad_ref,
+    out, query_grad_ref, kv_grad_ref, part, kv_total, kv_part, *scratch,
+):
+    place = Place()
+    me = lax.axis_index(AXIS)
+    tok_rows, features = query_ref.shape
+    blocks = window.shape[0] // tok_rows
+    start = jnp.maximum(me - (blocks - 1), 0)
+    ahead = (me - start) * tok_rows
+    units = product_units(
+        place, SumBuffers(scratch[: SumBuffers.COUNT]), part, chunk, left, right, out, None
+    )
+    sums = [unit for unit, _ in units]
+
+    def half(i, core):
+        y, x = place.side(*CORNERS[i])
+        return kv_part.at[:, y, x, core]
+
+    kv = Sum(
+        place, SumBuffers(scratch[SumBuffers.COUNT :]), 0, pl.ds(0, 2 * HD),
+        lambda i: half(i, place.core), lambda i: half(i, 1 - place.core), kv_grad_ref,
+    )
+    place.meet()
+    units[0][1]()
+    units[1][1]()
+    sums[0].stage0()
+    sums[1].stage0()
+    kv_total[...] = jnp.zeros_like(kv_total)
+    kv_part[...] = jnp.zeros_like(kv_part)
+
+    @pl.loop(0, features // (PAIR * HD))
+    def _(i):
+        here = pl.ds(pl.multiple_of(i * PAIR * HD, PAIR * HD), PAIR * HD)
+        query_grad, key_part, value_part = attend_back_pair(
+            ahead, query_ref[:, here], grad_ref[:, here], window[:, :HD], window[:, HD:],
+            log_ref[i][:, :1],
+        )
+        query_grad_ref[:, here] = query_grad
+        kv_total[:, :HD] += key_part
+        kv_total[:, HD:] += value_part
+
+    for j in range(blocks):
+        block = start + j
+        kv_part[block // 8, (block // 4) % 2, (block // 2) % 2, block % 2] = kv_total[
+            j * tok_rows : (j + 1) * tok_rows
+        ].astype(BF16)
+    kv.begin()
+    sums[0].stage1()
+    kv.stage0()
+    sums[1].stage1()
+    units[2][1]()
+    kv.stage1()
+    sums[0].stage2()
+    sums[2].stage0()
+    kv.stage2()
+    sums[1].stage2()
+    units[3][1]()
+    sums[2].stage1()
+    sums[3].stage0()
+    kv.stage3()
+    sums[0].stage3()
+    sums[2].stage2()
+    sums[3].stage1()
+    sums[1].stage3()
+    sums[3].stage2()
+    sums[2].stage3()
+    sums[3].stage3()
+    for unit in sums[2:] + [kv]:
+        unit.core_sent()
+    for unit in sums + [kv]:
+        unit.finish()
+
+
+def back_sums(left, right, queries, kv_window, logs, grad, collective_id):
+    rows, columns = left.shape[1] // 32, right.shape[1]
+    tok_rows, features = queries.shape
+    chunk = columns // 4
+    vmem = pl.BlockSpec(memory_space=pltpu.VMEM)
+    return pl.pallas_call(
+        functools.partial(back_sums_kernel, chunk),
+        out_shape=(
+            jax.ShapeDtypeStruct((rows, columns), F32),
+            jax.ShapeDtypeStruct((tok_rows, features), F32),
+            jax.ShapeDtypeStruct((tok_rows, 2 * HD), F32),
+        ),
+        in_specs=[vmem] * 6,
+        out_specs=(vmem,) * 3,
+        scratch_shapes=[
+            pltpu.VMEM((2, 4, 2, 2, 2, rows, chunk), BF16),
+            pltpu.VMEM(kv_window.shape, F32),
+            pltpu.VMEM((4, 2, 2, 2, tok_rows, 2 * HD), BF16),
+        ]
+        + SumBuffers.shapes(rows, columns, 4)
+        + SumBuffers.shapes(tok_rows, 2 * HD, 1),
+        compiler_params=pltpu.CompilerParams(
+            collective_id=collective_id, has_side_effects=True, vmem_limit_bytes=62 * 1024 * 1024
+        ),
+        name="back_sums",
+    )(left, right, queries, kv_window, logs, grad)
 
 
 PLANES=4
@@ -908,23 +941,10 @@
     return [lax.all_gather(values, AXIS, axis=0, tiled=True) for values in arrays]
 
 
-def sum_rows(partial, chunk, collective_id, name):
-    if lax.axis_size(AXIS) == DEVICES:
-        return sum_over_devices(partial.astype(BF16), chunk, collective_id, name)
+def sum_rows(partial):
     return lax.psum_scatter(
         partial.astype(BF16), AXIS, scatter_dimension=0, tiled=True
     ).astype(F32)
-
-
-def sum_products(left_a, right_a, left_b, right_b, extra):
-    if lax.axis_size(AXIS) == DEVICES:
-        return product_sums(left_a, right_a, left_b, right_b, extra, 640, 2, "sum_products")
-    product_a = dot(left_a, right_a, ((0,), (0,)))
-    product_b = dot(left_b, right_b, ((0,), (0,))).astype(BF16)
-    return (
-        sum_rows(product_a, None, None, None),
-        sum_rows(jnp.concatenate([product_b, extra], axis=1), None, None, None),
-    )
 
 
 def swap(pieces):
@@ -955,10 +975,8 @@
         gate_grad = (hidden_grad * up_pre * slope).astype(BF16)
         up_grad = (hidden_grad * activated).astype(BF16)
         both_grad = jnp.concatenate([gate_grad, up_grad], axis=1)
-        normed_grad = sum_rows(dot(both_grad, both_own, ((1,), (1,))), None, None, None)
-        ffn_out = sum_rows(
-            jnp.dot(hidden_ffn, down_own, preferred_element_type=F32), None, None, None
-        )
+        normed_grad = sum_rows(dot(both_grad, both_own, ((1,), (1,))))
+        ffn_out = sum_rows(jnp.dot(hidden_ffn, down_own, preferred_element_type=F32))
         shares = (
             dot(hidden_full, both_grad, ((0,), (0,))),
             dot(hidden_ffn, cotangent_piece, ((0,), (0,))),
@@ -1093,11 +1111,18 @@
     mid_grad_low = mid_grad.astype(BF16)
     attention_grad = dot(mid_grad_low, out_full, ((1,), (1,))).astype(BF16)
 
-    query_grad, kv_part = attend_back(place, queries, kv_window, logs, attention_grad)
-    kv_partial = lax.dynamic_update_slice_in_dim(
-        jnp.zeros((peers * tok_rows, 2 * HD), BF16), kv_part.astype(BF16), window_start, 0
-    )
-    kv_grad = sum_rows(kv_partial, 256, 3, "sum_grad_kv")
+    if peers == DEVICES:
+        grad_out, query_grad, kv_grad = back_sums(
+            attention, mid_grad_low, queries, kv_window, logs, attention_grad, 3
+        )
+    else:
+        grad_out = sum_rows(dot(attention, mid_grad_low, ((0,), (0,))))
+        query_grad, kv_part = attend_back(place, queries, kv_window, logs, attention_grad)
+        kv_grad = sum_rows(
+            lax.dynamic_update_slice_in_dim(
+                jnp.zeros((peers * tok_rows, 2 * HD), BF16), kv_part.astype(BF16), window_start, 0
+            )
+        )
     query_raw_grad = (
         rotate(
             query_grad.reshape(tok_rows, heads, HD) * query_scale,
@@ -1121,9 +1146,14 @@
     ).astype(BF16)
 
     parts = pad_columns(jnp.stack([norm1_part, norm2_part], axis=1), LANES)
-    grad_out, tail = sum_products(
-        attention, mid_grad_low, hidden_one, proj_grad, parts.astype(BF16)
-    )
+    if peers == DEVICES:
+        tail = product_sum(hidden_one, proj_grad, parts.astype(BF16), 640, 2, "sum_projections")
+    else:
+        tail = sum_rows(
+            jnp.concatenate(
+                [dot(hidden_one, proj_grad, ((0,), (0,))).astype(BF16), parts.astype(BF16)], axis=1
+            )
+        )
     grad_proj = tail[:, :proj_cols]
     norm1_share = tail[:, proj_cols]
     norm2_share = tail[:, proj_cols + 1]

time: 985 us -> 971 us (0.986)
  Pallas kernels: 848 us -> 834 us
    pallas_call x3 -> x2, Pallas kernels: 220 us -> 206 us  [the longest x1 110 us: back_sums(): pl.pallas_call(functools.partial(back_sums_kernel, chunk), out_shape=(jax...]
  transfers between devices with their start and end apart: 2 -> 2, of which waited for: 0 -> 0; matrix products, arithmetic and copies ran while one was open for 6% -> 7% of each run, Pallas kernels for 54% -> 54%
where the time goes in v5:
time: 971 us; the launch traced here: 963 us
  Pallas kernels  834 us (86%)
  local copies, waits for them, and re-layouts  54.8 us (6%)
  matrix products  35.6 us (4%)
  other arithmetic  25.1 us (3%)
  starting transfers between devices  11.9 us (1%)
    pallas_call x1, Pallas kernels, ffn(): pl.pallas_call(ffn_kernel, out_shape=(jax.ShapeDtypeStruct((tok_rows, wid...  315 us
    pallas_call x1, Pallas kernels, gather_attend(): pl.pallas_call(gather_attend_kernel, out_shape=tuple((jax.ShapeDtypeStruc...  169 us
    pallas_call x1, Pallas kernels, gather_all(): pl.pallas_call(functools.partial(gather_kernel, chunks), out_shape=tuple(...  145 us
    pallas_call x1, Pallas kernels, back_sums(): pl.pallas_call(functools.partial(back_sums_kernel, chunk), out_shape=(jax...  110 us
    pallas_call x1, Pallas kernels, product_sum(): pl.pallas_call(functools.partial(product_sum_kernel, chunk), out_shape=ja...  96.3 us
    dot_general x2, matrix products, dot(): lax.dot_general(left, right, (contract, ((), ())), preferred_element_type...  22 us
  transfers between devices with their start and end apart: 2, of which 0 were waited for; matrix products, arithmetic and copies ran while one was open for 7% of the time, Pallas kernels for 54%

profile of v5, /device:TPU:0, one launch (start us, length us, event | category | flops | bytes accessed | tf_op | source)
XLA Modules:
  0.0 962.7 jit_solution(16639221002175947042)
XLA Ops:
  0.6 4.0 reshape.219
  4.7 0.7 copy.94
  5.4 4.0 reshape.220
  9.5 0.7 copy.95
  10.2 2.0 fusion.7
  12.2 7.9 all-to-all-start
  20.6 0.8 fusion.22.refs_0_
  21.4 144.5 %gather_weights.1 = bf16[4,2,2,2,80,3200]{5,4,3,2,1,0:T(8,128)(2,1)} custom-call(bf16[80,3200]{1,0:T(8,128)(2,1)} %fusion.22.refs_0_), custom_call_target="tpu_custom_call" | custom-call | tf_op jit(solution)/shard_map/gather_weights/pallas_call | solution.py:587
  165.9 1.1 slice.137
  167.8 7.0 fusion.2
  174.8 1.1 copy-done.16
  175.9 1.2 slice.143
  177.0 1.7 copy.90
  178.8 1.2 multiply_cosine_fusion
  180.8 2.7 pad.30.down_ref
  183.6 168.6 %gather_attend.1 = (bf16[4,2,2,2,128,512]{5,4,3,2,1,0:T(8,128)(2,1)}, bf16[4,2,2,2,80,2560]{5,4,3,2,1,0:T(8,128)(2,1)}, bf16[4,2,2,2,128,2560]{5,4,3,2,1,0:T(8,1...) custom-call(bf16[128,512]{1,0:T(8,128)(2,1)S(1)} %pad_maximum_fusion.1.kv_ref, ...), custom_call_target="tpu_custom_call" | custom-call | tf_op jit(solution)/shard_map/gather_attend/pallas_call | solution.py:684
  352.2 4.0 convert_reduce_fusion
  356.2 6.7 multiply_reduce_fusion.2
  363.0 0.6 pad_maximum_fusion.4
  364.0 1.0 multiply_convert_fusion.hidden_ref
  365.0 0.6 broadcast_in_dim.2.bias_ref
  365.6 314.9 %feed_forward.1 = (f32[128,2560]{1,0:T(8,128)}, f32[128,2560]{1,0:T(8,128)}, f32[512,2560]{1,0:T(8,128)}, f32[256,2560]{1,0:T(8,128)}, f32[8,512]{1,0:T(8,128)},...) custom-call(bf16[128,2560]{1,0:T(8,128)(2,1)} %multiply_convert_fusi, ...), custom_call_target="tpu_custom_call" | custom-call | tf_op jit(solution)/shard_map/feed_forward/pallas_call | solution.py:908
  680.5 2.3 multiply_reduce_fusion
  683.4 4.5 convert_bitcast_fusion.1
  687.9 4.5 copy.101
  692.3 3.9 all-to-all-start.1
  696.3 9.8 %convolution_convert_fusion.grad_ref = bf16[128,2560]{1,0:T(8,128)(2,1)} fusion(bf16[128,2560]{1,0:T(8,128)(2,1)S(1)} %fusion.44.right, bf16[2560,2560]{1,0:T(8,128)(2,1)} %bitcast.33), kind=kOutput, calls=%fused_computation.10 | convolution fusion | flops 1678049280 | bytes 14417920 | tf_op jit(solution)/shard_map/dot_general | solution.py:45
  706.1 109.7 %back_sums.1 = (f32[80,2560]{1,0:T(8,128)}, f32[128,2560]{1,0:T(8,128)}, f32[128,512]{1,0:T(8,128)}) custom-call(bf16[128,2560]{1,0:T(8,128)(2,1)} %copy-done.2, bf16[128,2560]{1,0:T(8,128)(2,1)} %copy-done.13, bf16[128,2560]{1,0:T(8,128)(2,1)} %copy-done.1, bf16[2176,512]{1,0:T(8,128)(2,1)} %copy-done.3, f32[5,256,128]{2,1,0:T(8,128)} %copy-done.4, ...), custom_call_target="tpu_custom_call" | custom-call | tf_op jit(solution)/shard_map/back_sums/pallas_call | solution.py:452
  815.8 1.4 broadcast_multiply_fusion
  817.2 1.5 copy.97
  819.1 1.2 slice.183
  820.3 1.2 subtract_convert_fusion
  822.6 12.2 %fusion.18 = (bf16[2560]{0:T(1024)(128)(2,1)S(1)}, f32[128]{0:T(128)S(1)}, f32[128,2560]{1,0:T(8,128)}) fusion(bf16[128,2560]{1,0:T(8,128)(2,1)S(1)} %copy-done.12, f32[128]{0:T(128)S(1)} %get-tuple-element.70, f32[2560]{0:T(1024)S(1)} %get-tuple-element.47, bf16[128,3072]{1,0:T(8,128)(2,1)S(1)} %concatenate.34.right, bf16[2560,3200]{1,0:T(8,128)(2,1)} %bitcast.37), kind=kOutput, calls=%fused_computation.27 | convolution fusion | flops 2015556992 | bytes 18497536 | tf_op jit(solution)/shard_map/dot_general | solution.py:45
  835.2 1.0 pad.33.extra
  836.2 96.3 %sum_projections.1 = f32[80,3200]{1,0:T(8,128)} custom-call(bf16[128,2560]{1,0:T(8,128)(2,1)} %copy-done.15, bf16[128,3072]{1,0:T(8,128)(2,1)} %copy-done.14, bf16[2560,128]{1,0:T(8,128)(2,1)} %pad.33.extra), custom_call_target="tpu_custom_call" | custom-call | tf_op jit(solution)/shard_map/sum_projections/pallas_call | solution.py:359
  932.5 1.6 slice.128
  934.1 2.2 slice.127
  936.3 3.4 slice.136
  939.7 1.6 slice_reduce_fusion
  941.3 1.3 fusion.46
  942.6 1.8 fusion.17
  944.4 2.5 convert_bitcast_fusion
  946.9 0.5 fusion.45
  947.4 3.0 copy.103
  950.4 4.1 reshape.224
  954.5 3.0 copy.102
  957.6 4.0 reshape.223
  961.6 0.9 copy.106
  (90 shorter events, 5.0 us)
Async XLA Ops:
  12.2 8.0 copy-start.11
  12.2 8.2 copy-start.23
  12.2 8.2 copy-start.24
  12.2 8.2 copy-start.25
  12.2 8.4 copy-start.20
  12.2 8.4 copy-start.22
  12.2 352.8 %all-to-all-start = ((bf16[32,80,512]{2,1,0:T(8,128)(2,1)}), bf16[32,80,512]{2,1,0:T(8,128)(2,1)}, u32[]{:S(2)}, u32[]{:S(2)}) async-start(bf16[32,80,512]{2,1,0:T(8,128)(2,1)} %fusion.7), calls=%async_computation | async-start | bytes 5242880 | tf_op jit(solution)/shard_map/all_to_all | solution.py:951
  167.7 7.0 copy-start.15
  174.7 1.1 copy-start.16
  180.7 2.8 copy-start.1
  180.8 2.8 copy-start
  180.8 2.8 copy-start.5
  352.2 10.7 %copy-start.2 = (bf16[128,2560]{1,0:T(8,128)(2,1)}, bf16[128,2560]{1,0:T(8,128)(2,1)S(1)}, u32[]{:S(2)}) copy-start(bf16[128,2560]{1,0:T(8,128)(2,1)S(1)} %get-tuple-element.28.left) | copy-start | bytes 1966084
  352.2 10.7 %copy-start.3 = (bf16[2176,512]{1,0:T(8,128)(2,1)}, bf16[2176,512]{1,0:T(8,128)(2,1)S(1)}, u32[]{:S(2)}) copy-start(bf16[2176,512]{1,0:T(8,128)(2,1)S(1)} %get-tuple-element.33.window) | copy-start | bytes 6684676
  352.2 10.7 %copy-start.4 = (f32[5,256,128]{2,1,0:T(8,128)}, f32[5,256,128]{2,1,0:T(8,128)S(1)}, u32[]{:S(2)}) copy-start(f32[5,256,128]{2,1,0:T(8,128)S(1)} %get-tuple-element.34.log_ref) | copy-start | bytes 1966084
  356.2 7.4 copy-start.26
  356.2 7.4 copy-start.27
  362.9 1.1 copy-start.6
  680.5 2.3 copy-start.7
  680.5 2.5 copy-start.9
  683.4 12.9 %copy-start.13 = (bf16[128,2560]{1,0:T(8,128)(2,1)}, bf16[128,2560]{1,0:T(8,128)(2,1)S(1)}, u32[]{:S(2)}) copy-start(bf16[128,2560]{1,0:T(8,128)(2,1)S(1)} %fusion.44.right) | copy-start | bytes 1966084
  692.3 252.1 %all-to-all-start.1 = ((bf16[32,80,512]{2,1,0:T(8,128)(2,1)}), bf16[32,80,512]{2,1,0:T(8,128)(2,1)}, u32[]{:S(2)}, u32[]{:S(2)}) async-start(bf16[32,80,512]{2,1,0:T(8,128)(2,1)} %bitcast.38), calls=%async_computation.1 | async-start | bytes 5242880 | tf_op jit(solution)/shard_map/all_to_all | solution.py:951
  817.2 1.5 copy-start.21
  821.5 1.1 copy-start.12
  822.6 12.2 %copy-start.14 = (bf16[128,3072]{1,0:T(8,128)(2,1)}, bf16[128,3072]{1,0:T(8,128)(2,1)S(1)}, u32[]{:S(2)}) copy-start(bf16[128,3072]{1,0:T(8,128)(2,1)S(1)} %concatenate.34.right) | copy-start | bytes 2359300
  934.1 8.5 copy-start.18
  936.3 6.3 copy-start.8
  936.3 6.3 copy-start.10
  936.3 6.3 copy-start.17
  957.6 4.0 copy-start.19

commit v6 on v5

--- a/solution.py
+++ b/solution.py
@@ -848,6 +848,8 @@
                 acc[kind, k, i] = jnp.where(place.core == 0, low, high)
                 outgoing[kind, i % 2] = jnp.where(place.core == 0, high, low)
                 sums[kind][k].across(i).start()
+
+    def weight_grads(k):
         step = 512
         @pl.loop(0, width // step)
         def _(j):
@@ -870,22 +872,26 @@
     compute(0)
     gather.line(3)
     gather.side(2)
+    weight_grads(0)
     gather.diag(1)
+    compute(1)
     gather.side(3)
-    compute(1)
+    both("stage0", 1)
     gather.diag(2)
+    weight_grads(1)
     gather.diag(3)
-    both("stage0", 1)
+    both("stage1", 1)
     compute(2)
-    both("stage1", 1)
     both("stage0", 2)
+    both("stage2", 1)
+    weight_grads(2)
     compute(3)
-    both("stage2", 1)
     both("stage1", 2)
     both("stage0", 3)
     both("stage2", 2)
     both("stage1", 3)
     both("stage0", 0)
+    weight_grads(3)
     both("stage2", 3)
     both("stage1", 0)
     both("stage2", 0)

time: 971 us -> 960 us (0.989)
  Pallas kernels: 834 us -> 823 us
    pallas_call x1, Pallas kernels: 315 us -> 304 us  [ffn(): pl.pallas_call(ffn_kernel, out_shape=(jax.ShapeDtypeStruct((tok_rows, wid...]
  transfers between devices with their start and end apart: 2 -> 2, of which waited for: 0 -> 0; matrix products, arithmetic and copies ran while one was open for 7% -> 8% of each run, Pallas kernels for 54% -> 55%
where the time goes in v6:
time: 960 us; the launch traced here: 952 us
  Pallas kernels  823 us (86%)
  local copies, waits for them, and re-layouts  54.8 us (6%)
  matrix products  35.6 us (4%)
  other arithmetic  25.1 us (3%)
  starting transfers between devices  11.9 us (1%)
    pallas_call x1, Pallas kernels, ffn(): pl.pallas_call(ffn_kernel, out_shape=(jax.ShapeDtypeStruct((tok_rows, wid...  304 us
    pallas_call x1, Pallas kernels, gather_attend(): pl.pallas_call(gather_attend_kernel, out_shape=tuple((jax.ShapeDtypeStruc...  169 us
    pallas_call x1, Pallas kernels, gather_all(): pl.pallas_call(functools.partial(gather_kernel, chunks), out_shape=tuple(...  145 us
    pallas_call x1, Pallas kernels, back_sums(): pl.pallas_call(functools.partial(back_sums_kernel, chunk), out_shape=(jax...  110 us
    pallas_call x1, Pallas kernels, product_sum(): pl.pallas_call(functools.partial(product_sum_kernel, chunk), out_shape=ja...  96.3 us
    dot_general x2, matrix products, dot(): lax.dot_general(left, right, (contract, ((), ())), preferred_element_type...  22 us
  transfers between devices with their start and end apart: 2, of which 0 were waited for; matrix products, arithmetic and copies ran while one was open for 8% of the time, Pallas kernels for 55%

profile of v6, /device:TPU:0, one launch (start us, length us, event | category | flops | bytes accessed | tf_op | source)
XLA Modules:
  0.0 951.8 jit_solution(15184992935527892991)
XLA Ops:
  0.6 4.0 reshape.219
  4.7 0.7 copy.94
  5.4 4.0 reshape.220
  9.5 0.7 copy.95
  10.2 2.0 fusion.7
  12.2 7.9 all-to-all-start
  20.6 0.8 fusion.22.refs_0_
  21.4 144.5 %gather_weights.1 = bf16[4,2,2,2,80,3200]{5,4,3,2,1,0:T(8,128)(2,1)} custom-call(bf16[80,3200]{1,0:T(8,128)(2,1)} %fusion.22.refs_0_), custom_call_target="tpu_custom_call" | custom-call | tf_op jit(solution)/shard_map/gather_weights/pallas_call | solution.py:587
  165.9 1.1 slice.137
  167.8 7.0 fusion.2
  174.8 1.1 copy-done.16
  175.9 1.2 slice.143
  177.0 1.7 copy.90
  178.8 1.2 multiply_cosine_fusion
  180.8 2.7 pad.30.down_ref
  183.6 168.6 %gather_attend.1 = (bf16[4,2,2,2,128,512]{5,4,3,2,1,0:T(8,128)(2,1)}, bf16[4,2,2,2,80,2560]{5,4,3,2,1,0:T(8,128)(2,1)}, bf16[4,2,2,2,128,2560]{5,4,3,2,1,0:T(8,1...) custom-call(bf16[128,512]{1,0:T(8,128)(2,1)S(1)} %pad_maximum_fusion.1.kv_ref, ...), custom_call_target="tpu_custom_call" | custom-call | tf_op jit(solution)/shard_map/gather_attend/pallas_call | solution.py:684
  352.2 4.0 convert_reduce_fusion
  356.2 6.7 multiply_reduce_fusion.2
  363.0 0.6 pad_maximum_fusion.4
  364.0 1.0 multiply_convert_fusion.hidden_ref
  365.0 0.6 broadcast_in_dim.2.bias_ref
  365.6 304.0 %feed_forward.1 = (f32[128,2560]{1,0:T(8,128)}, f32[128,2560]{1,0:T(8,128)}, f32[512,2560]{1,0:T(8,128)}, f32[256,2560]{1,0:T(8,128)}, f32[8,512]{1,0:T(8,128)},...) custom-call(bf16[128,2560]{1,0:T(8,128)(2,1)} %multiply_convert_fusi, ...), custom_call_target="tpu_custom_call" | custom-call | tf_op jit(solution)/shard_map/feed_forward/pallas_call | solution.py:914
  669.6 2.3 multiply_reduce_fusion
  672.5 4.5 convert_bitcast_fusion.1
  677.0 4.5 copy.101
  681.5 3.9 all-to-all-start.1
  685.4 9.8 %convolution_convert_fusion.grad_ref = bf16[128,2560]{1,0:T(8,128)(2,1)} fusion(bf16[128,2560]{1,0:T(8,128)(2,1)S(1)} %fusion.44.right, bf16[2560,2560]{1,0:T(8,128)(2,1)} %bitcast.33), kind=kOutput, calls=%fused_computation.10 | convolution fusion | flops 1678049280 | bytes 14417920 | tf_op jit(solution)/shard_map/dot_general | solution.py:45
  695.2 109.7 %back_sums.1 = (f32[80,2560]{1,0:T(8,128)}, f32[128,2560]{1,0:T(8,128)}, f32[128,512]{1,0:T(8,128)}) custom-call(bf16[128,2560]{1,0:T(8,128)(2,1)} %copy-done.2, bf16[128,2560]{1,0:T(8,128)(2,1)} %copy-done.13, bf16[128,2560]{1,0:T(8,128)(2,1)} %copy-done.1, bf16[2176,512]{1,0:T(8,128)(2,1)} %copy-done.3, f32[5,256,128]{2,1,0:T(8,128)} %copy-done.4, ...), custom_call_target="tpu_custom_call" | custom-call | tf_op jit(solution)/shard_map/back_sums/pallas_call | solution.py:452
  804.9 1.4 broadcast_multiply_fusion
  806.4 1.5 copy.97
  808.2 1.2 slice.183
  809.4 1.2 subtract_convert_fusion
  811.7 12.2 %fusion.18 = (bf16[2560]{0:T(1024)(128)(2,1)S(1)}, f32[128]{0:T(128)S(1)}, f32[128,2560]{1,0:T(8,128)}) fusion(bf16[128,2560]{1,0:T(8,128)(2,1)S(1)} %copy-done.12, f32[128]{0:T(128)S(1)} %get-tuple-element.70, f32[2560]{0:T(1024)S(1)} %get-tuple-element.47, bf16[128,3072]{1,0:T(8,128)(2,1)S(1)} %concatenate.34.right, bf16[2560,3200]{1,0:T(8,128)(2,1)} %bitcast.37), kind=kOutput, calls=%fused_computation.27 | convolution fusion | flops 2015556992 | bytes 18497536 | tf_op jit(solution)/shard_map/dot_general | solution.py:45
  824.4 1.0 pad.33.extra
  825.3 96.3 %sum_projections.1 = f32[80,3200]{1,0:T(8,128)} custom-call(bf16[128,2560]{1,0:T(8,128)(2,1)} %copy-done.15, bf16[128,3072]{1,0:T(8,128)(2,1)} %copy-done.14, bf16[2560,128]{1,0:T(8,128)(2,1)} %pad.33.extra), custom_call_target="tpu_custom_call" | custom-call | tf_op jit(solution)/shard_map/sum_projections/pallas_call | solution.py:359
  921.6 1.6 slice.128
  923.2 2.2 slice.127
  925.4 3.4 slice.136
  928.9 1.6 slice_reduce_fusion
  930.4 1.3 fusion.46
  931.7 1.8 fusion.17
  933.6 2.5 convert_bitcast_fusion
  936.0 0.5 fusion.45
  936.5 3.0 copy.103
  939.5 4.1 reshape.224
  943.7 3.0 copy.102
  946.7 4.0 reshape.223
  950.7 0.9 copy.106
  (90 shorter events, 5.0 us)
Async XLA Ops:
  12.2 8.0 copy-start.11
  12.2 8.2 copy-start.23
  12.2 8.2 copy-start.24
  12.2 8.2 copy-start.25
  12.2 8.4 copy-start.20
  12.2 8.4 copy-start.22
  12.2 352.8 %all-to-all-start = ((bf16[32,80,512]{2,1,0:T(8,128)(2,1)}), bf16[32,80,512]{2,1,0:T(8,128)(2,1)}, u32[]{:S(2)}, u32[]{:S(2)}) async-start(bf16[32,80,512]{2,1,0:T(8,128)(2,1)} %fusion.7), calls=%async_computation | async-start | bytes 5242880 | tf_op jit(solution)/shard_map/all_to_all | solution.py:957
  167.7 7.0 copy-start.15
  174.7 1.1 copy-start.16
  180.7 2.8 copy-start.1
  180.8 2.8 copy-start
  180.8 2.8 copy-start.5
  352.2 10.7 %copy-start.2 = (bf16[128,2560]{1,0:T(8,128)(2,1)}, bf16[128,2560]{1,0:T(8,128)(2,1)S(1)}, u32[]{:S(2)}) copy-start(bf16[128,2560]{1,0:T(8,128)(2,1)S(1)} %get-tuple-element.28.left) | copy-start | bytes 1966084
  352.2 10.7 %copy-start.3 = (bf16[2176,512]{1,0:T(8,128)(2,1)}, bf16[2176,512]{1,0:T(8,128)(2,1)S(1)}, u32[]{:S(2)}) copy-start(bf16[2176,512]{1,0:T(8,128)(2,1)S(1)} %get-tuple-element.33.window) | copy-start | bytes 6684676
  352.2 10.7 %copy-start.4 = (f32[5,256,128]{2,1,0:T(8,128)}, f32[5,256,128]{2,1,0:T(8,128)S(1)}, u32[]{:S(2)}) copy-start(f32[5,256,128]{2,1,0:T(8,128)S(1)} %get-tuple-element.34.log_ref) | copy-start | bytes 1966084
  356.2 7.4 copy-start.26
  356.2 7.4 copy-start.27
  362.9 1.1 copy-start.6
  669.6 2.3 copy-start.7
  669.6 2.5 copy-start.9
  672.5 12.9 %copy-start.13 = (bf16[128,2560]{1,0:T(8,128)(2,1)}, bf16[128,2560]{1,0:T(8,128)(2,1)S(1)}, u32[]{:S(2)}) copy-start(bf16[128,2560]{1,0:T(8,128)(2,1)S(1)} %fusion.44.right) | copy-start | bytes 1966084
  681.5 252.1 %all-to-all-start.1 = ((bf16[32,80,512]{2,1,0:T(8,128)(2,1)}), bf16[32,80,512]{2,1,0:T(8,128)(2,1)}, u32[]{:S(2)}, u32[]{:S(2)}) async-start(bf16[32,80,512]{2,1,0:T(8,128)(2,1)} %bitcast.38), calls=%async_computation.1 | async-start | bytes 5242880 | tf_op jit(solution)/shard_map/all_to_all | solution.py:957
  806.4 1.5 copy-start.21
  810.6 1.1 copy-start.12
  811.7 12.2 %copy-start.14 = (bf16[128,3072]{1,0:T(8,128)(2,1)}, bf16[128,3072]{1,0:T(8,128)(2,1)S(1)}, u32[]{:S(2)}) copy-start(bf16[128,3072]{1,0:T(8,128)(2,1)S(1)} %concatenate.34.right) | copy-start | bytes 2359300
  923.2 8.5 copy-start.18
  925.4 6.3 copy-start.8
  925.4 6.3 copy-start.10
  925.4 6.3 copy-start.17
  946.7 4.0 copy-start.19

commit v7 on v6

--- a/solution.py
+++ b/solution.py
@@ -208,7 +208,7 @@
 
 def add_tiles(count, rows, target, parts):
     steps = rows // TILE
-    @pl.loop(0, count * steps)
+    @pl.loop(0, count * steps, unroll=2)
     def _(i):
         index, here = i // steps, pl.ds(pl.multiple_of((i % steps) * TILE, TILE), TILE)
         total = None
@@ -741,7 +741,7 @@
         copy.start()
         return copy
     def add(self, target, slots, rows):
-        @pl.loop(0, rows // TILE)
+        @pl.loop(0, rows // TILE, unroll=2)
         def _(i):
             here = pl.ds(pl.multiple_of(i * TILE, TILE), TILE)
             total = target[here].astype(F32)

time: 960 us -> 959 us (level)
  no operation moved by 1% of the time
where the time goes in v7:
time: 959 us; the launch traced here: 951 us
  Pallas kernels  822 us (86%)
  local copies, waits for them, and re-layouts  54.8 us (6%)
  matrix products  35.7 us (4%)
  other arithmetic  25.1 us (3%)
  starting transfers between devices  11.3 us (1%)
    pallas_call x1, Pallas kernels, ffn(): pl.pallas_call(ffn_kernel, out_shape=(jax.ShapeDtypeStruct((tok_rows, wid...  304 us
    pallas_call x1, Pallas kernels, gather_attend(): pl.pallas_call(gather_attend_kernel, out_shape=tuple((jax.ShapeDtypeStruc...  169 us
    pallas_call x1, Pallas kernels, gather_all(): pl.pallas_call(functools.partial(gather_kernel, chunks), out_shape=tuple(...  145 us
    pallas_call x1, Pallas kernels, back_sums(): pl.pallas_call(functools.partial(back_sums_kernel, chunk), out_shape=(jax...  109 us
    pallas_call x1, Pallas kernels, product_sum(): pl.pallas_call(functools.partial(product_sum_kernel, chunk), out_shape=ja...  96.2 us
    dot_general x2, matrix products, dot(): lax.dot_general(left, right, (contract, ((), ())), preferred_element_type...  22 us
  transfers between devices with their start and end apart: 2, of which 0 were waited for; matrix products, arithmetic and copies ran while one was open for 8% of the time, Pallas kernels for 55%

profile of v7, /device:TPU:0, one launch (start us, length us, event | category | flops | bytes accessed | tf_op | source)
XLA Modules:
  0.0 950.8 jit_solution(18256504242073538163)
XLA Ops:
  0.6 4.0 reshape.219
  4.7 0.7 copy.94
  5.4 4.0 reshape.220
  9.5 0.7 copy.95
  10.2 2.0 fusion.7
  12.2 7.6 all-to-all-start
  20.2 0.8 fusion.22.refs_0_
  21.0 144.5 %gather_weights.1 = bf16[4,2,2,2,80,3200]{5,4,3,2,1,0:T(8,128)(2,1)} custom-call(bf16[80,3200]{1,0:T(8,128)(2,1)} %fusion.22.refs_0_), custom_call_target="tpu_custom_call" | custom-call | tf_op jit(solution)/shard_map/gather_weights/pallas_call | solution.py:587
  165.5 1.1 slice.137
  167.4 7.0 fusion.2
  174.4 1.1 copy-done.16
  175.5 1.2 slice.143
  176.7 1.7 copy.90
  178.4 1.2 multiply_cosine_fusion
  180.4 2.7 pad.30.down_ref
  183.2 168.6 %gather_attend.1 = (bf16[4,2,2,2,128,512]{5,4,3,2,1,0:T(8,128)(2,1)}, bf16[4,2,2,2,80,2560]{5,4,3,2,1,0:T(8,128)(2,1)}, bf16[4,2,2,2,128,2560]{5,4,3,2,1,0:T(8,1...) custom-call(bf16[128,512]{1,0:T(8,128)(2,1)S(1)} %pad_maximum_fusion.1.kv_ref, ...), custom_call_target="tpu_custom_call" | custom-call | tf_op jit(solution)/shard_map/gather_attend/pallas_call | solution.py:684
  351.8 4.0 convert_reduce_fusion
  355.8 6.7 multiply_reduce_fusion.2
  362.6 0.6 pad_maximum_fusion.4
  363.6 1.0 multiply_convert_fusion.hidden_ref
  364.7 0.6 broadcast_in_dim.2.bias_ref
  365.3 304.1 %feed_forward.1 = (f32[128,2560]{1,0:T(8,128)}, f32[128,2560]{1,0:T(8,128)}, f32[512,2560]{1,0:T(8,128)}, f32[256,2560]{1,0:T(8,128)}, f32[8,512]{1,0:T(8,128)},...) custom-call(bf16[128,2560]{1,0:T(8,128)(2,1)} %multiply_convert_fusi, ...), custom_call_target="tpu_custom_call" | custom-call | tf_op jit(solution)/shard_map/feed_forward/pallas_call | solution.py:914
  669.4 2.3 multiply_reduce_fusion
  672.3 4.5 convert_bitcast_fusion.1
  676.8 4.5 copy.101
  681.2 3.7 all-to-all-start.1
  685.0 9.8 %convolution_convert_fusion.grad_ref = bf16[128,2560]{1,0:T(8,128)(2,1)} fusion(bf16[128,2560]{1,0:T(8,128)(2,1)S(1)} %fusion.44.right, bf16[2560,2560]{1,0:T(8,128)(2,1)} %bitcast.33), kind=kOutput, calls=%fused_computation.10 | convolution fusion | flops 1678049280 | bytes 14417920 | tf_op jit(solution)/shard_map/dot_general | solution.py:45
  694.8 109.2 %back_sums.1 = (f32[80,2560]{1,0:T(8,128)}, f32[128,2560]{1,0:T(8,128)}, f32[128,512]{1,0:T(8,128)}) custom-call(bf16[128,2560]{1,0:T(8,128)(2,1)} %copy-done.2, bf16[128,2560]{1,0:T(8,128)(2,1)} %copy-done.13, bf16[128,2560]{1,0:T(8,128)(2,1)} %copy-done.1, bf16[2176,512]{1,0:T(8,128)(2,1)} %copy-done.3, f32[5,256,128]{2,1,0:T(8,128)} %copy-done.4, ...), custom_call_target="tpu_custom_call" | custom-call | tf_op jit(solution)/shard_map/back_sums/pallas_call | solution.py:452
  804.0 1.4 broadcast_multiply_fusion
  805.4 1.5 copy.97
  807.3 1.2 slice.183
  808.4 1.2 subtract_convert_fusion
  810.8 12.2 %fusion.18 = (bf16[2560]{0:T(1024)(128)(2,1)S(1)}, f32[128]{0:T(128)S(1)}, f32[128,2560]{1,0:T(8,128)}) fusion(bf16[128,2560]{1,0:T(8,128)(2,1)S(1)} %copy-done.12, f32[128]{0:T(128)S(1)} %get-tuple-element.70, f32[2560]{0:T(1024)S(1)} %get-tuple-element.47, bf16[128,3072]{1,0:T(8,128)(2,1)S(1)} %concatenate.34.right, bf16[2560,3200]{1,0:T(8,128)(2,1)} %bitcast.37), kind=kOutput, calls=%fused_computation.27 | convolution fusion | flops 2015556992 | bytes 18497536 | tf_op jit(solution)/shard_map/dot_general | solution.py:45
  823.4 1.0 pad.33.extra
  824.4 96.2 %sum_projections.1 = f32[80,3200]{1,0:T(8,128)} custom-call(bf16[128,2560]{1,0:T(8,128)(2,1)} %copy-done.15, bf16[128,3072]{1,0:T(8,128)(2,1)} %copy-done.14, bf16[2560,128]{1,0:T(8,128)(2,1)} %pad.33.extra), custom_call_target="tpu_custom_call" | custom-call | tf_op jit(solution)/shard_map/sum_projections/pallas_call | solution.py:359
  920.5 1.6 slice.128
  922.1 2.2 slice.127
  924.3 3.4 slice.136
  927.8 1.6 slice_reduce_fusion
  929.3 1.3 fusion.46
  930.6 1.8 fusion.17
  932.5 2.5 convert_bitcast_fusion
  934.9 0.5 fusion.45
  935.4 3.0 copy.103
  938.4 4.2 reshape.224
  942.6 3.0 copy.102
  945.6 4.0 reshape.223
  949.6 0.9 copy.106
  (90 shorter events, 5.0 us)
Async XLA Ops:
  12.2 7.6 copy-start.11
  12.2 7.9 copy-start.23
  12.2 7.9 copy-start.24
  12.2 7.9 copy-start.25
  12.2 8.0 copy-start.20
  12.2 8.0 copy-start.22
  12.2 352.4 %all-to-all-start = ((bf16[32,80,512]{2,1,0:T(8,128)(2,1)}), bf16[32,80,512]{2,1,0:T(8,128)(2,1)}, u32[]{:S(2)}, u32[]{:S(2)}) async-start(bf16[32,80,512]{2,1,0:T(8,128)(2,1)} %fusion.7), calls=%async_computation | async-start | bytes 5242880 | tf_op jit(solution)/shard_map/all_to_all | solution.py:957
  167.4 7.0 copy-start.15
  174.4 1.1 copy-start.16
  180.4 2.8 copy-start.1
  180.4 2.8 copy-start
  180.4 2.8 copy-start.5
  351.8 10.7 %copy-start.2 = (bf16[128,2560]{1,0:T(8,128)(2,1)}, bf16[128,2560]{1,0:T(8,128)(2,1)S(1)}, u32[]{:S(2)}) copy-start(bf16[128,2560]{1,0:T(8,128)(2,1)S(1)} %get-tuple-element.28.left) | copy-start | bytes 1966084
  351.8 10.7 %copy-start.3 = (bf16[2176,512]{1,0:T(8,128)(2,1)}, bf16[2176,512]{1,0:T(8,128)(2,1)S(1)}, u32[]{:S(2)}) copy-start(bf16[2176,512]{1,0:T(8,128)(2,1)S(1)} %get-tuple-element.33.window) | copy-start | bytes 6684676
  351.8 10.7 %copy-start.4 = (f32[5,256,128]{2,1,0:T(8,128)}, f32[5,256,128]{2,1,0:T(8,128)S(1)}, u32[]{:S(2)}) copy-start(f32[5,256,128]{2,1,0:T(8,128)S(1)} %get-tuple-element.34.log_ref) | copy-start | bytes 1966084
  355.8 7.4 copy-start.26
  355.8 7.4 copy-start.27
  362.6 1.1 copy-start.6
  669.4 2.3 copy-start.7
  669.4 2.5 copy-start.9
  672.3 12.6 %copy-start.13 = (bf16[128,2560]{1,0:T(8,128)(2,1)}, bf16[128,2560]{1,0:T(8,128)(2,1)S(1)}, u32[]{:S(2)}) copy-start(bf16[128,2560]{1,0:T(8,128)(2,1)S(1)} %fusion.44.right) | copy-start | bytes 1966084
  681.2 251.2 %all-to-all-start.1 = ((bf16[32,80,512]{2,1,0:T(8,128)(2,1)}), bf16[32,80,512]{2,1,0:T(8,128)(2,1)}, u32[]{:S(2)}, u32[]{:S(2)}) async-start(bf16[32,80,512]{2,1,0:T(8,128)(2,1)} %bitcast.38), calls=%async_computation.1 | async-start | bytes 5242880 | tf_op jit(solution)/shard_map/all_to_all | solution.py:957
  805.4 1.5 copy-start.21
  809.7 1.1 copy-start.12
  810.8 12.2 %copy-start.14 = (bf16[128,3072]{1,0:T(8,128)(2,1)}, bf16[128,3072]{1,0:T(8,128)(2,1)S(1)}, u32[]{:S(2)}) copy-start(bf16[128,3072]{1,0:T(8,128)(2,1)S(1)} %concatenate.34.right) | copy-start | bytes 2359300
  922.1 8.5 copy-start.18
  924.3 6.3 copy-start.8
  924.3 6.3 copy-start.10
  924.3 6.3 copy-start.17
  945.6 4.0 copy-start.19
